TPU v7x, 32 devices: a whole 2x2x4 slice. The times are simulated.
32 devices in a mesh: dp: 4 (over x, core), fsdp: 8 (over z, y).
Axes of the slice: x: 2, y: 2, z: 4, core: 2. Of those that a mesh axis runs over, the one named last changes fastest.
Arguments:
- tokens: bfloat16 [65536, 768], P(('dp', 'fsdp')), may hold values from -6 to 6
- masked: int32 [65536], P(('dp', 'fsdp')), may hold values 0 or 1
- replace_ids: int32 [65536], P(('dp', 'fsdp')), may hold values from 0 to 1023
- in_weight: bfloat16 [768, 1536], P(('dp', 'fsdp')), may hold values from -0.21875 to 0.21875
- depth_weight: bfloat16 [9, 768], P(None, ('dp', 'fsdp')), may hold values from -2 to 2
- point_weight: bfloat16 [768, 384], P(('dp', 'fsdp')), may hold values from -0.21875 to 0.21875
- kernel_weight: bfloat16 [384, 54], P('fsdp'), may hold values from -0.3125 to 0.3125
- out_weight: bfloat16 [768, 768], P(('dp', 'fsdp')), may hold values from -0.875 to 0.875
- gain_one: bfloat16 [768], P(('dp', 'fsdp')), may hold values from 0.099609375 to 1.8984375
- shift_one: bfloat16 [768], P(('dp', 'fsdp')), may hold values from -3 to 3
- ffn_in: bfloat16 [2, 384, 1536], P(None, None, ('dp', 'fsdp')), may hold values from -0.3125 to 0.3125
- feedforward_output: bfloat16 [2, 1536, 384], P(None, ('dp', 'fsdp')), may hold values from -0.15625 to 0.15625
- gain_two: bfloat16 [768], P(('dp', 'fsdp')), may hold values from 0.099609375 to 1.8984375
- shift_two: bfloat16 [768], P(('dp', 'fsdp')), may hold values from -3 to 3
- cotangent: bfloat16 [65536, 768], P(('dp', 'fsdp')), may hold values from -6 to 6
Outputs:
- layer_out: bfloat16 [65536, 768], P(('dp', 'fsdp'))
- grad_tokens: float32 [65536, 768], P(('dp', 'fsdp'))
- grad_in_weight: float32 [768, 1536], P(('dp', 'fsdp'))
- grad_depth_weight: float32 [9, 768], P(None, ('dp', 'fsdp'))
- grad_point_weight: float32 [768, 384], P(('dp', 'fsdp'))
- grad_kernel_weight: float32 [384, 54], P('fsdp')
- grad_out_weight: float32 [768, 768], P(('dp', 'fsdp'))
- grad_gain_one: float32 [768], P(('dp', 'fsdp'))
- grad_shift_one: float32 [768], P(('dp', 'fsdp'))
- grad_ffn_in: float32 [2, 384, 1536], P(None, None, ('dp', 'fsdp'))
- grad_ffn_out: float32 [2, 1536, 384], P(None, ('dp', 'fsdp'))
- grad_gain_two: float32 [768], P(('dp', 'fsdp'))
- grad_shift_two: float32 [768], P(('dp', 'fsdp'))
Inputs may be any that keep to these rules, and one draw needn't show every extreme that they name: 1 marks a masked token. `replace_ids`: a position within the same sequence.
All inputs are finite; a program needn't handle non-finite values. No bound on the sum of `masked` on one device may be relied on, other than what follows from the above.
Results may differ from a plain program's by a relative error of at most 0.014.
Values may be sent and summed in bfloat16 or wider, within the bound.
No kernel may reach another device: no remote copies, remote signals or barrier semaphores. Data moves between devices by JAX's collectives and lax.ppermute only.
A program may use at most 256 MiB of HBM per device.

v0:
```python
from functools import partial
import math

import jax
import jax.numpy as jnp
from jax import lax
from jax.sharding import PartitionSpec as P

HEADS = 6
HEAD = 64
SEQUENCE_TOKENS = 1024


def product(left, right):
    return jnp.dot(left, right, preferred_element_type=jnp.float32)


def norm_rows(field_in, gain_vec, shift_vec):
    mean_rows = jnp.mean(field_in, -1, keepdims=True)
    centred = field_in - mean_rows
    variance = jnp.mean(centred * centred, -1, keepdims=True)
    return centred * lax.rsqrt(variance + 1e-12) * gain_vec + shift_vec


def depthwise(field_in, tap_weights):
    kernel_len = tap_weights.shape[0]
    half_span = kernel_len // 2
    length_rows = field_in.shape[-2]
    pads = ((0, 0),) * (field_in.ndim - 2) + ((half_span, half_span), (0, 0))
    padded = jnp.pad(field_in, pads)
    summed = jnp.zeros_like(field_in)
    for offset in range(kernel_len):
        summed = summed + tap_weights[offset] * padded[..., offset : offset + length_rows, :]
    return summed


def dynamic_conv(logits, values, head_count):
    kernels = jax.nn.softmax(logits.reshape(logits.shape[:-1] + (head_count, -1)), axis=-1)
    kernel_len = kernels.shape[-1]
    half_span = kernel_len // 2
    length_rows = values.shape[-2]
    split_heads = values.reshape(values.shape[:-1] + (head_count, -1))
    pads = ((0, 0),) * (split_heads.ndim - 3) + ((half_span, half_span), (0, 0), (0, 0))
    padded = jnp.pad(split_heads, pads)
    summed = jnp.zeros_like(split_heads)
    for offset in range(kernel_len):
        summed = (
            summed
            + kernels[..., offset : offset + 1] * padded[..., offset : offset + length_rows, :, :]
        )
    return summed.reshape(values.shape)


def attend_forward(pieces):
    query_one, key_one, value_one = pieces
    scale = 1.0 / math.sqrt(query_one.shape[-1])
    raw_scores = (
        jnp.einsum("qhd,khd->hqk", query_one, key_one, preferred_element_type=jnp.float32) * scale
    )
    row_top = jnp.max(raw_scores, -1, keepdims=True)
    exp_scores = jnp.exp(raw_scores - row_top)
    row_total = jnp.sum(exp_scores, -1, keepdims=True)
    soft_low = (exp_scores / row_total).astype(jnp.bfloat16)
    attended = jnp.einsum("hqk,khd->qhd", soft_low, value_one, preferred_element_type=jnp.float32)
    return (attended, row_top + jnp.log(row_total))


def attend_backward(pieces):
    query_one, key_one, value_one, d_attended, log_total = pieces
    scale = 1.0 / math.sqrt(query_one.shape[-1])
    soft = jnp.exp(
        jnp.einsum("qhd,khd->hqk", query_one, key_one, preferred_element_type=jnp.float32) * scale
        - log_total
    )
    d_soft = jnp.einsum("qhd,khd->hqk", d_attended, value_one, preferred_element_type=jnp.float32)
    row_dot = jnp.sum(soft * d_soft, -1, keepdims=True)
    d_scores = (soft * (d_soft - row_dot)).astype(jnp.bfloat16)
    d_query_att = (
        jnp.einsum("hqk,khd->qhd", d_scores, key_one, preferred_element_type=jnp.float32) * scale
    )
    d_keys = (
        jnp.einsum("hqk,qhd->khd", d_scores, query_one, preferred_element_type=jnp.float32) * scale
    ).astype(jnp.bfloat16)
    d_values = jnp.einsum(
        "hqk,qhd->khd", soft.astype(jnp.bfloat16), d_attended, preferred_element_type=jnp.float32
    ).astype(jnp.bfloat16)
    return (d_query_att, d_keys, d_values)


def per_device(
    tokens,
    masked,
    replace_ids,
    in_weight,
    depth_weight,
    point_weight,
    kernel_weight,
    out_weight,
    gain_one,
    shift_one,
    ffn_in,
    feedforward_output,
    gain_two,
    shift_two,
    cotangent,
):
    row_count, model_width = tokens.shape
    seq_count = row_count // SEQUENCE_TOKENS
    head_count = HEADS
    att_width = head_count * HEAD
    groups_all = ffn_in.shape[0]
    source_rows = (
        jnp.arange(row_count, dtype=jnp.int32) // SEQUENCE_TOKENS * SEQUENCE_TOKENS + replace_ids
    )
    is_masked = (masked == 1)[:, None]
    inputs = jnp.where(is_masked, jnp.take(tokens, source_rows, axis=0), tokens)

    def collect():
        gathered = (
            lax.all_gather(in_weight, ("dp", "fsdp"), axis=0, tiled=True),
            lax.all_gather(depth_weight, ("dp", "fsdp"), axis=1, tiled=True),
            lax.all_gather(point_weight, ("dp", "fsdp"), axis=0, tiled=True),
            lax.all_gather(out_weight, ("dp", "fsdp"), axis=0, tiled=True),
            lax.all_gather(gain_one, ("dp", "fsdp"), axis=0, tiled=True),
            lax.all_gather(shift_one, ("dp", "fsdp"), axis=0, tiled=True),
            lax.all_gather(ffn_in, ("dp", "fsdp"), axis=2, tiled=True),
            lax.all_gather(feedforward_output, ("dp", "fsdp"), axis=1, tiled=True),
            lax.all_gather(gain_two, ("dp", "fsdp"), axis=0, tiled=True),
            lax.all_gather(shift_two, ("dp", "fsdp"), axis=0, tiled=True),
        )
        kernel_full = lax.all_gather(kernel_weight, "fsdp", axis=0, tiled=True)
        return (gathered, kernel_full)

    gathered, kernel_full = collect()
    w_in, w_depth, w_point, w_out, g_one, s_one, w_up, down_weight, g_two, s_two = gathered
    projected = product(inputs, w_in).astype(jnp.bfloat16)
    queries = projected[:, :att_width]
    key_rows = projected[:, att_width : 2 * att_width]
    value_rows = projected[:, 2 * att_width : 3 * att_width]
    conv_values = projected[:, 3 * att_width :]
    seq_inputs = inputs.astype(jnp.float32).reshape(seq_count, SEQUENCE_TOKENS, model_width)
    spread_full, depth_back = jax.vjp(depthwise, seq_inputs, w_depth.astype(jnp.float32))
    spread = spread_full.reshape(row_count, model_width).astype(jnp.bfloat16)
    conv_keys = product(spread, w_point).astype(jnp.bfloat16)
    query_full = queries.astype(jnp.float32)
    conv_key_full = conv_keys.astype(jnp.float32)
    mixed = (conv_key_full * query_full).astype(jnp.bfloat16)
    kernel_logits = product(mixed, kernel_full)
    conv_out, conv_back = jax.vjp(
        partial(dynamic_conv, head_count=head_count),
        kernel_logits.reshape(seq_count, SEQUENCE_TOKENS, -1),
        conv_values.astype(jnp.float32).reshape(seq_count, SEQUENCE_TOKENS, att_width),
    )
    query_heads = queries.reshape(seq_count, SEQUENCE_TOKENS, head_count, HEAD)
    key_heads = key_rows.reshape(seq_count, SEQUENCE_TOKENS, head_count, HEAD)
    value_heads = value_rows.reshape(seq_count, SEQUENCE_TOKENS, head_count, HEAD)
    attended, log_total = lax.map(attend_forward, (query_heads, key_heads, value_heads))
    context = jnp.concatenate(
        [attended.reshape(row_count, att_width), conv_out.reshape(row_count, att_width)], -1
    ).astype(jnp.bfloat16)
    first_in = product(context, w_out) + inputs.astype(jnp.float32)
    first, first_back = jax.vjp(
        norm_rows, first_in, g_one.astype(jnp.float32), s_one.astype(jnp.float32)
    )
    grouped = first.astype(jnp.bfloat16).reshape(row_count, groups_all, -1)
    inner = jnp.einsum("ngc,gcf->ngf", grouped, w_up, preferred_element_type=jnp.float32)
    active_full, gelu_back = jax.vjp(partial(jax.nn.gelu, approximate=False), inner)
    active_hidden = active_full.astype(jnp.bfloat16)
    outer_hidden = jnp.einsum(
        "tza,zah->tzh", active_hidden, down_weight, preferred_element_type=jnp.float32
    ).reshape(row_count, model_width)
    result, second_back = jax.vjp(
        norm_rows, outer_hidden + first, g_two.astype(jnp.float32), s_two.astype(jnp.float32)
    )
    gathered, kernel_full = collect()
    w_in, w_depth, w_point, w_out, g_one, s_one, w_up, down_weight, g_two, s_two = gathered
    d_second, d_gain_two, d_shift_two = second_back(cotangent.astype(jnp.float32))
    outer_gradient = d_second.astype(jnp.bfloat16).reshape(row_count, groups_all, -1)
    down_weight_gradient = jnp.einsum(
        "mxu,mxe->xue", active_hidden, outer_gradient, preferred_element_type=jnp.float32
    )
    active_gradient = jnp.einsum(
        "xpy,pjy->xpj", outer_gradient, down_weight, preferred_element_type=jnp.float32
    )
    d_inner = gelu_back(active_gradient)[0].astype(jnp.bfloat16)
    d_up = jnp.einsum("ngc,ngf->gcf", grouped, d_inner, preferred_element_type=jnp.float32)
    d_first = (
        jnp.einsum("ngf,gcf->ngc", d_inner, w_up, preferred_element_type=jnp.float32).reshape(
            row_count, model_width
        )
        + d_second
    )
    d_first_in, d_gain_one, d_shift_one = first_back(d_first)
    d_dense = d_first_in.astype(jnp.bfloat16)
    d_out_w = jnp.einsum("nc,nd->cd", context, d_dense, preferred_element_type=jnp.float32)
    d_context = jnp.einsum("nd,cd->nc", d_dense, w_out, preferred_element_type=jnp.float32).astype(
        jnp.bfloat16
    )
    d_attended = d_context[:, :att_width].reshape(seq_count, SEQUENCE_TOKENS, head_count, HEAD)
    d_query_att, d_keys, d_values = lax.map(
        attend_backward, (query_heads, key_heads, value_heads, d_attended, log_total)
    )
    d_logits, d_conv_values = conv_back(
        d_context[:, att_width:].astype(jnp.float32).reshape(seq_count, SEQUENCE_TOKENS, att_width)
    )
    d_logits_low = d_logits.reshape(row_count, -1).astype(jnp.bfloat16)
    d_kernel = jnp.einsum("nc,nk->ck", mixed, d_logits_low, preferred_element_type=jnp.float32)
    d_mixed = jnp.einsum("nk,ck->nc", d_logits_low, kernel_full, preferred_element_type=jnp.float32)
    d_queries = (d_query_att.reshape(row_count, att_width) + d_mixed * conv_key_full).astype(
        jnp.bfloat16
    )
    d_conv_keys = (d_mixed * query_full).astype(jnp.bfloat16)
    d_point = jnp.einsum("nc,nk->ck", spread, d_conv_keys, preferred_element_type=jnp.float32)
    d_spread = jnp.einsum("nk,ck->nc", d_conv_keys, w_point, preferred_element_type=jnp.float32)
    d_seq_inputs, d_depth = depth_back(d_spread.reshape(seq_count, SEQUENCE_TOKENS, model_width))
    d_projected = jnp.concatenate(
        [
            d_queries,
            d_keys.reshape(row_count, att_width),
            d_values.reshape(row_count, att_width),
            d_conv_values.reshape(row_count, att_width).astype(jnp.bfloat16),
        ],
        -1,
    )
    d_in = jnp.einsum("nc,nk->ck", inputs, d_projected, preferred_element_type=jnp.float32)
    d_inputs = (
        jnp.einsum("nk,ck->nc", d_projected, w_in, preferred_element_type=jnp.float32)
        + d_seq_inputs.reshape(row_count, model_width)
        + d_first_in
    )
    kept_part = jnp.where(is_masked, 0.0, d_inputs)
    moved_part = jnp.where(is_masked, d_inputs, 0.0)
    d_tokens = kept_part + jnp.zeros_like(d_inputs).at[source_rows].add(moved_part)
    grad_scale = 1.0 / math.sqrt(row_count * lax.axis_size("dp") * lax.axis_size("fsdp"))
    kernel_part = lax.psum_scatter(d_kernel, "fsdp", scatter_dimension=0, tiled=True)
    kernel_sum = lax.psum(kernel_part, "dp")
    (
        sum_in,
        sum_depth,
        sum_point,
        sum_out,
        sum_gain_one,
        sum_shift_one,
        sum_up,
        sum_down,
        sum_gain_two,
        sum_shift_two,
    ) = (
        lax.psum_scatter(d_in, ("dp", "fsdp"), scatter_dimension=0, tiled=True),
        lax.psum_scatter(d_depth, ("dp", "fsdp"), scatter_dimension=1, tiled=True),
        lax.psum_scatter(d_point, ("dp", "fsdp"), scatter_dimension=0, tiled=True),
        lax.psum_scatter(d_out_w, ("dp", "fsdp"), scatter_dimension=0, tiled=True),
        lax.psum_scatter(d_gain_one, ("dp", "fsdp"), scatter_dimension=0, tiled=True),
        lax.psum_scatter(d_shift_one, ("dp", "fsdp"), scatter_dimension=0, tiled=True),
        lax.psum_scatter(d_up, ("dp", "fsdp"), scatter_dimension=2, tiled=True),
        lax.psum_scatter(down_weight_gradient, ("dp", "fsdp"), scatter_dimension=1, tiled=True),
        lax.psum_scatter(d_gain_two, ("dp", "fsdp"), scatter_dimension=0, tiled=True),
        lax.psum_scatter(d_shift_two, ("dp", "fsdp"), scatter_dimension=0, tiled=True),
    )
    return (
        result.astype(jnp.bfloat16),
        d_tokens,
        sum_in * grad_scale,
        sum_depth * grad_scale,
        sum_point * grad_scale,
        kernel_sum * grad_scale,
        sum_out * grad_scale,
        sum_gain_one * grad_scale,
        sum_shift_one * grad_scale,
        sum_up * grad_scale,
        sum_down * grad_scale,
        sum_gain_two * grad_scale,
        sum_shift_two * grad_scale,
    )


def solution(mesh):
    return jax.shard_map(
        per_device,
        mesh=mesh,
        in_specs=(
            P(("dp", "fsdp"), None),
            P(("dp", "fsdp")),
            P(("dp", "fsdp")),
            P(("dp", "fsdp"), None),
            P(None, ("dp", "fsdp")),
            P(("dp", "fsdp"), None),
            P("fsdp", None),
            P(("dp", "fsdp"), None),
            P(("dp", "fsdp")),
            P(("dp", "fsdp")),
            P(None, None, ("dp", "fsdp")),
            P(None, ("dp", "fsdp"), None),
            P(("dp", "fsdp")),
            P(("dp", "fsdp")),
            P(("dp", "fsdp"), None),
        ),
        out_specs=(
            P(("dp", "fsdp"), None),
            P(("dp", "fsdp"), None),
            P(("dp", "fsdp"), None),
            P(None, ("dp", "fsdp")),
            P(("dp", "fsdp"), None),
            P("fsdp", None),
            P(("dp", "fsdp"), None),
            P(("dp", "fsdp")),
            P(("dp", "fsdp")),
            P(None, None, ("dp", "fsdp")),
            P(None, ("dp", "fsdp"), None),
            P(("dp", "fsdp")),
            P(("dp", "fsdp")),
        ),
        check_vma=False,
    )
```

profile of v0, /device:TPU:0, one launch (start us, length us, event | category | flops | bytes accessed | tf_op | source)
XLA Modules:
  0.0 1437.3 jit_solution(3514618851266802435)
XLA Ops:
  14.1 42.1 %all-reduce.49 = (bf16[768]{0:T(1024)(128)(2,1)S(1)}, bf16[768]{0:T(1024)(128)(2,1)S(1)}, bf16[768]{0:T(1024)(128)(2,1)S(1)}, bf16[768]{0:T(1024)(128)(2,1)S(1)}) all-reduce(bf16[768]{0:T(1024)(128)(2,1)S(1)} %dynamic-update-slice.1, bf16[768]{0:T(1024)(128)(2,1)S(1)} %dynamic-update-slice, ...), channel_id=1, replica_groups=mesh['dp'=4,'fsdp'=8] {'dp','fsdp'}, use_global_device_ids=true, to_apply=%add.39 | all-reduce | flops 3072 | bytes 12288
  59.4 30.8 %all_gather.42 = bf16[384,54]{1,0:T(8,128)(2,1)S(1)} all-gather(bf16[48,54]{1,0:T(8,128)(2,1)} %param.25), channel_id=1, replica_groups=mesh['dp'=4,'fsdp'=8] {'fsdp'}, dimensions={0}, use_global_device_ids=true | all-gather | bytes 46656 | tf_op jit(solution)/shard_map/all_gather | solution.py:131
  90.2 65.7 %all-gather = bf16[32,24,9]{1,2,0:T(8,128)(2,1)S(1)} all-gather(bf16[1,24,9]{1,2,0:T(8,128)(2,1)} %bitcast.350), channel_id=1, replica_groups=mesh['dp'=4,'fsdp'=8] {'dp','fsdp'}, dimensions={0}, use_global_device_ids=true | all-gather | bytes 14256 | tf_op jit(solution)/shard_map/all_gather | solution.py:121
  156.4 74.5 %all_gather.41 = bf16[768,384]{1,0:T(8,128)(2,1)} all-gather(bf16[24,384]{1,0:T(8,128)(2,1)} %param.24), channel_id=1, replica_groups=mesh['dp'=4,'fsdp'=8] {'dp','fsdp'}, dimensions={0}, use_global_device_ids=true | all-gather | bytes 608256 | tf_op jit(solution)/shard_map/all_gather | solution.py:122
  259.9 22.6 %add_convert_fusion.1 = bf16[2,1024,768]{2,1,0:T(8,128)(2,1)S(1)} fusion(f32[2,1024,768]{2,1,0:T(8,128)} %bitcast.314, f32[768]{0:T(1024)S(1)} %get-tuple-element.238, f32[768]{0:T(1024)S(1)} %get-tuple-element.239, f32[768]{0:T(1024)S(1)} %get-tuple-element.240, f32[768]{0:T(1024)S(1)} %get-tuple-element.241, f32[768]{0:T(1024)S(1)} %get-tuple-element.242, ...), kind=kLoop, calls=%fused_computation.121 | loop fusion | flops 28311552 | bytes 9464832 | tf_op jit(solution)/shard_map/convert_element_type | solution.py:143
  309.9 27.2 %add_convert_fusion.4 = bf16[2,1024,6,64]{1,0,3,2:T(2,128)(2,1)S(1)} fusion(f32[2,1024,6,64]{1,0,3,2:T(2,128)S(1)} %reshape.285, f32[2,1024,6]{1,0,2:T(2,128)S(1)} %get-tuple-element.328, f32[2,1024,6]{1,0,2:T(2,128)S(1)} %get-tuple-element.329, f32[2,1024,6]{1,0,2:T(2,128)S(1)} %get-tuple-element.330, f32[2,1024,6]{1,0,2:T(2,128)S(1)} %get-tuple-element.331, ...), kind=kLoop, calls=%fused_computation.159 | loop fusion | flops 14155776 | bytes 5160960 | tf_op jit(solution)/shard_map/convert.5
  359.0 60.4 %while.26 = (s32[]{:T(128)}, bf16[2,1024,6,64]{1,3,2,0:T(8,128)(2,1)}, f32[2,6,1024,1]{2,1,3,0:T(8,128)}, bf16[2,1024,6,64]{1,3,2,0:T(8,128)(2,1)}, bf16[2,1024,...) while((s32[]{:T(128)}, bf16[2,1024,6,64]{1,3,2,0:T(8,128)(2,1)}, ...), condition=%wide.region_3.4_spmd, body=%wide.region_0.0_spmd.sunk | while | flops 1667229696 | bytes 180299888 | solution.py:157
  435.1 63.7 %fusion.57 = (bf16[2048,2,1536]{2,0,1:T(8,128)(2,1)}, f32[2048,2,1536]{2,0,1:T(8,128)}, f32[2,2048,1536]{2,1,0:T(8,128)}) fusion(bf16[2048,2,384]{0,2,1:T(8,128)(2,1)S(1)} %bitcast.332, bf16[2,384,1536]{1,2,0:T(8,128)(2,1)} %all-gather.10.cloned.1.call-done), kind=kOutput, calls=%fused_computation.71 | convolution fusion | flops 5240782848 | bytes 68419584 | tf_op jit(solution)/shard_map/ngc,gcf->ngf/dot_general | solution.py:166
  524.9 24.9 %fusion.54 = bf16[2048,2,1536]{2,0,1:T(8,128)(2,1)} fusion(f32[2048,2,1536]{2,0,1:T(8,128)} %get-tuple-element.293, f32[2,2048,1536]{2,1,0:T(8,128)} %get-tuple-element.340, bf16[2048,2,384]{0,2,1:T(8,128)(2,1)} %bitcast.334, bf16[2,1536,384]{2,1,0:T(8,128)(2,1)} %all-gather.12.cloned.1.call-done), kind=kOutput, calls=%fused_computation.63 | convolution fusion | flops 4919918592 | bytes 68419584 | tf_op jit(solution)/shard_map/xpy,pjy->xpj/dot_general | solution.py:182
  585.5 191.6 %while.27 = (s32[]{:T(128)}, f32[2,1024,6,64]{1,0,3,2:T(2,128)}, bf16[2,1024,6,64]{1,3,2,0:T(8,128)(2,1)}, bf16[2,1024,6,64]{1,3,2,0:T(8,128)(2,1)}, bf16[2,1024...) while((s32[]{:T(128)}, f32[2,1024,6,64]{1,0,3,2:T(2,128)}, ...), condition=%wide.region_16.17_spmd, body=%wide.region_14.16_spmd.sunk | while | flops 4103596032 | bytes 203862160 | solution.py:200
  627.2 16.9 %multiply_convert_fusion.4 = bf16[6,1024,1024]{1,2,0:T(8,128)(2,1)S(1)} fusion(f32[6,1024,1024]{1,2,0:T(8,128)} %get-tuple-element.446, f32[6,1024,1024]{1,2,0:T(8,128)} %fusion.167, f32[6,1024]{1,0:T(8,128)S(1)} %get-tuple-element.447, f32[6,1024]{1,0:T(8,128)S(1)} %dynamic-slice_bitcast_fusion.2), kind=kLoop, calls=%fused_computation.19.clone.1 | loop fusion | flops 31457280 | bytes 62963712 | tf_op jit(solution)/shard_map/while/body/eval_jaxpr/convert_element_type | solution.py:77
  653.9 27.5 %dynamic_update_slice.31 = f32[2,1024,6,64]{1,0,3,2:T(2,128)} dynamic-update-slice(f32[2,1024,6,64]{1,0,3,2:T(2,128)} %get-tuple-element.481, f32[1,1024,6,64]{1,0,3,2:T(1,128)S(1)} %copy.345, s32[]{:T(128)S(6)} %copy.369, s32[]{:T(128)} %constant.47.clone.1..sunk, s32[]{:T(128)} %constant.47.clone.1..sunk, s32[]{:T(128)} %constant.47.clone.1..sunk) | dynamic-update-slice | bytes 3145732 | tf_op jit(solution)/shard_map/while/body/jit(dynamic_update_index_in_dim)/dynamic_update_slice | solution.py:157
  722.8 16.9 %multiply_convert_fusion.4 = bf16[6,1024,1024]{1,2,0:T(8,128)(2,1)S(1)} fusion(f32[6,1024,1024]{1,2,0:T(8,128)} %get-tuple-element.446, f32[6,1024,1024]{1,2,0:T(8,128)} %fusion.167, f32[6,1024]{1,0:T(8,128)S(1)} %get-tuple-element.447, f32[6,1024]{1,0:T(8,128)S(1)} %dynamic-slice_bitcast_fusion.2), kind=kLoop, calls=%fused_computation.19.clone.1 | loop fusion | flops 31457280 | bytes 62963712 | tf_op jit(solution)/shard_map/while/body/eval_jaxpr/convert_element_type | solution.py:77
  749.5 27.5 %dynamic_update_slice.31 = f32[2,1024,6,64]{1,0,3,2:T(2,128)} dynamic-update-slice(f32[2,1024,6,64]{1,0,3,2:T(2,128)} %get-tuple-element.481, f32[1,1024,6,64]{1,0,3,2:T(1,128)S(1)} %copy.345, s32[]{:T(128)S(6)} %copy.369, s32[]{:T(128)} %constant.47.clone.1..sunk, s32[]{:T(128)} %constant.47.clone.1..sunk, s32[]{:T(128)} %constant.47.clone.1..sunk) | dynamic-update-slice | bytes 3145732 | tf_op jit(solution)/shard_map/while/body/jit(dynamic_update_index_in_dim)/dynamic_update_slice | solution.py:157
  792.2 29.0 %multiply_reduce_fusion.23 = (f32[2,1024,6]{1,0,2:T(2,128)S(1)}, f32[2,1024,6]{1,0,2:T(2,128)S(1)}, f32[2,1024,6]{1,0,2:T(2,128)S(1)}, f32[2,1024,6]{1,0,2:T(2,1...) fusion(f32[2,1024,6,64]{1,0,3,2:T(2,128)} %reshape.286, ...), kind=kLoop, calls=%fused_computation.156 | loop fusion | flops 14045184 | bytes 6733824 | tf_op jit(solution)/shard_map/transpose(jvp())/reduce_sum | solution.py:49
  879.5 24.1 %multiply_reduce_fusion.11 = (f32[768]{0:T(1024)S(1)}, f32[768]{0:T(1024)S(1)}, f32[768]{0:T(1024)S(1)}, f32[768]{0:T(1024)S(1)}, f32[768]{0:T(1024)S(1)}, /*ind...) fusion(f32[2,1024,768]{2,1,0:T(8,128)} %bitcast.315, ...), kind=kOutput, calls=%fused_computation.114 | convolution fusion | flops 1235478528 | bytes 17915904 | tf_op jit(solution)/shard_map/nk,ck->nc/dot_general | solution.py:214
  946.1 16.9 %fusion.79 = bf16[2,1024,6,64]{1,0,3,2:T(2,128)(2,1)S(1)} fusion(f32[2,1024,6,64]{1,0,3,2:T(2,128)S(1)} %get-tuple-element.319, f32[2,1024,6,64]{1,0,3,2:T(2,128)S(1)} %get-tuple-element.320, f32[2,1024,6,64]{1,0,3,2:T(2,128)S(1)} %get-tuple-element.321, f32[2,1024,6,64]{1,0,3,2:T(2,128)S(1)} %get-tuple-element.322, ...), kind=kLoop, calls=%fused_computation.143 | loop fusion | flops 4718592 | bytes 20447232 | tf_op jit(solution)/shard_map/convert.2
  977.4 17.9 %broadcast_multiply_fusion = (f32[2,1024,768]{2,1,0:T(8,128)S(1)}, f32[2,1024,768]{2,1,0:T(8,128)}, f32[2,1024,768]{2,1,0:T(8,128)}, f32[2,1024,768]{2,1,0:T(8,1...) fusion(f32[2,1024,768]{2,1,0:T(8,128)} %bitcast.316, ...), kind=kLoop, calls=%fused_computation.160 | loop fusion | flops 14155776 | bytes 62942208 | tf_op jit(solution)/shard_map/transpose(jvp())/mul | solution.py:33
  1000.7 17.2 %pad_add_fusion.1 = f32[2,1024,768]{2,1,0:T(8,128)} fusion(f32[2,1024,768]{2,1,0:T(8,128)} %get-tuple-element.304, f32[2,1024,768]{2,1,0:T(8,128)} %get-tuple-element.305, f32[2,1024,768]{2,1,0:T(8,128)} %get-tuple-element.306, f32[2,1024,768]{2,1,0:T(8,128)} %get-tuple-element.307, f32[2,1024,768]{2,1,0:T(8,128)} %get-tuple-element.308, ...), kind=kLoop, calls=%fused_computation.96 | loop fusion | flops 9437184 | bytes 50331648 | tf_op jit(solution)/shard_map/transpose(jvp())/add_any | solution.py:33
  1050.4 20.0 %scatter_fusion = f32[2048,768]{1,0:T(8,128)} fusion(f32[2048,768]{1,0:T(8,128)} %copy.242, s32[2048]{0:T(1024)S(1)} %copy-done.67, f32[2048,768]{1,0:T(8,128)} %copy.243), kind=kCustom, calls=%fused_computation.1 | custom fusion | flops 1572864 | bytes 18882560 | tf_op jit(solution)/shard_map/scatter-add | solution.py:233
  1070.6 38.3 %all-reduce.48 = (f32[9,768]{1,0:T(8,128)S(1)}, f32[768]{0:T(1024)S(1)}, f32[768]{0:T(1024)S(1)}, f32[768]{0:T(1024)S(1)}, f32[768]{0:T(1024)S(1)}) all-reduce(f32[9,768]{1,0:T(8,128)S(1)} %pad_add_fusion.14, f32[768]{0:T(1024)S(1)} %copy-done.90, f32[768]{0:T(1024)S(1)} %copy-done.91, ...), channel_id=3, replica_groups=mesh['dp'=4,'fsdp'=8] {'dp','fsdp'}, use_global_device_ids=true, to_apply=%region_38.39.clone | all-reduce | flops 9984 | bytes 79872
  1125.3 79.5 %reduce-scatter.18.cloned.1.call-done = f32[2,48,384]{2,1,0:T(8,128)} async-done(((f32[2,1536,384]{2,1,0:T(8,128)}), f32[2,48,384]{2,1,0:T(8,128)}) %reduce-scatter.18.cloned.1.call-update) | async-done | bytes 147472 | tf_op jit(solution)/shard_map/reduce_scatter | solution.py:256
  1206.4 110.0 %reduce-scatter.16.cloned.1.call-done = f32[2,384,48]{1,2,0:T(8,128)} async-done(((f32[2,384,1536]{1,2,0:T(8,128)}), f32[2,384,48]{1,2,0:T(8,128)}) %reduce-scatter.16.cloned.1.call-update) | async-done | bytes 147472 | tf_op jit(solution)/shard_map/reduce_scatter | solution.py:255
  1318.0 110.7 %reduce-scatter.10.cloned.1.call-done = f32[24,1536]{1,0:T(8,128)} async-done(((f32[768,1536]{1,0:T(8,128)}), f32[24,1536]{1,0:T(8,128)}) %reduce-scatter.10.cloned.1.call-update) | async-done | bytes 147472 | tf_op jit(solution)/shard_map/reduce_scatter | solution.py:249
  (380 shorter events, 516.5 us)
Async XLA Ops:
  7.2 228.3 %copy-start.1 = (bf16[2048,768]{1,0:T(8,128)(2,1)S(1)}, bf16[2048,768]{1,0:T(8,128)(2,1)}, u32[]{:S(2)}) copy-start(bf16[2048,768]{1,0:T(8,128)(2,1)} %param.19) | copy-start | bytes 9437188
  7.2 279.9 %all-gather.6.cloned.1.call-start = ((), (), s32[]{:S(2)}) async-start(), calls=%async_computation.6 | async-start | bytes 2433024 | tf_op jit(solution)/shard_map/all_gather | solution.py:120
  7.9 417.7 %all-gather.8.cloned.1.call-start = ((), (), s32[]{:S(2)}) async-start(), calls=%async_computation.7 | async-start | bytes 1216512 | tf_op jit(solution)/shard_map/all_gather | solution.py:123
  8.7 426.5 %all-gather.10.cloned.1.call-start = ((), (), s32[]{:S(2)}) async-start(), calls=%async_computation.8 | async-start | bytes 2433024 | tf_op jit(solution)/shard_map/all_gather | solution.py:126
  9.4 490.1 %all-gather.12.cloned.1.call-start = ((), (), s32[]{:S(2)}) async-start(), calls=%async_computation.9 | async-start | bytes 2433024 | tf_op jit(solution)/shard_map/all_gather | solution.py:127
  10.0 1100.7 %reduce-scatter.12.cloned.1.call-start = ((), (), s32[]{:S(2)}) async-start(), calls=%async_computation.11 | async-start | bytes 221184 | tf_op jit(solution)/shard_map/reduce_scatter | solution.py:235
  10.8 241.9 %copy-start.95 = (pred[2048]{0:T(1024)(128)(4,1)}, pred[2048]{0:T(1024)(128)(4,1)S(1)}, u32[]{:S(2)}) copy-start(pred[2048]{0:T(1024)(128)(4,1)S(1)} %broadcast_compare_fusion) | copy-start | bytes 6148
  90.2 207.2 %copy-start.32 = (bf16[384,54]{1,0:T(8,128)(2,1)}, bf16[384,54]{1,0:T(8,128)(2,1)S(1)}, u32[]{:S(2)}) copy-start(bf16[384,54]{1,0:T(8,128)(2,1)S(1)} %all_gather.42) | copy-start | bytes 124420
  156.3 103.5 %copy-start.68 = (f32[768]{0:T(1024)}, f32[768]{0:T(1024)S(1)}, u32[]{:S(2)}) copy-start(f32[768]{0:T(1024)S(1)} %get-tuple-element.237) | copy-start | bytes 9220
  156.3 103.5 %copy-start.70 = (f32[768]{0:T(1024)}, f32[768]{0:T(1024)S(1)}, u32[]{:S(2)}) copy-start(f32[768]{0:T(1024)S(1)} %get-tuple-element.238) | copy-start | bytes 9220
  156.3 103.5 %copy-start.72 = (f32[768]{0:T(1024)}, f32[768]{0:T(1024)S(1)}, u32[]{:S(2)}) copy-start(f32[768]{0:T(1024)S(1)} %get-tuple-element.239) | copy-start | bytes 9220
  156.3 103.5 %copy-start.74 = (f32[768]{0:T(1024)}, f32[768]{0:T(1024)S(1)}, u32[]{:S(2)}) copy-start(f32[768]{0:T(1024)S(1)} %get-tuple-element.240) | copy-start | bytes 9220
  156.3 103.5 %copy-start.76 = (f32[768]{0:T(1024)}, f32[768]{0:T(1024)S(1)}, u32[]{:S(2)}) copy-start(f32[768]{0:T(1024)S(1)} %get-tuple-element.241) | copy-start | bytes 9220
  156.3 103.5 %copy-start.78 = (f32[768]{0:T(1024)}, f32[768]{0:T(1024)S(1)}, u32[]{:S(2)}) copy-start(f32[768]{0:T(1024)S(1)} %get-tuple-element.242) | copy-start | bytes 9220
  156.3 103.5 %copy-start.80 = (f32[768]{0:T(1024)}, f32[768]{0:T(1024)S(1)}, u32[]{:S(2)}) copy-start(f32[768]{0:T(1024)S(1)} %get-tuple-element.243) | copy-start | bytes 9220
  156.4 103.5 %copy-start.82 = (f32[768]{0:T(1024)}, f32[768]{0:T(1024)S(1)}, u32[]{:S(2)}) copy-start(f32[768]{0:T(1024)S(1)} %get-tuple-element.244) | copy-start | bytes 9220
  156.4 103.5 %copy-start.84 = (f32[768]{0:T(1024)}, f32[768]{0:T(1024)S(1)}, u32[]{:S(2)}) copy-start(f32[768]{0:T(1024)S(1)} %get-tuple-element.245) | copy-start | bytes 9220
  435.1 63.8 %copy-start.25 = (bf16[2048,768]{0,1:T(8,128)(2,1)}, bf16[2048,768]{0,1:T(8,128)(2,1)S(1)}, u32[]{:S(2)}) copy-start(bf16[2048,768]{0,1:T(8,128)(2,1)S(1)} %fusion.74) | copy-start | bytes 9437188
  435.1 63.8 %copy-start.35 = (f32[2,1024,6]{1,0,2:T(2,128)S(1)}, f32[2,1024,6]{1,0,2:T(2,128)}, u32[]{:S(2)}) copy-start(f32[2,1024,6]{1,0,2:T(2,128)} %copy-done.34) | copy-start | bytes 147460
  829.5 292.9 %reduce-scatter.20.cloned.1.call-start = ((), (), s32[]{:S(2)}) async-start(), calls=%async_computation.15 | async-start | bytes 1216512
  835.7 288.1 %reduce-scatter.14.cloned.1.call-start = ((), (), s32[]{:S(2)}) async-start(), calls=%async_computation.12 | async-start | bytes 2433024 | tf_op jit(solution)/shard_map/reduce_scatter | solution.py:252
  843.7 361.1 %reduce-scatter.18.cloned.1.call-start = ((), (), s32[]{:S(2)}) async-start(), calls=%async_computation.14 | async-start | bytes 4866048 | tf_op jit(solution)/shard_map/reduce_scatter | solution.py:256
  858.2 458.1 %reduce-scatter.16.cloned.1.call-start = ((), (), s32[]{:S(2)}) async-start(), calls=%async_computation.13 | async-start | bytes 4866048 | tf_op jit(solution)/shard_map/reduce_scatter | solution.py:255
  879.4 549.3 %reduce-scatter.10.cloned.1.call-start = ((), (), s32[]{:S(2)}) async-start(), calls=%async_computation.10 | async-start | bytes 4866048 | tf_op jit(solution)/shard_map/reduce_scatter | solution.py:249
  (85 other events, 837.1 us)
Sparse Core Ops, SparseCore 0:
  10.9 60.2 all-gather.5
  74.1 52.8 all-gather.7
  129.9 57.0 all-gather.9
  189.7 56.1 all-gather.11
  829.6 59.0 reduce-scatter.11
  893.7 95.2 reduce-scatter.19
  994.2 98.1 reduce-scatter.13
  1098.8 105.9 reduce-scatter.17
  1210.3 106.0 reduce-scatter.15
  1322.6 106.0 reduce-scatter.9
where the time goes:
time: 1450 us; the launch traced here: 1440 us
  matrix products  354 us (24%)
  waiting for transfers between devices  303 us (21%)
  other arithmetic  288 us (20%)
  blocking collectives  262 us (18%)
  local copies, waits for them, and re-layouts  213 us (15%)
  between operations  15.9 us (1%)
    reduce_scatter x1, waiting for transfers between devices, per_device(): lax.psum_scatter(d_in, ('dp', 'fsdp'), scatter_dimension=0, tiled=True)  111 us
    reduce_scatter x1, waiting for transfers between devices, per_device(): lax.psum_scatter(d_up, ('dp', 'fsdp'), scatter_dimension=2, tiled=True)  110 us
    unnamed x2, blocking collectives  80.5 us
    reduce_scatter x1, waiting for transfers between devices, per_device(): lax.psum_scatter(down_weight_gradient, ('dp', 'fsdp'), scatter_dimension=...  79.5 us
    all_gather x1, blocking collectives, collect(): lax.all_gather(point_weight, ('dp', 'fsdp'), axis=0, tiled=True)  74.5 us
    all_gather x1, blocking collectives, collect(): lax.all_gather(depth_weight, ('dp', 'fsdp'), axis=1, tiled=True)  65.7 us
    dot_general x1, matrix products, per_device(): jnp.einsum('ngc,gcf->ngf', grouped, w_up, preferred_element_type=jnp.floa...  63.7 us
    dynamic_update_slice x4, local copies, waits for them, and re-layouts, per_device(): lax.map(attend_forward, (query_heads, key_heads, value_heads))  58.2 us
  transfers between devices with their start and end apart: 10, of which 3 were waited for; matrix products, arithmetic and copies ran while one was open for 35% of the time, Pallas kernels for 0%

commit v1 on v0

v1 whole, which is shorter than its diff:
```python
from functools import partial
import math

import jax
import jax.numpy as jnp
from jax import lax
from jax.experimental import pallas as pl
from jax.experimental.pallas import tpu as pltpu
from jax.sharding import PartitionSpec as P

BF = jnp.bfloat16
F32 = jnp.float32
HEADS = 6
HEAD = 64
SEQ = 1024
KER = 9
ATT = HEADS * HEAD
WIDTH = 768
VMEM_MAX = 60 * 1024 * 1024


def mm(a, b):
    return jnp.dot(a, b, preferred_element_type=F32)


def mm_nt(a, b):
    return lax.dot_general(a, b, (((1,), (1,)), ((), ())), preferred_element_type=F32)


def mm_tn(a, b):
    return lax.dot_general(a, b, (((0,), (0,)), ((), ())), preferred_element_type=F32)


def params(count):
    return pltpu.CompilerParams(
        dimension_semantics=("arbitrary",) * count, vmem_limit_bytes=VMEM_MAX
    )


def whole(shape):
    zeros = (0,) * len(shape)
    return pl.BlockSpec(shape, lambda *_: zeros, pipeline_mode=pl.Buffered(1))


def whole_out(shape):
    zeros = (0,) * len(shape)
    return pl.BlockSpec(shape, lambda *_: zeros)


def lane_groups(x, combine):
    for step in (64, 32, 16, 8):
        x = combine(x, pltpu.roll(x, step, 1))
    return x


def tap_spread(block):
    rows = lax.broadcasted_iota(jnp.int32, (128, KER * 128), 0)
    cols = lax.broadcasted_iota(jnp.int32, (128, KER * 128), 1)
    want = (cols // 128) * 8 + block * 2 + (cols % 128) // HEAD
    return (rows == want).astype(F32).astype(BF)


CH = 256
HALO = CH + 16


def enter_kernel(
    pick_ref, tok_ref, w_in_ref, w_depth_ref, w_point_ref, w_kern_ref,
    inp_ref, proj_ref, spread_ref, ck_ref, kern_ref, conv_ref,
    x_pad, cv_pad,
):
    x_pad[0:8, :] = jnp.zeros((8, WIDTH), F32)
    x_pad[SEQ + 8 : SEQ + 16, :] = jnp.zeros((8, WIDTH), F32)
    cv_pad[0:8, :] = jnp.zeros((8, ATT), F32)
    cv_pad[SEQ + 8 : SEQ + 16, :] = jnp.zeros((8, ATT), F32)

    def load(i, carry):
        r = pl.multiple_of(i * CH, CH)
        pick = pick_ref[pl.ds(r, CH), :]
        cols = lax.broadcasted_iota(jnp.int32, (CH, SEQ), 1)
        hot = (cols == pick).astype(F32).astype(BF)
        rows = mm(hot, tok_ref[...])
        x_pad[pl.ds(r + 8, CH), :] = rows
        low = rows.astype(BF)
        inp_ref[pl.ds(r, CH), :] = low
        proj = mm(low, w_in_ref[...])
        proj_low = proj.astype(BF)
        proj_ref[pl.ds(r, CH), :] = proj_low
        cv_pad[pl.ds(r + 8, CH), :] = proj_low[:, 3 * ATT :].astype(F32)
        return carry

    lax.fori_loop(0, SEQ // CH, load, 0)

    def conv(i, carry):
        r = pl.multiple_of(i * CH, CH)
        for b in range(WIDTH // 128):
            lanes = slice(b * 128, (b + 1) * 128)
            xs = x_pad[pl.ds(r, HALO), lanes]
            shifted = [xs] + [pltpu.roll(xs, HALO - s, 0) for s in (1, 2, 3)]
            tap = lambda j: w_depth_ref[j : j + 1, lanes]
            low_part = sum(tap(s) * shifted[s] for s in range(4))
            mid_part = sum(tap(4 + s) * shifted[s] for s in range(4))
            high_part = tap(8) * xs
            low_part = pltpu.roll(low_part, HALO - 4, 0)
            high_part = pltpu.roll(high_part, HALO - 4, 0)
            total = low_part[0:CH] + mid_part[8 : 8 + CH] + high_part[8 : 8 + CH]
            spread_ref[pl.ds(r, CH), lanes] = total.astype(BF)
        ck = mm(spread_ref[pl.ds(r, CH), :], w_point_ref[...]).astype(BF)
        ck_ref[pl.ds(r, CH), :] = ck
        q = proj_ref[pl.ds(r, CH), 0:ATT].astype(F32)
        mixed = (ck.astype(F32) * q).astype(BF)
        logits = mm(mixed, w_kern_ref[...])
        lane = lax.broadcasted_iota(jnp.int32, (CH, 128), 1)
        logits = jnp.where(lane < KER * 8, logits, -1e30)
        top = lane_groups(logits, jnp.maximum)
        e = jnp.exp(logits - top)
        kern = e / lane_groups(e, jnp.add)
        kern_ref[pl.ds(r, CH), :] = kern
        kern_low = kern.astype(BF)
        for b in range(ATT // 128):
            lanes = slice(b * 128, (b + 1) * 128)
            wide = mm(kern_low, tap_spread(b))
            cs = cv_pad[pl.ds(r, HALO), lanes]
            total = jnp.zeros((CH, 128), F32)
            for j in range(KER):
                moved = cs if j == 4 else pltpu.roll(cs, (HALO - (j - 4)) % HALO, 0)
                total = total + wide[:, j * 128 : (j + 1) * 128] * moved[8 : 8 + CH]
            conv_ref[pl.ds(r, CH), lanes] = total.astype(BF)
        return carry

    lax.fori_loop(0, SEQ // CH, conv, 0)


def enter(pick, tokens, w_in, w_depth, w_point, w_kern):
    rows = tokens.shape[0]
    block = lambda n: pl.BlockSpec((SEQ, n), lambda s: (s, 0))
    return pl.pallas_call(
        enter_kernel,
        grid=(rows // SEQ,),
        in_specs=[
            block(1), block(WIDTH), whole((WIDTH, 4 * ATT)), whole((KER, WIDTH)),
            whole((WIDTH, ATT)), whole((ATT, 128)),
        ],
        out_specs=[block(WIDTH), block(4 * ATT), block(WIDTH), block(ATT), block(128), block(ATT)],
        out_shape=[
            jax.ShapeDtypeStruct((rows, WIDTH), BF),
            jax.ShapeDtypeStruct((rows, 4 * ATT), BF),
            jax.ShapeDtypeStruct((rows, WIDTH), BF),
            jax.ShapeDtypeStruct((rows, ATT), BF),
            jax.ShapeDtypeStruct((rows, 128), F32),
            jax.ShapeDtypeStruct((rows, ATT), BF),
        ],
        scratch_shapes=[pltpu.VMEM((SEQ + 16, WIDTH), F32), pltpu.VMEM((SEQ + 16, ATT), F32)],
        compiler_params=params(1),
        name="enter",
    )(pick, tokens, w_in, w_depth, w_point, w_kern)


def own_lanes(rows, head):
    lane = lax.broadcasted_iota(jnp.int32, (rows, 128), 1)
    return (lane // HEAD) == head


def attend_kernel(q_ref, k_ref, v_ref, p_ref, o_ref, inv_ref):
    k = k_ref[...]
    for head in (0, 1):
        mine = own_lanes(SEQ, head)
        v = jnp.where(mine, v_ref[...].astype(F32), 1.0).astype(BF)

        def part(i, carry):
            r = pl.multiple_of(i * CH, CH)
            mine_q = own_lanes(CH, head)
            q = jnp.where(mine_q, q_ref[pl.ds(r, CH), :].astype(F32) * (HEAD**-0.5), 0.0).astype(BF)
            s = mm_nt(q, k)
            p = jnp.exp(s - jnp.max(s, -1, keepdims=True)).astype(BF)
            p_ref[0, head, pl.ds(r, CH), :] = p
            o = mm(p, v)
            total = jnp.where(mine_q, pltpu.roll(o, HEAD, 1), o)
            inv = 1.0 / total
            res = o * inv
            if head == 0:
                o_ref[pl.ds(r, CH), :] = res.astype(BF)
                inv_ref[pl.ds(r, CH), :] = inv
            else:
                o_ref[pl.ds(r, CH), :] = jnp.where(
                    mine_q, res, o_ref[pl.ds(r, CH), :].astype(F32)
                ).astype(BF)
                inv_ref[pl.ds(r, CH), :] = jnp.where(mine_q, inv, inv_ref[pl.ds(r, CH), :])
            return carry

        lax.fori_loop(0, SEQ // CH, part, 0)


def attend(proj):
    rows = proj.shape[0]
    pairs = HEADS // 2
    col = lambda base: pl.BlockSpec((SEQ, 128), lambda s, p: (s, base + p))
    return pl.pallas_call(
        attend_kernel,
        grid=(rows // SEQ, pairs),
        in_specs=[col(0), col(pairs), col(2 * pairs)],
        out_specs=[pl.BlockSpec((1, 2, SEQ, SEQ), lambda s, p: (s, p, 0, 0)), col(0), col(0)],
        out_shape=[
            jax.ShapeDtypeStruct((rows // SEQ, HEADS, SEQ, SEQ), BF),
            jax.ShapeDtypeStruct((rows, ATT), BF),
            jax.ShapeDtypeStruct((rows, ATT), F32),
        ],
        compiler_params=params(2),
        name="attend",
    )(proj, proj, proj)


ERF_P = 0.3275911 / math.sqrt(2.0)
ERF_A = (0.254829592, -0.284496736, 1.421413741, -1.453152027, 1.061405429)
PHI = 1.0 / math.sqrt(2.0 * math.pi)


def gelu_both(u):
    mag = jnp.abs(u)
    t = 1.0 / (1.0 + ERF_P * mag)
    poly = ERF_A[4]
    for a in ERF_A[3::-1]:
        poly = poly * t + a
    e = jnp.exp(-0.5 * (u * u))
    tail = (0.5 * t) * poly * e
    cdf = jnp.where(u > 0, 1.0 - tail, tail)
    return u * cdf, cdf + (PHI * u) * e


def norm_parts(z):
    mean = jnp.mean(z, -1, keepdims=True)
    centred = z - mean
    var = jnp.mean(centred * centred, -1, keepdims=True)
    r = lax.rsqrt(var + 1e-12)
    return centred * r, r


def norm_back(c, xh, r, gain):
    gc = c * gain
    return r * (gc - jnp.mean(gc, -1, keepdims=True) - xh * jnp.mean(gc * xh, -1, keepdims=True))


def fold_rows(x):
    return jnp.sum(x.reshape(-1, 8, x.shape[-1]), 0)


MID = 256
FF = 1536
FC = 512


def middle_kernel(
    att_ref, conv_ref, inp_ref, cot_ref, w_out_ref, w_up_ref, w_down_ref, vec_ref,
    out_ref, dctx_ref, dfirst_ref, dout_ref, dup_ref, ddown_ref, dvec_ref,
    acc_out, acc_up, acc_down, acc_vec, act_ref, slope_ref,
):
    step = pl.program_id(0)
    last = pl.num_programs(0) - 1

    @pl.when(step == 0)
    def _():
        acc_out[...] = jnp.zeros_like(acc_out)
        acc_up[...] = jnp.zeros_like(acc_up)
        acc_down[...] = jnp.zeros_like(acc_down)
        acc_vec[...] = jnp.zeros_like(acc_vec)

    ctx = jnp.concatenate([att_ref[...], conv_ref[...]], -1)
    g_one, s_one = vec_ref[0:1, :], vec_ref[1:2, :]
    g_two, s_two = vec_ref[2:3, :], vec_ref[3:4, :]
    first_in = mm(ctx, w_out_ref[...]) + inp_ref[...].astype(F32)
    xh_one, r_one = norm_parts(first_in)
    first = xh_one * g_one + s_one
    first_low = first.astype(BF)
    outs = []
    for g in (0, 1):
        cols = slice(g * ATT, (g + 1) * ATT)
        total = None
        for f in range(FF // FC):
            hid = slice(f * FC, (f + 1) * FC)
            inner = mm_nt(first_low[:, cols], w_up_ref[g, hid, :])
            act, slope = gelu_both(inner)
            act = act.astype(BF)
            act_ref[g, :, hid] = act
            slope_ref[g, :, hid] = slope.astype(slope_ref.dtype)
            part = mm(act, w_down_ref[g, hid, :])
            total = part if total is None else total + part
        outs.append(total)
    xh_two, r_two = norm_parts(jnp.concatenate(outs, -1) + first)
    out_ref[...] = (xh_two * g_two + s_two).astype(BF)
    c = cot_ref[...].astype(F32)
    acc_vec[2] += fold_rows(c * xh_two)
    acc_vec[3] += fold_rows(c)
    d_second = norm_back(c, xh_two, r_two, g_two)
    d_outer = d_second.astype(BF)
    d_outer_t = d_second.T.astype(BF)
    first_t = first.T.astype(BF)
    backs = []
    for g in (0, 1):
        cols = slice(g * ATT, (g + 1) * ATT)
        total = None
        for f in range(FF // FC):
            hid = slice(f * FC, (f + 1) * FC)
            d_act = mm_nt(d_outer[:, cols], w_down_ref[g, hid, :])
            d_inner = (d_act * slope_ref[g, :, hid].astype(F32)).astype(BF)
            acc_down[g, :, hid] += mm(d_outer_t[cols, :], act_ref[g, :, hid])
            acc_up[g, :, hid] += mm(first_t[cols, :], d_inner)
            part = mm(d_inner, w_up_ref[g, hid, :])
            total = part if total is None else total + part
        backs.append(total)
    d_first = jnp.concatenate(backs, -1) + d_second
    acc_vec[0] += fold_rows(d_first * xh_one)
    acc_vec[1] += fold_rows(d_first)
    d_first_in = norm_back(d_first, xh_one, r_one, g_one)
    dfirst_ref[...] = d_first_in
    d_dense = d_first_in.astype(BF)
    acc_out[...] += mm_tn(ctx, d_dense)
    dctx_ref[...] = mm_nt(d_dense, w_out_ref[...]).astype(BF)

    @pl.when(step == last)
    def _():
        dout_ref[...] = acc_out[...].astype(dout_ref.dtype)
        for g in (0, 1):
            dup_ref[g] = acc_up[g].T.astype(dup_ref.dtype)
            ddown_ref[g] = acc_down[g].T.astype(ddown_ref.dtype)
        dvec_ref[...] = jnp.sum(acc_vec[...], 1)


def middle(att, conv, inputs, cot, w_out, w_up, w_down, vecs, grad_type=BF):
    rows = att.shape[0]
    block = lambda n: pl.BlockSpec((MID, n), lambda s: (s, 0))
    return pl.pallas_call(
        middle_kernel,
        grid=(rows // MID,),
        in_specs=[
            block(ATT), block(ATT), block(WIDTH), block(WIDTH),
            whole((WIDTH, WIDTH)), whole((2, FF, ATT)), whole((2, FF, ATT)), whole((4, WIDTH)),
        ],
        out_specs=[
            block(WIDTH), block(WIDTH), block(WIDTH), whole_out((WIDTH, WIDTH)),
            whole_out((2, FF, ATT)), whole_out((2, FF, ATT)), whole_out((4, WIDTH)),
        ],
        out_shape=[
            jax.ShapeDtypeStruct((rows, WIDTH), BF),
            jax.ShapeDtypeStruct((rows, WIDTH), BF),
            jax.ShapeDtypeStruct((rows, WIDTH), F32),
            jax.ShapeDtypeStruct((WIDTH, WIDTH), grad_type),
            jax.ShapeDtypeStruct((2, FF, ATT), grad_type),
            jax.ShapeDtypeStruct((2, FF, ATT), grad_type),
            jax.ShapeDtypeStruct((4, WIDTH), F32),
        ],
        scratch_shapes=[
            pltpu.VMEM((WIDTH, WIDTH), F32),
            pltpu.VMEM((2, ATT, FF), F32),
            pltpu.VMEM((2, ATT, FF), F32),
            pltpu.VMEM((4, 8, WIDTH), F32),
            pltpu.VMEM((2, MID, FF), BF),
            pltpu.VMEM((2, MID, FF), F32),
        ],
        compiler_params=params(1),
        name="middle",
    )(att, conv, inputs, cot, w_out, w_up, w_down, vecs)


def conv_back_kernel(
    dconv_ref, kern_ref, q_ref, cv_ref, ck_ref, spread_ref, inp_ref, w_depth_ref, w_point_ref, w_kern_ref,
    dq_ref, dcv_ref, din_ref, dpoint_ref, dkern_ref, ddepth_ref,
    x_pad, cv_pad, dc_pad, kl_pad, ds_pad, acc_point, acc_kern, acc_depth,
):
    step = pl.program_id(0)
    last = pl.num_programs(0) - 1
    zero = lambda n: jnp.zeros((8, n), F32)
    for ref, n in ((x_pad, WIDTH), (cv_pad, ATT), (dc_pad, ATT), (kl_pad, 128), (ds_pad, WIDTH)):
        ref[0:8, :] = zero(n)
        ref[SEQ + 8 : SEQ + 16, :] = zero(n)

    @pl.when(step == 0)
    def _():
        acc_point[...] = jnp.zeros_like(acc_point)
        acc_kern[...] = jnp.zeros_like(acc_kern)
        acc_depth[...] = jnp.zeros_like(acc_depth)

    def fill(i, carry):
        r = pl.multiple_of(i * CH, CH)
        rows = pl.ds(r, CH)
        there = pl.ds(r + 8, CH)
        x_pad[there, :] = inp_ref[rows, :].astype(F32)
        cv_pad[there, :] = cv_ref[rows, :].astype(F32)
        dc_pad[there, :] = dconv_ref[rows, :].astype(F32)
        kl_pad[there, :] = kern_ref[rows, :]
        return carry

    lax.fori_loop(0, SEQ // CH, fill, 0)

    def back(i, carry):
        r = pl.multiple_of(i * CH, CH)
        rows = pl.ds(r, CH)
        d_kern = jnp.zeros((CH, 128), F32)
        kl = kl_pad[pl.ds(r, HALO), :].astype(BF)
        for b in range(ATT // 128):
            lanes = slice(b * 128, (b + 1) * 128)
            spreader = tap_spread(b)
            cs = cv_pad[pl.ds(r, HALO), lanes]
            dc = dc_pad[pl.ds(r + 8, CH), lanes]
            prods = []
            for j in range(KER):
                moved = cs if j == 4 else pltpu.roll(cs, (HALO - (j - 4)) % HALO, 0)
                prods.append((dc * moved[8 : 8 + CH]).astype(BF))
            d_kern = d_kern + mm_nt(jnp.concatenate(prods, -1), spreader)
            wide = mm(kl, spreader)
            dch = dc_pad[pl.ds(r, HALO), lanes]
            total = jnp.zeros((CH, 128), F32)
            for j in range(KER):
                term = wide[:, j * 128 : (j + 1) * 128] * dch
                moved = term if j == 4 else pltpu.roll(term, (HALO + (j - 4)) % HALO, 0)
                total = total + moved[8 : 8 + CH]
            dcv_ref[rows, lanes] = total.astype(BF)
        kern = kern_ref[rows, :]
        dot_rows = lane_groups(kern * d_kern, jnp.add)
        d_logits = (kern * (d_kern - dot_rows)).astype(BF)
        q = q_ref[rows, :].astype(F32)
        ck = ck_ref[rows, :].astype(F32)
        mixed = (ck * q).astype(BF)
        acc_kern[...] += mm_tn(mixed, d_logits)
        d_mixed = mm_nt(d_logits, w_kern_ref[...])
        dq_ref[rows, :] = d_mixed * ck
        d_ck = (d_mixed * q).astype(BF)
        acc_point[...] += mm_tn(spread_ref[rows, :], d_ck)
        ds_pad[pl.ds(r + 8, CH), :] = mm_nt(d_ck, w_point_ref[...])
        return carry

    lax.fori_loop(0, SEQ // CH, back, 0)

    def depth(i, carry):
        r = pl.multiple_of(i * CH, CH)
        rows = pl.ds(r, CH)
        for b in range(WIDTH // 128):
            lanes = slice(b * 128, (b + 1) * 128)
            dsh = ds_pad[pl.ds(r, HALO), lanes]
            tap = lambda j: w_depth_ref[j : j + 1, lanes]
            shifted = [dsh] + [pltpu.roll(dsh, s, 0) for s in (1, 2, 3)]
            low_part = sum(tap(s) * shifted[s] for s in range(4))
            mid_part = sum(tap(4 + s) * shifted[s] for s in range(4))
            high_part = tap(8) * dsh
            low_part = pltpu.roll(low_part, HALO - 4, 0)
            high_part = pltpu.roll(high_part, 4, 0)
            din_ref[rows, lanes] = (low_part + mid_part + high_part)[8 : 8 + CH]
            xs = x_pad[pl.ds(r + 8, CH), lanes]
            far_low = [pltpu.roll(shifted[s], HALO - 4, 0) for s in range(4)]
            far_high = pltpu.roll(dsh, 4, 0)
            for j in range(KER):
                src = far_low[j] if j < 4 else (shifted[j - 4] if j < 8 else far_high)
                acc_depth[j, :, lanes] += fold_rows(src[8 : 8 + CH] * xs)
        return carry

    lax.fori_loop(0, SEQ // CH, depth, 0)

    @pl.when(step == last)
    def _():
        dpoint_ref[...] = acc_point[...].astype(dpoint_ref.dtype)
        dkern_ref[...] = acc_kern[...]
        ddepth_ref[...] = jnp.sum(acc_depth[...], 1)


def conv_back(dctx, kern, proj, ck, spread, inputs, w_depth, w_point, w_kern, grad_type=BF):
    rows = inputs.shape[0]
    block = lambda n: pl.BlockSpec((SEQ, n), lambda s: (s, 0))
    at = lambda c: pl.BlockSpec((SEQ, ATT), lambda s: (s, c))
    return pl.pallas_call(
        conv_back_kernel,
        grid=(rows // SEQ,),
        in_specs=[
            at(1), block(128), at(0), at(3), block(ATT), block(WIDTH), block(WIDTH),
            whole((KER, WIDTH)), whole((WIDTH, ATT)), whole((ATT, 128)),
        ],
        out_specs=[
            block(ATT), block(ATT), block(WIDTH), whole_out((WIDTH, ATT)), whole_out((ATT, 128)),
            whole_out((KER, WIDTH)),
        ],
        out_shape=[
            jax.ShapeDtypeStruct((rows, ATT), F32),
            jax.ShapeDtypeStruct((rows, ATT), BF),
            jax.ShapeDtypeStruct((rows, WIDTH), F32),
            jax.ShapeDtypeStruct((WIDTH, ATT), grad_type),
            jax.ShapeDtypeStruct((ATT, 128), F32),
            jax.ShapeDtypeStruct((KER, WIDTH), F32),
        ],
        scratch_shapes=[
            pltpu.VMEM((SEQ + 16, WIDTH), F32),
            pltpu.VMEM((SEQ + 16, ATT), F32),
            pltpu.VMEM((SEQ + 16, ATT), F32),
            pltpu.VMEM((SEQ + 16, 128), F32),
            pltpu.VMEM((SEQ + 16, WIDTH), F32),
            pltpu.VMEM((WIDTH, ATT), F32),
            pltpu.VMEM((ATT, 128), F32),
            pltpu.VMEM((KER, 8, WIDTH), F32),
        ],
        compiler_params=params(1),
        name="conv_back",
    )(dctx, kern, proj, proj, ck, spread, inputs, w_depth, w_point, w_kern)


def attend_back_kernel(
    q_ref, k_ref, v_ref, p_ref, o_ref, inv_ref, datt_ref, dqc_ref, dq_ref, dk_ref, dv_ref, acc_k, acc_v
):
    scale = HEAD**-0.5
    acc_k[...] = jnp.zeros_like(acc_k)
    acc_v[...] = jnp.zeros_like(acc_v)
    v = v_ref[...]

    def part(i, carry):
        r = pl.multiple_of(i * CH, CH)
        rows = pl.ds(r, CH)
        d_att = datt_ref[rows, :].astype(F32) * inv_ref[rows, :]
        o = o_ref[rows, :].astype(F32)
        dq = dqc_ref[rows, :]
        for head in (0, 1):
            mine = own_lanes(CH, head)
            da = jnp.where(mine, d_att, 0.0)
            dot_rows = jnp.sum(da * o, -1, keepdims=True)
            da = da.astype(BF)
            p = p_ref[0, head, rows, :]
            ds = mm_nt(da, v)
            ds = (p.astype(F32) * (ds - dot_rows)).astype(BF)
            k_own = jnp.where(own_lanes(SEQ, head), k_ref[...].astype(F32) * scale, 0.0).astype(BF)
            dq = dq + mm(ds, k_own)
            q_own = jnp.where(mine, q_ref[rows, :].astype(F32) * scale, 0.0)
            acc_k[...] += mm_tn(ds, q_own.astype(BF))
            acc_v[...] += mm_tn(p, da)
        dq_ref[rows, :] = dq.astype(BF)
        return carry

    lax.fori_loop(0, SEQ // CH, part, 0)
    dk_ref[...] = acc_k[...].astype(BF)
    dv_ref[...] = acc_v[...].astype(BF)


def attend_back(proj, probs, att, inv, dctx, dq_conv):
    rows = proj.shape[0]
    pairs = HEADS // 2
    col = lambda base: pl.BlockSpec((SEQ, 128), lambda s, p: (s, base + p))
    return pl.pallas_call(
        attend_back_kernel,
        grid=(rows // SEQ, pairs),
        in_specs=[
            col(0), col(pairs), col(2 * pairs),
            pl.BlockSpec((1, 2, SEQ, SEQ), lambda s, p: (s, p, 0, 0)),
            col(0), col(0), col(0), col(0),
        ],
        out_specs=[col(0)] * 3,
        out_shape=[jax.ShapeDtypeStruct((rows, ATT), BF)] * 3,
        scratch_shapes=[pltpu.VMEM((SEQ, 128), F32), pltpu.VMEM((SEQ, 128), F32)],
        compiler_params=params(2),
        name="attend_back",
    )(proj, proj, proj, probs, att, inv, dctx, dq_conv)


def weight_kernel(inp_ref, dq_ref, dk_ref, dv_ref, dcv_ref, din_ref, acc):
    step = pl.program_id(0)
    last = pl.num_programs(0) - 1
    inp_t = inp_ref[...].astype(F32).T.astype(BF)
    for i, ref in enumerate((dq_ref, dk_ref, dv_ref, dcv_ref)):
        cols = slice(i * ATT, (i + 1) * ATT)
        part = mm(inp_t, ref[...])

        @pl.when(step == 0)
        def _():
            acc[:, cols] = part

        @pl.when(step > 0)
        def _():
            acc[:, cols] += part

    @pl.when(step == last)
    def _():
        din_ref[...] = acc[...].astype(din_ref.dtype)


def weight_grad(inputs, dq, dk, dv, dcv, grad_type=BF):
    rows = inputs.shape[0]
    block = lambda n: pl.BlockSpec((512, n), lambda s: (s, 0))
    return pl.pallas_call(
        weight_kernel,
        grid=(rows // 512,),
        in_specs=[block(WIDTH)] + [block(ATT)] * 4,
        out_specs=whole_out((WIDTH, 4 * ATT)),
        out_shape=jax.ShapeDtypeStruct((WIDTH, 4 * ATT), grad_type),
        scratch_shapes=[pltpu.VMEM((WIDTH, 4 * ATT), F32)],
        compiler_params=params(1),
        name="weight_grad",
    )(inputs, dq, dk, dv, dcv)


def leave_kernel(
    dq_ref, dk_ref, dv_ref, dcv_ref, conv_ref, first_ref, mask_ref, to_ref, w_in_ref, out_ref, moved
):
    def make(i, carry):
        rows = pl.ds(pl.multiple_of(i * CH, CH), CH)
        total = conv_ref[rows, :] + first_ref[rows, :]
        for n, ref in enumerate((dq_ref, dk_ref, dv_ref, dcv_ref)):
            total = total + mm_nt(ref[rows, :], w_in_ref[:, n * ATT : (n + 1) * ATT])
        moved[rows, :] = total.astype(BF)
        out_ref[rows, :] = jnp.where(mask_ref[rows, :] == 1, 0.0, total)
        return carry

    lax.fori_loop(0, SEQ // CH, make, 0)

    def scatter(i, carry):
        r = pl.multiple_of(i * CH, CH)
        rows = pl.ds(r, CH)
        target = lax.broadcasted_iota(jnp.int32, (CH, SEQ), 0) + r
        hot = (target == to_ref[0]).astype(F32).astype(BF)
        out_ref[rows, :] += mm(hot, moved[...])
        return carry

    lax.fori_loop(0, SEQ // CH, scatter, 0)


def leave(dq, dk, dv, dcv, d_conv_in, d_first_in, mask_col, to_row, w_in):
    rows = dq.shape[0]
    block = lambda n: pl.BlockSpec((SEQ, n), lambda s: (s, 0))
    return pl.pallas_call(
        leave_kernel,
        grid=(rows // SEQ,),
        in_specs=[block(ATT)] * 4
        + [block(WIDTH)] * 2
        + [block(1), pl.BlockSpec((1, 1, SEQ), lambda s: (s, 0, 0)), whole((WIDTH, 4 * ATT))],
        out_specs=block(WIDTH),
        out_shape=jax.ShapeDtypeStruct((rows, WIDTH), F32),
        scratch_shapes=[pltpu.VMEM((SEQ, WIDTH), BF)],
        compiler_params=params(1),
        name="leave",
    )(dq, dk, dv, dcv, d_conv_in, d_first_in, mask_col, to_row, w_in)


def pack_taps(kernel_full):
    by_tap = kernel_full.reshape(ATT, HEADS, KER).transpose(0, 2, 1)
    return jnp.pad(by_tap, ((0, 0), (0, 16 - KER), (0, 8 - HEADS))).reshape(ATT, 128)


def unpack_taps(packed):
    return packed.reshape(ATT, 16, 8)[:, :KER, :HEADS].transpose(0, 2, 1).reshape(ATT, HEADS * KER)


AXES = ("dp", "fsdp")
LANES = 384


def as_rows(x):
    flat = x.reshape(-1)
    return jnp.pad(flat, (0, -flat.size % LANES)).reshape(-1, LANES)


def per_device(
    tokens,
    masked,
    replace_ids,
    in_weight,
    depth_weight,
    point_weight,
    kernel_weight,
    out_weight,
    gain_one,
    shift_one,
    ffn_in,
    feedforward_output,
    gain_two,
    shift_two,
    cotangent,
):
    rows = tokens.shape[0]
    seqs = rows // SEQ
    dp, fsdp = lax.axis_size("dp"), lax.axis_size("fsdp")
    devices = dp * fsdp
    own = in_weight.shape[0]
    hit = masked == 1
    here = jnp.arange(rows, dtype=jnp.int32) % SEQ
    pick = jnp.where(hit, replace_ids, here)[:, None]
    to_row = jnp.where(hit, replace_ids, -1).reshape(seqs, 1, SEQ)

    vec_own = jnp.stack([gain_one, shift_one, gain_two, shift_two])
    small = as_rows(
        jnp.concatenate([depth_weight.reshape(-1), vec_own.reshape(-1), kernel_weight.reshape(-1)])
    )
    head_own = jnp.concatenate([in_weight.reshape(-1, LANES), point_weight, small])
    head = lax.all_gather(head_own, AXES, axis=0)
    mid_own = jnp.concatenate(
        [
            out_weight.reshape(-1, LANES),
            ffn_in.transpose(0, 2, 1).reshape(-1, LANES),
            feedforward_output.reshape(-1, LANES),
        ]
    )
    mid = lax.all_gather(mid_own, AXES, axis=0)
    w_in = head[:, : 4 * own].reshape(WIDTH, 4 * ATT)
    w_point = head[:, 4 * own : 5 * own].reshape(WIDTH, ATT)
    small_all = head[:, 5 * own :].reshape(devices, -1)
    n_depth, n_vec = KER * own, 4 * own
    w_depth = small_all[:, :n_depth].reshape(devices, KER, own).transpose(1, 0, 2).reshape(KER, WIDTH)
    vecs = small_all[:, n_depth : n_depth + n_vec].reshape(devices, 4, own).transpose(1, 0, 2)
    vecs = vecs.reshape(4, WIDTH).astype(F32)
    w_depth = w_depth.astype(F32)
    kern_full = small_all[:fsdp, n_depth + n_vec :][:, : kernel_weight.size].reshape(ATT, HEADS * KER)
    w_kern = pack_taps(kern_full)
    hid = ffn_in.shape[2]
    w_out = mid[:, : 2 * own].reshape(WIDTH, WIDTH)
    up = mid[:, 2 * own : 2 * own + 2 * hid].reshape(devices, 2, hid, ATT)
    w_up_t = up.transpose(1, 0, 2, 3).reshape(2, FF, ATT)
    down = mid[:, 2 * own + 2 * hid :].reshape(devices, 2, hid, ATT)
    w_down = down.transpose(1, 0, 2, 3).reshape(2, FF, ATT)

    inputs, proj, spread, ck, kern, conv = enter(pick, tokens, w_in, w_depth, w_point, w_kern)
    probs, att, inv = attend(proj)
    out, dctx, d_first_in, d_out, d_up_t, d_down, d_vecs = middle(
        att, conv, inputs, cotangent, w_out, w_up_t, w_down, vecs
    )
    split = lambda g: g.reshape(2, devices, hid, ATT).transpose(1, 0, 2, 3).reshape(devices, -1, LANES)
    mid_grads = jnp.concatenate(
        [d_out.reshape(devices, -1, LANES), split(d_up_t), split(d_down)], 1
    )
    mid_sum = lax.psum_scatter(mid_grads, AXES, scatter_dimension=0, tiled=True)[0]
    dq_conv, dcv, d_conv_in, d_point, d_kern, d_depth = conv_back(
        dctx, kern, proj, ck, spread, inputs, w_depth, w_point, w_kern
    )
    dq, dk, dv = attend_back(proj, probs, att, inv, dctx, dq_conv)
    d_in = weight_grad(inputs, dq, dk, dv, dcv)
    by_owner = lambda g: g.reshape(-1, devices, own).transpose(1, 0, 2).reshape(devices, -1)
    kern_by = jnp.tile(unpack_taps(d_kern).reshape(fsdp, -1), (dp, 1))
    small_grad = jnp.concatenate([by_owner(d_depth), by_owner(d_vecs), kern_by], 1).astype(BF)
    small_grad = jnp.pad(small_grad, ((0, 0), (0, -small_grad.shape[1] % LANES)))
    tail = jnp.concatenate(
        [
            d_in.reshape(devices, -1, LANES),
            d_point.reshape(devices, -1, LANES),
            small_grad.reshape(devices, -1, LANES),
        ],
        1,
    )
    tail_sum = lax.psum_scatter(tail, AXES, scatter_dimension=0, tiled=True)[0]
    d_tokens = leave(dq, dk, dv, dcv, d_conv_in, d_first_in, masked[:, None], to_row, w_in)

    scale = 1.0 / math.sqrt(rows * devices)
    mid_sum = mid_sum.astype(F32) * scale
    tail_sum = tail_sum.astype(F32) * scale
    small_sum = tail_sum[5 * own :].reshape(-1)
    vec_sum = small_sum[n_depth : n_depth + n_vec].reshape(4, own)
    kern_sum = small_sum[n_depth + n_vec :][: kernel_weight.size].reshape(kernel_weight.shape)
    return (
        out,
        d_tokens,
        tail_sum[: 4 * own].reshape(own, 4 * ATT),
        small_sum[:n_depth].reshape(KER, own),
        tail_sum[4 * own : 5 * own],
        kern_sum,
        mid_sum[: 2 * own].reshape(own, WIDTH),
        vec_sum[0],
        vec_sum[1],
        mid_sum[2 * own : 2 * own + 2 * hid].reshape(2, hid, ATT).transpose(0, 2, 1),
        mid_sum[2 * own + 2 * hid :].reshape(2, hid, ATT),
        vec_sum[2],
        vec_sum[3],
    )


def solution(mesh):
    return jax.shard_map(
        per_device,
        mesh=mesh,
        in_specs=(
            P(("dp", "fsdp"), None),
            P(("dp", "fsdp")),
            P(("dp", "fsdp")),
            P(("dp", "fsdp"), None),
            P(None, ("dp", "fsdp")),
            P(("dp", "fsdp"), None),
            P("fsdp", None),
            P(("dp", "fsdp"), None),
            P(("dp", "fsdp")),
            P(("dp", "fsdp")),
            P(None, None, ("dp", "fsdp")),
            P(None, ("dp", "fsdp"), None),
            P(("dp", "fsdp")),
            P(("dp", "fsdp")),
            P(("dp", "fsdp"), None),
        ),
        out_specs=(
            P(("dp", "fsdp"), None),
            P(("dp", "fsdp"), None),
            P(("dp", "fsdp"), None),
            P(None, ("dp", "fsdp")),
            P(("dp", "fsdp"), None),
            P("fsdp", None),
            P(("dp", "fsdp"), None),
            P(("dp", "fsdp")),
            P(("dp", "fsdp")),
            P(None, None, ("dp", "fsdp")),
            P(None, ("dp", "fsdp"), None),
            P(("dp", "fsdp")),
            P(("dp", "fsdp")),
        ),
        check_vma=False,
    )
```

time: 1450 us -> 578 us (0.40)
  matrix products: 354 us -> 0 us
  other arithmetic: 288 us -> 15.8 us
  Pallas kernels: 0 us -> 268 us
  blocking collectives: 262 us -> 0 us
  local copies, waits for them, and re-layouts: 213 us -> 44 us
  waiting for transfers between devices: 303 us -> 236 us
    dot_general x32 -> x0, matrix products: 354 us -> none  [the longest x1 63.7 us: per_device(): jnp.einsum('ngc,gcf->ngf', grouped, w_up, preferred_element_type=jnp.floa...]
    pallas_call x0 -> x7, Pallas kernels: none -> 268 us  [the longest x1 81.3 us: middle(): pl.pallas_call(middle_kernel, grid=(rows // MID,), in_specs=[block(ATT),...]
    all_gather x3 -> x0, blocking collectives: 171 us -> none  [the longest x1 74.5 us: collect(): lax.all_gather(point_weight, ('dp', 'fsdp'), axis=0, tiled=True)]
    reduce_scatter x5 -> x2, waiting for transfers between devices: 300 us -> 179 us  [the longest x1 113 us: per_device(): lax.psum_scatter(mid_grads, AXES, scatter_dimension=0, tiled=True)[0]]
    unnamed x2 -> x0, blocking collectives: 80.5 us -> none
    reduce_sum x12 -> x0, other arithmetic: 67.6 us -> none  [the longest x1 29 us: dynamic_conv(): kernels[..., offset:offset + 1]]
    convert_element_type x10 -> x2, other arithmetic: 63.8 us -> 0.08 us  [the longest x1 0.07 us: per_device(): vecs = vecs.reshape(4, WIDTH).astype(F32)]
    dynamic_update_slice x4 -> x0, local copies, waits for them, and re-layouts: 58.2 us -> none  [per_device(): lax.map(attend_forward, (query_heads, key_heads, value_heads))]
  transfers between devices with their start and end apart: 10 -> 4, of which waited for: 3 -> 3; matrix products, arithmetic and copies ran while one was open for 35% -> 6% of each run, Pallas kernels for 0% -> 17%
where the time goes in v1:
time: 578 us; the launch traced here: 577 us
  Pallas kernels  268 us (46%)
  waiting for transfers between devices  236 us (41%)
  local copies, waits for them, and re-layouts  44 us (8%)
  other arithmetic  15.8 us (3%)
  between operations  14.1 us (2%)
    reduce_scatter x1, waiting for transfers between devices, per_device(): lax.psum_scatter(mid_grads, AXES, scatter_dimension=0, tiled=True)[0]  113 us
    pallas_call x1, Pallas kernels, middle(): pl.pallas_call(middle_kernel, grid=(rows // MID,), in_specs=[block(ATT),...  81.3 us
    reduce_scatter x1, waiting for transfers between devices, per_device(): tail_sum = lax.psum_scatter(tail, AXES, scatter_dimension=0, tiled=True)[0]  66.5 us
    all_gather x1, waiting for transfers between devices, per_device(): head = lax.all_gather(head_own, AXES, axis=0)  56.1 us
    pallas_call x1, Pallas kernels, conv_back(): pl.pallas_call(conv_back_kernel, grid=(rows // SEQ,), in_specs=[at(1), bl...  39.4 us
    pallas_call x1, Pallas kernels, attend(): pl.pallas_call(attend_kernel, grid=(rows // SEQ, pairs), in_specs=[col(0)...  37.6 us
    pallas_call x1, Pallas kernels, enter(): pl.pallas_call(enter_kernel, grid=(rows // SEQ,), in_specs=[block(1), blo...  37.6 us
    pallas_call x1, Pallas kernels, attend_back(): pl.pallas_call(attend_back_kernel, grid=(rows // SEQ, pairs), in_specs=[c...  36.5 us
  transfers between devices with their start and end apart: 4, of which 3 were waited for; matrix products, arithmetic and copies ran while one was open for 6% of the time, Pallas kernels for 17%

profile of v1, /device:TPU:0, one launch (start us, length us, event | category | flops | bytes accessed | tf_op | source)
XLA Modules:
  0.0 577.2 jit_solution(12453553952988022178)
XLA Ops:
  12.9 1.6 pad_maximum_fusion.2
  18.0 56.1 %all-gather.5.cloned.1.call-done = bf16[4096,384]{1,0:T(8,128)(2,1)} async-done(((bf16[128,384]{1,0:T(8,128)(2,1)}), bf16[4096,384]{1,0:T(8,128)(2,1)}) %all-gather.5.cloned.1.call-update) | async-done | bytes 3145744 | tf_op jit(solution)/shard_map/all_gather | solution.py:685
  75.0 1.9 slice.114
  76.9 2.0 slice.117
  82.0 2.7 reshape.192.w_in_ref
  84.7 37.6 %enter.1 = (bf16[2048,768]{1,0:T(8,128)(2,1)}, bf16[2048,1536]{1,0:T(8,128)(2,1)}, bf16[2048,768]{1,0:T(8,128)(2,1)}, bf16[2048,384]{1,0:T(8,128)(2,1)}, f32[2048,128]{1,0:T(8,128)}, /*index=5*/bf16[2048,384]{1,0:T(8,128)(2,1)}) custom-call(s32[2048,1]{1,0:T(8,128)} %copy.50.pick_ref, bf16[2048,768]{1,0:T(8,128)(2,1)} %tok_ref.1, ...), custom_call_target="tpu_custom_call" | custom-call | tf_op jit(solution)/shard_map/enter/pallas_call | solution.py:137
  122.2 37.6 %attend.1 = (bf16[2,6,1024,1024]{3,2,1,0:T(8,128)(2,1)}, bf16[2048,384]{1,0:T(8,128)(2,1)}, f32[2048,384]{1,0:T(8,128)}) custom-call(bf16[2048,1536]{1,0:T(8,128)(2,1)} %get-tuple-element.38.q_ref.k_ref.v_ref.cv_ref, bf16[2048,1536]{1,0:T(8,128)(2,1)} %get-tuple-element.38.q_ref.k_ref.v_ref.cv_ref, bf16[2048,1536]{1,0:T(8,128)(2,1)} %get-tuple-element.38.q_ref.k_ref.v_ref.cv_ref), custom_call_target="tpu_custom_call" | custom-call | tf_op jit(solution)/shard_map/attend/pallas_call | solution.py:198
  160.8 2.9 fusion.5
  163.6 1.4 slice.119
  165.0 1.6 copy.52
  166.6 1.6 copy.53
  169.5 81.3 %middle.1 = (bf16[2048,768]{1,0:T(8,128)(2,1)}, bf16[2048,768]{1,0:T(8,128)(2,1)}, f32[2048,768]{1,0:T(8,128)}, bf16[768,768]{1,0:T(8,128)(2,1)}, bf16[2,1536,38...) custom-call(bf16[2048,384]{1,0:T(8,128)(2,1)} %get-tuple-element.39.att_ref.o_ref, ...), custom_call_target="tpu_custom_call" | custom-call | tf_op jit(solution)/shard_map/middle/pallas_call | solution.py:331
  250.8 39.4 %conv_back.1 = (f32[2048,384]{1,0:T(8,128)}, bf16[2048,384]{1,0:T(8,128)(2,1)}, f32[2048,768]{1,0:T(8,128)}, bf16[768,384]{1,0:T(8,128)(2,1)}, f32[384,128]{1,0:T(8,128)}, /*index=5*/f32[9,768]{1,0:T(8,128)}) custom-call(bf16[2048,768]{1,0:T(8,128)(2,1)} %get-tuple-element.45.dconv_ref.datt_ref, f32[2048,128]{1,0:T(8,128)} %get-tuple-element.46.kern_ref, ...), custom_call_target="tpu_custom_call" | custom-call | tf_op jit(solution)/shard_map/conv_back/pallas_call | solution.py:468
  290.2 36.5 %attend_back.1 = (bf16[2048,384]{1,0:T(8,128)(2,1)}, bf16[2048,384]{1,0:T(8,128)(2,1)}, bf16[2048,384]{1,0:T(8,128)(2,1)}) custom-call(bf16[2048,1536]{1,0:T(8,128)(2,1)} %get-tuple-element.38.q_ref.k_ref.v_ref.cv_ref, bf16[2048,1536]{1,0:T(8,128)(2,1)} %get-tuple-element.38.q_ref.k_ref.v_ref.cv_ref, ...), custom_call_target="tpu_custom_call" | custom-call | tf_op jit(solution)/shard_map/attend_back/pallas_call | solution.py:541
  326.7 14.4 %weight_grad.1 = bf16[768,1536]{1,0:T(8,128)(2,1)} custom-call(bf16[2048,768]{1,0:T(8,128)(2,1)} %get-tuple-element.41.inp_ref, bf16[2048,384]{1,0:T(8,128)(2,1)} %get-tuple-element.50.dq_ref, bf16[2048,384]{1,0:T(8,128)(2,1)} %get-tuple-element.51.dk_ref, bf16[2048,384]{1,0:T(8,128)(2,1)} %get-tuple-element.52.dv_ref, ...), custom_call_target="tpu_custom_call" | custom-call | tf_op jit(solution)/shard_map/weight_grad/pallas_call | solution.py:581
  341.0 3.9 reshape.205
  347.2 3.3 pad_maximum_fusion.1
  350.6 2.1 copy.62
  352.9 1.7 copy.63
  354.6 2.2 reshape.216
  356.8 4.8 pad_maximum_fusion
  363.7 20.9 %leave.1 = f32[2048,768]{1,0:T(8,128)} custom-call(bf16[2048,384]{1,0:T(8,128)(2,1)} %get-tuple-element.50.dq_ref, bf16[2048,384]{1,0:T(8,128)(2,1)} %get-tuple-element.51.dk_ref, bf16[2048,384]{1,0:T(8,128)(2,1)} %get-tuple-element.52.dv_ref, bf16[2048,384]{1,0:T(8,128)(2,1)} %get-tuple-element.53.dcv_ref, f32[2048,768]{1,0:T(8,128)} %get-tuple-element.54.conv_ref, ...), custom_call_target="tpu_custom_call" | custom-call | tf_op jit(solution)/shard_map/leave/pallas_call | solution.py:621
  384.5 66.5 %reduce-scatter.3.cloned.1.call-done = bf16[1,128,384]{2,1,0:T(8,128)(2,1)} async-done(((bf16[32,128,384]{2,1,0:T(8,128)(2,1)}), bf16[1,128,384]{2,1,0:T(8,128)(2,1)}) %reduce-scatter.3.cloned.1.call-update) | async-done | bytes 98320 | tf_op jit(solution)/shard_map/reduce_scatter | solution.py:738
  455.4 112.9 %reduce-scatter.5.cloned.1.call-done = bf16[1,240,384]{2,1,0:T(8,128)(2,1)} async-done(((bf16[32,240,384]{2,1,0:T(8,128)(2,1)}), bf16[1,240,384]{2,1,0:T(8,128)(2,1)}) %reduce-scatter.5.cloned.1.call-update) | async-done | bytes 184336 | tf_op jit(solution)/shard_map/reduce_scatter | solution.py:720
  (80 shorter events, 26.4 us)
Async XLA Ops:
  7.2 66.9 %all-gather.5.cloned.1.call-start = ((), (), s32[]{:S(2)}) async-start(), calls=%async_computation.4 | async-start | bytes 3244032 | tf_op jit(solution)/shard_map/all_gather | solution.py:685
  12.1 148.7 %all-gather.7.cloned.1.call-start = ((), (), s32[]{:S(2)}) async-start(), calls=%async_computation.5 | async-start | bytes 6082560 | tf_op jit(solution)/shard_map/all_gather | solution.py:693
  14.6 436.5 %reduce-scatter.3.cloned.1.call-start = ((), (), s32[]{:S(2)}) async-start(), calls=%async_computation.2 | async-start | bytes 3244032 | tf_op jit(solution)/shard_map/reduce_scatter | solution.py:738
  341.0 3.9 copy-start.1
  341.0 5.3 copy-start.2
  341.0 5.6 copy-start.4
  350.5 217.8 %reduce-scatter.5.cloned.1.call-start = ((), (), s32[]{:S(2)}) async-start(), calls=%async_computation.3 | async-start | bytes 6082560 | tf_op jit(solution)/shard_map/reduce_scatter | solution.py:720
  350.6 2.4 copy-start
  361.6 0.7 copy-start.3
Sparse Core Ops, SparseCore 0:
  12.2 61.7 all-gather.4
  77.0 66.9 all-gather.6
  350.6 100.3 reduce-scatter.2
  456.6 111.6 reduce-scatter.4

commit v2 on v1

v2 whole, which is shorter than its diff:
```python
from functools import partial
import math

import jax
import jax.numpy as jnp
from jax import lax
from jax.experimental import pallas as pl
from jax.experimental.pallas import tpu as pltpu
from jax.sharding import PartitionSpec as P

BF = jnp.bfloat16
F32 = jnp.float32
HEADS = 6
HEAD = 64
SEQ = 1024
KER = 9
ATT = HEADS * HEAD
WIDTH = 768
VMEM_MAX = 60 * 1024 * 1024


def mm(a, b):
    return jnp.dot(a, b, preferred_element_type=F32)


def mm_nt(a, b):
    return lax.dot_general(a, b, (((1,), (1,)), ((), ())), preferred_element_type=F32)


def mm_tn(a, b):
    return lax.dot_general(a, b, (((0,), (0,)), ((), ())), preferred_element_type=F32)


def params(count):
    return pltpu.CompilerParams(
        dimension_semantics=("arbitrary",) * count, vmem_limit_bytes=VMEM_MAX
    )


def cost(flops, moved):
    return pl.CostEstimate(flops=int(flops), bytes_accessed=int(moved), transcendentals=0)


def whole(shape):
    zeros = (0,) * len(shape)
    return pl.BlockSpec(shape, lambda *_: zeros, pipeline_mode=pl.Buffered(1))


def whole_out(shape):
    zeros = (0,) * len(shape)
    return pl.BlockSpec(shape, lambda *_: zeros)


AXES = ("dp", "fsdp")
LANES = 384
NEAR = {"dp": 4, "fsdp": 8}
X_BIT, CORE_BIT, Z_BIT, Y_BIT = 16, 8, 2, 1


def as_rows(x):
    flat = x.reshape(-1)
    return jnp.pad(flat, (0, -flat.size % LANES)).reshape(-1, LANES)


def place():
    return lax.axis_index("dp") * NEAR["fsdp"] + lax.axis_index("fsdp")


def hop(x, mask):
    return lax.ppermute(x, AXES, [(i, i ^ mask) for i in range(32)])


def tie(first, second):
    return lax.optimization_barrier((first, second))


def fold_xy_kernel(me_ref, mine_ref, other_ref, *outs):
    x, y = me_ref[0] // X_BIT, me_ref[0] % 2
    for k, out in enumerate(outs):
        at = (x ^ (k // 2), 0, y ^ (k % 2))
        out[0] = (mine_ref[at].astype(F32) + other_ref[at].astype(F32)).astype(BF)


def fold_xy(me, mine, other):
    rows = mine.shape[-2]
    views = [a.reshape(2, 4, 2, rows, LANES) for a in (mine, other)]
    return pl.pallas_call(
        fold_xy_kernel,
        grid=(4,),
        in_specs=[pl.BlockSpec(memory_space=pltpu.SMEM)]
        + [pl.BlockSpec((2, 1, 2, rows, LANES), lambda z: (0, z, 0, 0, 0))] * 2,
        out_specs=[pl.BlockSpec((1, rows, LANES), lambda z: (z, 0, 0))] * 4,
        out_shape=[jax.ShapeDtypeStruct((4, rows, LANES), BF)] * 4,
        compiler_params=params(1),
        cost_estimate=cost(0, 6 * mine.size),
        name="fold_xy",
    )(me, *views)


def fold_z_kernel(me_ref, *refs):
    z = (me_ref[0] // Z_BIT) % 4
    for k, out in enumerate(refs[4:]):
        total = refs[0][z ^ k].astype(F32)
        for ref in refs[1:4]:
            total = total + ref[z ^ k].astype(F32)
        out[...] = total.astype(BF)


def fold_z(me, arrays):
    rows = arrays[0].shape[-2]
    return pl.pallas_call(
        fold_z_kernel,
        in_specs=[pl.BlockSpec(memory_space=pltpu.SMEM)] + [pl.BlockSpec(memory_space=pltpu.VMEM)] * 4,
        out_specs=[pl.BlockSpec(memory_space=pltpu.VMEM)] * 4,
        out_shape=[jax.ShapeDtypeStruct((rows, LANES), BF)] * 4,
        compiler_params=pltpu.CompilerParams(vmem_limit_bytes=16 * 1024 * 1024),
        cost_estimate=cost(0, 10 * arrays[0].size),
        name="fold_z",
    )(me, *arrays)


def finish_kernel(scale, a_ref, b_ref, c_ref, d_ref, in_ref, point_ref, small_ref):
    total = sum(ref[...].astype(F32) for ref in (a_ref, b_ref, c_ref, d_ref)) * scale
    for n in range(4):
        in_ref[:, n * ATT : (n + 1) * ATT] = total[24 * n : 24 * n + 24]
    point_ref[...] = total[96:120]
    small_ref[...] = total[120:128]


def finish(scale, arrays):
    vmem = pl.BlockSpec(memory_space=pltpu.VMEM)
    return pl.pallas_call(
        partial(finish_kernel, scale),
        in_specs=[vmem] * 4,
        out_specs=[vmem] * 3,
        out_shape=[
            jax.ShapeDtypeStruct((24, 4 * ATT), F32),
            jax.ShapeDtypeStruct((24, ATT), F32),
            jax.ShapeDtypeStruct((8, LANES), F32),
        ],
        name="finish",
    )(*arrays)


def finish_mid_kernel(scale, sum_ref, out_ref, up_ref, down_ref):
    total = sum_ref[...].astype(F32) * scale
    out_ref[:, :ATT] = total[:24]
    out_ref[:, ATT:] = total[24:48]
    for g in (0, 1):
        up_ref[g] = total[48 + 48 * g : 96 + 48 * g].T
        down_ref[g] = total[144 + 48 * g : 192 + 48 * g]


def finish_mid(scale, packed):
    vmem = pl.BlockSpec(memory_space=pltpu.VMEM)
    return pl.pallas_call(
        partial(finish_mid_kernel, scale),
        in_specs=[vmem],
        out_specs=[vmem] * 3,
        out_shape=[
            jax.ShapeDtypeStruct((24, WIDTH), F32),
            jax.ShapeDtypeStruct((2, ATT, 48), F32),
            jax.ShapeDtypeStruct((2, 48, ATT), F32),
        ],
        name="finish_mid",
    )(packed)


SLAB_BITS = [((s // 4) % 2 * X_BIT + (s // 8) * CORE_BIT + s % 4 * Z_BIT) // 2 for s in range(16)]


def pair_slab(own, small):
    packed = jnp.concatenate([own.reshape(-1, LANES), small])
    other = hop(packed, Y_BIT)
    even = place() % 2 == 0
    first, second = jnp.where(even, packed, other), jnp.where(even, other, packed)
    both = [x[:120].reshape(5, 24, LANES) for x in (first, second)]
    return jnp.concatenate([jnp.concatenate(both, 1).reshape(-1, LANES), first[120:], second[120:]])


def small_rows(slabs, pair):
    spot = jnp.array([SLAB_BITS.index(b) for b in range(16)], jnp.int32)
    order = jnp.take(spot, jnp.arange(16, dtype=jnp.int32) ^ pair)
    return jnp.take(jnp.stack([slab[240:] for slab in slabs]), order, axis=0).reshape(32, -1)


def lane_groups(x, combine):
    for step in (64, 32, 16, 8):
        x = combine(x, pltpu.roll(x, step, 1))
    return x


def tap_spread(block):
    rows = lax.broadcasted_iota(jnp.int32, (128, KER * 128), 0)
    cols = lax.broadcasted_iota(jnp.int32, (128, KER * 128), 1)
    want = (cols // 128) * 8 + block * 2 + (cols % 128) // HEAD
    return (rows == want).astype(F32).astype(BF)


EC = 1024
FB = 512
BB = 1024
DB = 512


def pick_kernel(pick_ref, tok_ref, inp_ref):
    cols = lax.broadcasted_iota(jnp.int32, (SEQ, SEQ), 1)
    hot = (cols == pick_ref[...]).astype(F32).astype(BF)
    inp_ref[...] = mm(hot, tok_ref[...]).astype(BF)


def pick_rows(pick, tokens):
    block = lambda n: pl.BlockSpec((SEQ, n), lambda s: (s, 0))
    return pl.pallas_call(
        pick_kernel,
        grid=(tokens.shape[0] // SEQ,),
        in_specs=[block(1), block(WIDTH)],
        out_specs=block(WIDTH),
        out_shape=jax.ShapeDtypeStruct(tokens.shape, BF),
        compiler_params=params(1),
        cost_estimate=cost(6e9, 6e6),
        name="pick",
    )(pick, tokens)


def enter_kernel(
    inp_ref, w_in_ref, w_depth_ref, w_point_ref, w_kern_ref,
    proj_ref, spread_ref, ck_ref, kern_ref, conv_ref,
    x_pad, cv_pad,
):
    x_pad[0:8, :] = jnp.zeros((8, WIDTH), F32)
    x_pad[SEQ + 8 : SEQ + 16, :] = jnp.zeros((8, WIDTH), F32)
    cv_pad[0:8, :] = jnp.zeros((8, ATT), F32)
    cv_pad[SEQ + 8 : SEQ + 16, :] = jnp.zeros((8, ATT), F32)

    def load(i, carry):
        r = pl.multiple_of(i * EC, EC)
        low = inp_ref[pl.ds(r, EC), :]
        x_pad[pl.ds(r + 8, EC), :] = low.astype(F32)
        proj = mm(low, w_in_ref[...])
        proj_low = proj.astype(BF)
        proj_ref[pl.ds(r, EC), :] = proj_low
        cv_pad[pl.ds(r + 8, EC), :] = proj_low[:, 3 * ATT :].astype(F32)
        return carry

    lax.fori_loop(0, SEQ // EC, load, 0)

    def conv(i, carry):
        r = pl.multiple_of(i * EC, EC)
        for b in range(WIDTH // 128):
            lanes = slice(b * 128, (b + 1) * 128)
            xs = x_pad[pl.ds(r, (EC + 16)), lanes]
            shifted = [xs] + [pltpu.roll(xs, (EC + 16) - s, 0) for s in (1, 2, 3)]
            tap = lambda j: w_depth_ref[j : j + 1, lanes]
            low_part = sum(tap(s) * shifted[s] for s in range(4))
            mid_part = sum(tap(4 + s) * shifted[s] for s in range(4))
            high_part = tap(8) * xs
            low_part = pltpu.roll(low_part, (EC + 16) - 4, 0)
            high_part = pltpu.roll(high_part, (EC + 16) - 4, 0)
            total = low_part[0:EC] + mid_part[8 : 8 + EC] + high_part[8 : 8 + EC]
            spread_ref[pl.ds(r, EC), lanes] = total.astype(BF)
        ck = mm(spread_ref[pl.ds(r, EC), :], w_point_ref[...]).astype(BF)
        ck_ref[pl.ds(r, EC), :] = ck
        q = proj_ref[pl.ds(r, EC), 0:ATT].astype(F32)
        mixed = (ck.astype(F32) * q).astype(BF)
        logits = mm(mixed, w_kern_ref[...])
        lane = lax.broadcasted_iota(jnp.int32, (EC, 128), 1)
        logits = jnp.where(lane < KER * 8, logits, -1e30)
        top = lane_groups(logits, jnp.maximum)
        e = jnp.exp(logits - top)
        kern = e / lane_groups(e, jnp.add)
        kern_ref[pl.ds(r, EC), :] = kern
        kern_low = kern.astype(BF)
        for b in range(ATT // 128):
            lanes = slice(b * 128, (b + 1) * 128)
            wide = mm(kern_low, tap_spread(b))
            cs = cv_pad[pl.ds(r, (EC + 16)), lanes]
            total = jnp.zeros((EC, 128), F32)
            for j in range(KER):
                moved = cs if j == 4 else pltpu.roll(cs, ((EC + 16) - (j - 4)) % (EC + 16), 0)
                total = total + wide[:, j * 128 : (j + 1) * 128] * moved[8 : 8 + EC]
            conv_ref[pl.ds(r, EC), lanes] = total.astype(BF)
        return carry

    lax.fori_loop(0, SEQ // EC, conv, 0)


def enter_slabs_kernel(pair_ref, inp_ref, w_depth_ref, w_kern_ref, *refs):
    slabs, outs = refs[:16], refs[16:]
    results, w_in_ref, w_point_ref, scratch, sems = outs[:5], outs[5], outs[6], outs[7:9], outs[9]

    @pl.when(pl.program_id(0) == 0)
    def _():
        copies = []
        for s, slab in enumerate(slabs):
            spot = pl.ds(pl.multiple_of((pair_ref[0] ^ SLAB_BITS[s]) * 48, 16), 48)
            for b in range(5):
                to = w_in_ref.at[spot, b * ATT : (b + 1) * ATT] if b < 4 else w_point_ref.at[spot, :]
                copies.append(pltpu.make_async_copy(slab.at[b * 48 : (b + 1) * 48, :], to, sems.at[s, b]))
        for copy in copies:
            copy.start()
        for copy in copies:
            copy.wait()

    enter_kernel(inp_ref, w_in_ref, w_depth_ref, w_point_ref, w_kern_ref, *results, *scratch)


def enter(inputs, pair, w_depth, w_kern, slabs):
    rows = inputs.shape[0]
    block = lambda n: pl.BlockSpec((SEQ, n), lambda s: (s, 0))
    widths = ((4 * ATT, BF), (WIDTH, BF), (ATT, BF), (128, F32), (ATT, BF))
    return pl.pallas_call(
        enter_slabs_kernel,
        grid=(rows // SEQ,),
        in_specs=[
            pl.BlockSpec(memory_space=pltpu.SMEM), block(WIDTH), whole((KER, WIDTH)), whole((ATT, 128)),
        ]
        + [pl.BlockSpec(memory_space=pl.ANY)] * 16,
        out_specs=[block(n) for n, _ in widths] + [whole_out((WIDTH, 4 * ATT)), whole_out((WIDTH, ATT))],
        out_shape=[jax.ShapeDtypeStruct((rows, n), t) for n, t in widths]
        + [jax.ShapeDtypeStruct((WIDTH, 4 * ATT), BF), jax.ShapeDtypeStruct((WIDTH, ATT), BF)],
        scratch_shapes=[
            pltpu.VMEM((SEQ + 16, WIDTH), F32),
            pltpu.VMEM((SEQ + 16, ATT), F32),
            pltpu.SemaphoreType.DMA((16, 5)),
        ],
        compiler_params=params(1),
        cost_estimate=cost(20e9, 20e6),
        name="enter",
    )(pair, inputs, w_depth, w_kern, *slabs)


def own_lanes(rows, head):
    lane = lax.broadcasted_iota(jnp.int32, (rows, 128), 1)
    return (lane // HEAD) == head


AC = 512


def attend_kernel(q_ref, k_ref, v_ref, p_ref, o_ref, inv_ref):
    k = k_ref[...]
    v_all = v_ref[...].astype(F32)
    vs = [jnp.where(own_lanes(SEQ, head), v_all, 1.0).astype(BF) for head in (0, 1)]
    first = own_lanes(AC, 0)

    def part(i, carry):
        rows = pl.ds(pl.multiple_of(i * AC, AC), AC)
        q_all = q_ref[rows, :].astype(F32) * (HEAD**-0.5)
        outs = []
        for head in (0, 1):
            q = jnp.where(first if head == 0 else ~first, q_all, 0.0).astype(BF)
            s = mm_nt(q, k)
            p = jnp.exp(s - jnp.max(s, -1, keepdims=True)).astype(BF)
            p_ref[0, head, rows, :] = p
            outs.append(mm(p, vs[head]))
        inv = 1.0 / pltpu.roll(jnp.where(first, outs[1], outs[0]), HEAD, 1)
        o_ref[rows, :] = (jnp.where(first, outs[0], outs[1]) * inv).astype(BF)
        inv_ref[rows, :] = inv
        return carry

    lax.fori_loop(0, SEQ // AC, part, 0, unroll=2)


def attend(proj):
    rows = proj.shape[0]
    pairs = HEADS // 2
    col = lambda base: pl.BlockSpec((SEQ, 128), lambda s, p: (s, base + p))
    return pl.pallas_call(
        attend_kernel,
        grid=(rows // SEQ, pairs),
        in_specs=[col(0), col(pairs), col(2 * pairs)],
        out_specs=[pl.BlockSpec((1, 2, SEQ, SEQ), lambda s, p: (s, p, 0, 0)), col(0), col(0)],
        out_shape=[
            jax.ShapeDtypeStruct((rows // SEQ, HEADS, SEQ, SEQ), BF),
            jax.ShapeDtypeStruct((rows, ATT), BF),
            jax.ShapeDtypeStruct((rows, ATT), F32),
        ],
        compiler_params=params(2),
        cost_estimate=cost(25e9, 35e6),
        name="attend",
    )(proj, proj, proj)


ERF_P = 0.3275911 / math.sqrt(2.0)
ERF_A = (0.254829592, -0.284496736, 1.421413741, -1.453152027, 1.061405429)
PHI = 1.0 / math.sqrt(2.0 * math.pi)


def gelu_both(u):
    mag = jnp.abs(u)
    t = 1.0 / (1.0 + ERF_P * mag)
    poly = ERF_A[4]
    for a in ERF_A[3::-1]:
        poly = poly * t + a
    e = jnp.exp(-0.5 * (u * u))
    tail = (0.5 * t) * poly * e
    cdf = jnp.where(u > 0, 1.0 - tail, tail)
    return u * cdf, cdf + (PHI * u) * e


def norm_parts(z):
    mean = jnp.mean(z, -1, keepdims=True)
    centred = z - mean
    var = jnp.mean(centred * centred, -1, keepdims=True)
    r = lax.rsqrt(var + 1e-12)
    return centred * r, r


def norm_back(c, xh, r, gain):
    gc = c * gain
    return r * (gc - jnp.mean(gc, -1, keepdims=True) - xh * jnp.mean(gc * xh, -1, keepdims=True))


def fold_rows(x):
    return jnp.sum(x.reshape(-1, 8, x.shape[-1]), 0)


MID = 256
FF = 1536
FC = 768
GROUP = 48
BLOCKS = FF // GROUP


def middle_kernel(
    att_ref, conv_ref, inp_ref, cot_ref, mid_ref, vec_ref,
    out_ref, dctx_ref, dfirst_ref, dvec_ref, packed_ref,
    acc_out, acc_up, acc_down, acc_vec, act_ref, slope_ref, flip_ref,
    w_out_ref, w_rows, w_up_blocks, w_down_blocks, sems,
):
    step = pl.program_id(0)
    last = pl.num_programs(0) - 1

    @pl.when(step == 0)
    def _():
        targets = [w_rows] + [w.at[g] for w in (w_up_blocks, w_down_blocks) for g in (0, 1)]
        copies = [
            pltpu.make_async_copy(mid_ref.at[:, n * GROUP : (n + 1) * GROUP, :], to, sems.at[n])
            for n, to in enumerate(targets)
        ]
        for copy in copies:
            copy.start()
        acc_up[...] = jnp.zeros_like(acc_up)
        acc_down[...] = jnp.zeros_like(acc_down)
        acc_vec[...] = jnp.zeros_like(acc_vec)
        copies[0].wait()
        half = GROUP // 2

        def unfold(i, carry):
            both = w_rows[i].astype(F32)
            rows = pl.ds(pl.multiple_of(i * half, 8), half)
            acc_out[rows, :] = jnp.concatenate([both[:half], both[half:]], 1)
            return carry

        lax.fori_loop(0, BLOCKS, unfold, 0)
        w_out_ref[...] = acc_out[...].astype(BF)
        acc_out[...] = jnp.zeros_like(acc_out)
        for copy in copies[1:]:
            copy.wait()

    def w_up(g, f):
        return w_up_blocks[g, f * FC // GROUP : (f + 1) * FC // GROUP].reshape(FC, ATT)

    def w_down(g, f):
        return w_down_blocks[g, f * FC // GROUP : (f + 1) * FC // GROUP].reshape(FC, ATT)

    ctx = jnp.concatenate([att_ref[...], conv_ref[...]], -1)
    g_one, s_one = vec_ref[0:1, :], vec_ref[1:2, :]
    g_two, s_two = vec_ref[2:3, :], vec_ref[3:4, :]
    first_in = mm(ctx, w_out_ref[...]) + inp_ref[...].astype(F32)
    xh_one, r_one = norm_parts(first_in)
    first = xh_one * g_one + s_one
    first_low = first.astype(BF)
    outs = []
    for g in (0, 1):
        cols = slice(g * ATT, (g + 1) * ATT)
        total = None
        for f in range(FF // FC):
            hid = slice(f * FC, (f + 1) * FC)
            inner = mm_nt(first_low[:, cols], w_up(g, f))
            act, slope = gelu_both(inner)
            act = act.astype(BF)
            act_ref[g, :, hid] = act
            slope_ref[g, :, hid] = slope.astype(slope_ref.dtype)
            part = mm(act, w_down(g, f))
            total = part if total is None else total + part
        outs.append(total)
    xh_two, r_two = norm_parts(jnp.concatenate(outs, -1) + first)
    out_ref[...] = (xh_two * g_two + s_two).astype(BF)
    c = cot_ref[...].astype(F32)
    acc_vec[2] += fold_rows(c * xh_two)
    acc_vec[3] += fold_rows(c)
    d_second = norm_back(c, xh_two, r_two, g_two)
    d_outer = d_second.astype(BF)
    d_outer_t = d_second.T.astype(BF)
    first_t = first.T.astype(BF)
    backs = []
    for g in (0, 1):
        cols = slice(g * ATT, (g + 1) * ATT)
        total = None
        for f in range(FF // FC):
            hid = slice(f * FC, (f + 1) * FC)
            d_act = mm_nt(d_outer[:, cols], w_down(g, f))
            d_inner = (d_act * slope_ref[g, :, hid].astype(F32)).astype(BF)
            acc_down[g, :, hid] += mm(d_outer_t[cols, :], act_ref[g, :, hid])
            acc_up[g, :, hid] += mm(first_t[cols, :], d_inner)
            part = mm(d_inner, w_up(g, f))
            total = part if total is None else total + part
        backs.append(total)
    d_first = jnp.concatenate(backs, -1) + d_second
    acc_vec[0] += fold_rows(d_first * xh_one)
    acc_vec[1] += fold_rows(d_first)
    d_first_in = norm_back(d_first, xh_one, r_one, g_one)
    dfirst_ref[...] = d_first_in
    d_dense = d_first_in.astype(BF)
    acc_out[...] += mm_tn(ctx, d_dense)
    dctx_ref[...] = mm_nt(d_dense, w_out_ref[...]).astype(BF)

    @pl.when(step == last)
    def _():
        dvec_ref[...] = jnp.sum(acc_vec[...], 1)
        for g in (0, 1):
            flip_ref[0, g] = acc_up[g].T.astype(BF)
            flip_ref[1, g] = acc_down[g].T.astype(BF)

        def emit(i, carry):
            o = acc_out[pl.ds(pl.multiple_of(i * 24, 8), 24), :]
            packed_ref[i, 0:48, :] = jnp.concatenate([o[:, :ATT], o[:, ATT:]], 0).astype(BF)
            hidden = pl.ds(pl.multiple_of(i * 48, 16), 48)
            for n in range(4):
                packed_ref[i, 48 * n + 48 : 48 * n + 96, :] = flip_ref[n // 2, n % 2, hidden, :]
            return carry

        lax.fori_loop(0, BLOCKS, emit, 0)


def middle(att, conv, inputs, cot, mid, vecs):
    rows = att.shape[0]
    block = lambda n: pl.BlockSpec((MID, n), lambda s: (s, 0))
    packed = (BLOCKS, 5 * GROUP, LANES)
    return pl.pallas_call(
        middle_kernel,
        grid=(rows // MID,),
        in_specs=[
            block(ATT), block(ATT), block(WIDTH), block(WIDTH),
            pl.BlockSpec(memory_space=pl.ANY), whole((4, WIDTH)),
        ],
        out_specs=[block(WIDTH), block(WIDTH), block(WIDTH), whole_out((4, WIDTH)), whole_out(packed)],
        out_shape=[
            jax.ShapeDtypeStruct((rows, WIDTH), BF),
            jax.ShapeDtypeStruct((rows, WIDTH), BF),
            jax.ShapeDtypeStruct((rows, WIDTH), F32),
            jax.ShapeDtypeStruct((4, WIDTH), F32),
            jax.ShapeDtypeStruct(packed, BF),
        ],
        scratch_shapes=[
            pltpu.VMEM((WIDTH, WIDTH), F32),
            pltpu.VMEM((2, ATT, FF), F32),
            pltpu.VMEM((2, ATT, FF), F32),
            pltpu.VMEM((4, 8, WIDTH), F32),
            pltpu.VMEM((2, MID, FF), BF),
            pltpu.VMEM((2, MID, FF), F32),
            pltpu.VMEM((2, 2, FF, ATT), BF),
            pltpu.VMEM((WIDTH, WIDTH), BF),
            pltpu.VMEM((BLOCKS, GROUP, LANES), BF),
            pltpu.VMEM((2, BLOCKS, GROUP, ATT), BF),
            pltpu.VMEM((2, BLOCKS, GROUP, ATT), BF),
            pltpu.SemaphoreType.DMA((5,)),
        ],
        compiler_params=params(1),
        cost_estimate=cost(60e9, 40e6),
        name="middle",
    )(att, conv, inputs, cot, mid, vecs)


def conv_back_kernel(
    dconv_ref, kern_ref, q_ref, cv_ref, ck_ref, spread_ref, inp_ref, first_ref, w_depth_ref, w_point_ref, w_kern_ref,
    dq_ref, dcv_ref, din_ref, dpoint_ref, dkern_ref, ddepth_ref,
    x_pad, cv_pad, dc_pad, kl_pad, ds_pad, acc_point, acc_kern, acc_depth,
):
    step = pl.program_id(0)
    last = pl.num_programs(0) - 1
    zero = lambda n: jnp.zeros((8, n), F32)
    for ref, n in ((x_pad, WIDTH), (cv_pad, ATT), (dc_pad, ATT), (kl_pad, 128), (ds_pad, WIDTH)):
        ref[0:8, :] = zero(n)
        ref[SEQ + 8 : SEQ + 16, :] = zero(n)

    @pl.when(step == 0)
    def _():
        acc_point[...] = jnp.zeros_like(acc_point)
        acc_kern[...] = jnp.zeros_like(acc_kern)
        acc_depth[...] = jnp.zeros_like(acc_depth)

    def fill(i, carry):
        r = pl.multiple_of(i * FB, FB)
        rows = pl.ds(r, FB)
        there = pl.ds(r + 8, FB)
        x_pad[there, :] = inp_ref[rows, :].astype(F32)
        cv_pad[there, :] = cv_ref[rows, :].astype(F32)
        dc_pad[there, :] = dconv_ref[rows, :].astype(F32)
        kl_pad[there, :] = kern_ref[rows, :]
        return carry

    lax.fori_loop(0, SEQ // FB, fill, 0)

    def back(i, carry):
        r = pl.multiple_of(i * BB, BB)
        rows = pl.ds(r, BB)
        d_kern = jnp.zeros((BB, 128), F32)
        kl = kl_pad[pl.ds(r, (BB + 16)), :].astype(BF)
        for b in range(ATT // 128):
            lanes = slice(b * 128, (b + 1) * 128)
            spreader = tap_spread(b)
            cs = cv_pad[pl.ds(r, (BB + 16)), lanes]
            dc = dc_pad[pl.ds(r + 8, BB), lanes]
            prods = []
            for j in range(KER):
                moved = cs if j == 4 else pltpu.roll(cs, ((BB + 16) - (j - 4)) % (BB + 16), 0)
                prods.append((dc * moved[8 : 8 + BB]).astype(BF))
            d_kern = d_kern + mm_nt(jnp.concatenate(prods, -1), spreader)
            wide = mm(kl, spreader)
            dch = dc_pad[pl.ds(r, (BB + 16)), lanes]
            total = jnp.zeros((BB, 128), F32)
            for j in range(KER):
                term = wide[:, j * 128 : (j + 1) * 128] * dch
                moved = term if j == 4 else pltpu.roll(term, ((BB + 16) + (j - 4)) % (BB + 16), 0)
                total = total + moved[8 : 8 + BB]
            dcv_ref[rows, lanes] = total.astype(BF)
        kern = kern_ref[rows, :]
        dot_rows = lane_groups(kern * d_kern, jnp.add)
        d_logits = (kern * (d_kern - dot_rows)).astype(BF)
        q = q_ref[rows, :].astype(F32)
        ck = ck_ref[rows, :].astype(F32)
        mixed = (ck * q).astype(BF)
        acc_kern[...] += mm_tn(mixed, d_logits)
        d_mixed = mm_nt(d_logits, w_kern_ref[...])
        dq_ref[rows, :] = d_mixed * ck
        d_ck = (d_mixed * q).astype(BF)
        acc_point[...] += mm_tn(spread_ref[rows, :], d_ck)
        ds_pad[pl.ds(r + 8, BB), :] = mm_nt(d_ck, w_point_ref[...])
        return carry

    lax.fori_loop(0, SEQ // BB, back, 0)

    def depth(i, carry):
        r = pl.multiple_of(i * DB, DB)
        rows = pl.ds(r, DB)
        for b in range(WIDTH // 128):
            lanes = slice(b * 128, (b + 1) * 128)
            dsh = ds_pad[pl.ds(r, (DB + 16)), lanes]
            tap = lambda j: w_depth_ref[j : j + 1, lanes]
            shifted = [dsh] + [pltpu.roll(dsh, s, 0) for s in (1, 2, 3)]
            low_part = sum(tap(s) * shifted[s] for s in range(4))
            mid_part = sum(tap(4 + s) * shifted[s] for s in range(4))
            high_part = tap(8) * dsh
            low_part = pltpu.roll(low_part, (DB + 16) - 4, 0)
            high_part = pltpu.roll(high_part, 4, 0)
            taps = (low_part + mid_part + high_part)[8 : 8 + DB]
            din_ref[rows, lanes] = taps + first_ref[rows, lanes]
            xs = x_pad[pl.ds(r + 8, DB), lanes]
            far_low = [pltpu.roll(shifted[s], (DB + 16) - 4, 0) for s in range(4)]
            far_high = pltpu.roll(dsh, 4, 0)
            for j in range(KER):
                src = far_low[j] if j < 4 else (shifted[j - 4] if j < 8 else far_high)
                acc_depth[j, :, lanes] += fold_rows(src[8 : 8 + DB] * xs)
        return carry

    lax.fori_loop(0, SEQ // DB, depth, 0)

    @pl.when(step == last)
    def _():
        dpoint_ref[...] = acc_point[...]
        dkern_ref[...] = acc_kern[...]
        ddepth_ref[...] = jnp.sum(acc_depth[...], 1)


def conv_back(dctx, kern, proj, ck, spread, inputs, d_first_in, w_depth, w_point, w_kern):
    rows = inputs.shape[0]
    block = lambda n: pl.BlockSpec((SEQ, n), lambda s: (s, 0))
    at = lambda c: pl.BlockSpec((SEQ, ATT), lambda s: (s, c))
    return pl.pallas_call(
        conv_back_kernel,
        grid=(rows // SEQ,),
        in_specs=[
            at(1), block(128), at(0), at(3), block(ATT), block(WIDTH), block(WIDTH), block(WIDTH),
            whole((KER, WIDTH)), whole((WIDTH, ATT)), whole((ATT, 128)),
        ],
        out_specs=[
            block(ATT), block(ATT), block(WIDTH), whole_out((WIDTH, ATT)), whole_out((ATT, 128)),
            whole_out((KER, WIDTH)),
        ],
        out_shape=[
            jax.ShapeDtypeStruct((rows, ATT), F32),
            jax.ShapeDtypeStruct((rows, ATT), BF),
            jax.ShapeDtypeStruct((rows, WIDTH), F32),
            jax.ShapeDtypeStruct((WIDTH, ATT), F32),
            jax.ShapeDtypeStruct((ATT, 128), F32),
            jax.ShapeDtypeStruct((KER, WIDTH), F32),
        ],
        scratch_shapes=[
            pltpu.VMEM((SEQ + 16, WIDTH), F32),
            pltpu.VMEM((SEQ + 16, ATT), F32),
            pltpu.VMEM((SEQ + 16, ATT), F32),
            pltpu.VMEM((SEQ + 16, 128), F32),
            pltpu.VMEM((SEQ + 16, WIDTH), F32),
            pltpu.VMEM((WIDTH, ATT), F32),
            pltpu.VMEM((ATT, 128), F32),
            pltpu.VMEM((KER, 8, WIDTH), F32),
        ],
        compiler_params=params(1),
        cost_estimate=cost(25e9, 30e6),
        name="conv_back",
    )(dctx, kern, proj, proj, ck, spread, inputs, d_first_in, w_depth, w_point, w_kern)


def attend_back_kernel(
    q_ref, k_ref, v_ref, p_ref, o_ref, inv_ref, datt_ref, dqc_ref, dq_ref, dk_ref, dv_ref
):
    scale = HEAD**-0.5
    v = v_ref[...]
    d_att = datt_ref[...].astype(F32) * inv_ref[...]
    o = o_ref[...].astype(F32)
    q_all = q_ref[...].astype(F32) * scale
    k_all = k_ref[...].astype(F32) * scale
    dq, dk_t, dv_t = dqc_ref[...], 0.0, 0.0
    for head in (0, 1):
        mine = own_lanes(SEQ, head)
        da = jnp.where(mine, d_att, 0.0)
        dot_rows = jnp.sum(da * o, -1, keepdims=True)
        p = p_ref[0, head]
        ds = mm_nt(da.astype(BF), v)
        ds = (p.astype(F32) * (ds - dot_rows)).astype(BF)
        dq = dq + mm(ds, jnp.where(mine, k_all, 0.0).astype(BF))
        dk_t = dk_t + mm(jnp.where(mine, q_all, 0.0).T.astype(BF), ds)
        dv_t = dv_t + mm(da.T.astype(BF), p)
    dq_ref[...] = dq.astype(BF)
    dk_ref[...] = dk_t.T.astype(BF)
    dv_ref[...] = dv_t.T.astype(BF)


def attend_back(proj, probs, att, inv, dctx, dq_conv):
    rows = proj.shape[0]
    pairs = HEADS // 2
    col = lambda base: pl.BlockSpec((SEQ, 128), lambda s, p: (s, base + p))
    return pl.pallas_call(
        attend_back_kernel,
        grid=(rows // SEQ, pairs),
        in_specs=[
            col(0), col(pairs), col(2 * pairs),
            pl.BlockSpec((1, 2, SEQ, SEQ), lambda s, p: (s, p, 0, 0)),
            col(0), col(0), col(0), col(0),
        ],
        out_specs=[col(0)] * 3,
        out_shape=[jax.ShapeDtypeStruct((rows, ATT), BF)] * 3,
        compiler_params=params(2),
        cost_estimate=cost(30e9, 40e6),
        name="attend_back",
    )(proj, proj, proj, probs, att, inv, dctx, dq_conv)


WB = 512


def weight_kernel(core_ref, inp_ref, dq_ref, dk_ref, dv_ref, dcv_ref, point_ref, extra_ref, *refs):
    grad_refs, acc = refs[:-1], refs[-1]
    step = pl.program_id(0)
    last = pl.num_programs(0) - 1
    inp = inp_ref[...]

    @pl.when(step == 0)
    def _():
        acc[...] = jnp.zeros_like(acc)

    for n, ref in enumerate((dq_ref, dk_ref, dv_ref, dcv_ref)):
        acc[:, n * ATT : (n + 1) * ATT] += mm_tn(inp, ref[...])

    @pl.when(step == last)
    def _():
        for c, grad in enumerate(grad_refs):

            def emit(i, carry):
                owner = i
                if len(grad_refs) == 2:
                    owner = (i // 8) * 16 + (core_ref[0] ^ c) * 8 + i % 8
                rows = pl.ds(pl.multiple_of(owner * 24, 8), 24)
                o = acc[rows, :]
                cols = [o[:, n * ATT : (n + 1) * ATT] for n in range(4)]
                grad[i] = jnp.concatenate(cols + [point_ref[rows, :], extra_ref[owner]], 0).astype(BF)
                return carry

            lax.fori_loop(0, grad.shape[0], emit, 0)


def weight_grad(inputs, dq, dk, dv, dcv, d_point, extra, core=None):
    rows = inputs.shape[0]
    block = lambda n: pl.BlockSpec((WB, n), lambda s: (s, 0))
    shapes = [(32, 128, LANES)] if core is None else [(16, 128, LANES)] * 2
    core = jnp.zeros((1,), jnp.int32) if core is None else core
    return pl.pallas_call(
        weight_kernel,
        grid=(rows // WB,),
        in_specs=[pl.BlockSpec(memory_space=pltpu.SMEM), block(WIDTH)]
        + [block(ATT)] * 4
        + [whole(d_point.shape), whole(extra.shape)],
        out_specs=[whole_out(s) for s in shapes],
        out_shape=[jax.ShapeDtypeStruct(s, BF) for s in shapes],
        scratch_shapes=[pltpu.VMEM((WIDTH, 4 * ATT), F32)],
        compiler_params=params(1),
        cost_estimate=cost(12e9, 12e6),
        name="weight_grad",
    )(core, inputs, dq, dk, dv, dcv, d_point, extra)


LC = 512
STEPS = SEQ // LC


def leave_kernel(
    dq_ref, dk_ref, dv_ref, dcv_ref, rest_ref, mask_ref, to_ref, w_in_ref, out_ref, moved, kept
):
    step = pl.program_id(1)
    rows = pl.ds(pl.multiple_of((step % STEPS) * LC, LC), LC)

    @pl.when(step < STEPS)
    def _():
        d_proj = jnp.concatenate([dq_ref[...], dk_ref[...], dv_ref[...], dcv_ref[...]], 1)
        total = mm_nt(d_proj, w_in_ref[...]) + rest_ref[...]
        moved[rows, :] = total.astype(BF)
        kept[rows, :] = jnp.where(mask_ref[...] == 1, 0.0, total)

    @pl.when(step >= STEPS)
    def _():
        target = lax.broadcasted_iota(jnp.int32, (LC, SEQ), 0) + (step - STEPS) * LC
        hot = (target == to_ref[0]).astype(F32).astype(BF)
        out_ref[...] = kept[rows, :] + mm(hot, moved[...])


def leave(dq, dk, dv, dcv, d_rest, mask_col, to_row, w_in):
    rows = dq.shape[0]
    block = lambda n: pl.BlockSpec((LC, n), lambda s, i: (s * STEPS + jnp.minimum(i, STEPS - 1), 0))
    return pl.pallas_call(
        leave_kernel,
        grid=(rows // SEQ, 2 * STEPS),
        in_specs=[block(ATT)] * 4
        + [block(WIDTH), block(1), pl.BlockSpec((1, 1, SEQ), lambda s, i: (s, 0, 0)), whole((WIDTH, 4 * ATT))],
        out_specs=pl.BlockSpec((LC, WIDTH), lambda s, i: (s * STEPS + jnp.maximum(i - STEPS, 0), 0)),
        out_shape=jax.ShapeDtypeStruct((rows, WIDTH), F32),
        scratch_shapes=[pltpu.VMEM((SEQ, WIDTH), BF), pltpu.VMEM((SEQ, WIDTH), F32)],
        compiler_params=params(2),
        cost_estimate=cost(15e9, 30e6),
        name="leave",
    )(dq, dk, dv, dcv, d_rest, mask_col, to_row, w_in)


def pack_taps(kernel_full):
    by_tap = kernel_full.reshape(ATT, HEADS, KER).transpose(0, 2, 1)
    return jnp.pad(by_tap, ((0, 0), (0, 16 - KER), (0, 8 - HEADS))).reshape(ATT, 128)


def unpack_taps(packed):
    return packed.reshape(ATT, 16, 8)[:, :KER, :HEADS].transpose(0, 2, 1).reshape(ATT, HEADS * KER)


def per_device(
    tokens,
    masked,
    replace_ids,
    in_weight,
    depth_weight,
    point_weight,
    kernel_weight,
    out_weight,
    gain_one,
    shift_one,
    ffn_in,
    feedforward_output,
    gain_two,
    shift_two,
    cotangent,
):
    rows = tokens.shape[0]
    seqs = rows // SEQ
    dp, fsdp = lax.axis_size("dp"), lax.axis_size("fsdp")
    devices = dp * fsdp
    near = dp == NEAR["dp"] and fsdp == NEAR["fsdp"]
    own, hid = in_weight.shape[0], ffn_in.shape[2]
    n_depth, n_kern, n_vec = KER * own, kernel_weight.size, 4 * own
    hit = masked == 1
    here = jnp.arange(rows, dtype=jnp.int32) % SEQ
    pick = jnp.where(hit, replace_ids, here)[:, None]
    to_row = jnp.where(hit, replace_ids, -1).reshape(seqs, 1, SEQ)
    scale = 1.0 / math.sqrt(rows * devices)

    vec_own = jnp.stack([gain_one, shift_one, gain_two, shift_two])
    small_own = as_rows(
        jnp.concatenate([depth_weight.reshape(-1), kernel_weight.reshape(-1), vec_own.reshape(-1)])
    )
    head_own = jnp.concatenate([in_weight.reshape(own, 4, ATT).transpose(1, 0, 2), point_weight[None]])
    mid_own = jnp.concatenate(
        [
            out_weight.reshape(own, 2, ATT).transpose(1, 0, 2).reshape(-1, LANES),
            ffn_in.transpose(0, 2, 1).reshape(-1, LANES),
            feedforward_output.reshape(-1, LANES),
        ]
    )
    if near:
        me = place().astype(jnp.int32).reshape(1)
        pair, core = me // 2, me // CORE_BIT % 2
        slab, pick = tie(pair_slab(head_own, small_own), pick)
        slabs = [slab] + [hop(slab, k * Z_BIT) for k in (1, 2, 3)]
        inputs, slabs = tie(pick_rows(pick, tokens), slabs)
        slabs, mid_own = tie(slabs, mid_own)
        mid = lax.all_gather(mid_own, AXES, axis=0)
        slabs = slabs + [hop(slab, X_BIT) for slab in slabs]
        slabs = slabs + [hop(slab, CORE_BIT) for slab in slabs]
        small_all = small_rows(slabs, pair)
    else:
        small_all = lax.all_gather(small_own, AXES, axis=0).reshape(devices, -1)
        w_all = lax.all_gather(head_own, AXES, axis=1, tiled=True).reshape(5, 16, 48, LANES)
        slabs = [w_all[:, bits].reshape(-1, LANES) for bits in SLAB_BITS]
        mid = lax.all_gather(mid_own, AXES, axis=0)
        w_out = mid[:, : 2 * own].reshape(devices, 2, own, ATT).transpose(1, 0, 2, 3)
        w_out = w_out.reshape(2, BLOCKS, 24, ATT).transpose(1, 0, 2, 3).reshape(BLOCKS, 48, ATT)
        w_ffn = mid[:, 2 * own :].reshape(devices, 4, hid, ATT).transpose(1, 0, 2, 3)
        w_ffn = w_ffn.reshape(4, BLOCKS, 48, ATT).transpose(1, 0, 2, 3).reshape(BLOCKS, 192, ATT)
        mid = jnp.concatenate([w_out, w_ffn], 1)
        pair, core = jnp.zeros((1,), jnp.int32), None
        inputs = pick_rows(pick, tokens)
    w_depth = small_all[:, :n_depth].reshape(devices, KER, own).transpose(1, 0, 2).reshape(KER, WIDTH)
    w_depth = w_depth.astype(F32)
    w_kern = pack_taps(small_all[:fsdp, n_depth : n_depth + n_kern].reshape(ATT, HEADS * KER))
    vecs = small_all[:, n_depth + n_kern :][:, :n_vec].reshape(devices, 4, own)
    vecs = vecs.transpose(1, 0, 2).reshape(4, WIDTH).astype(F32)

    proj, spread, ck, kern, conv, w_in, w_point = enter(inputs, pair, w_depth, w_kern, slabs)
    probs, att, inv = attend(proj)
    out, dctx, d_first_in, d_vecs, mid_grad = middle(att, conv, inputs, cotangent, mid, vecs)
    if near:
        mid_sum = lax.psum_scatter(mid_grad, AXES, scatter_dimension=0, tiled=True)[0]
    dq_conv, dcv, d_rest, d_point, d_kern, d_depth = conv_back(
        dctx, kern, proj, ck, spread, inputs, d_first_in, w_depth, w_point, w_kern
    )
    by_owner = lambda g: g.reshape(-1, devices, own).transpose(1, 0, 2).reshape(devices, -1)
    kern_by = jnp.tile(unpack_taps(d_kern).reshape(fsdp, -1), (dp, 1))
    small_grad = jnp.concatenate([by_owner(d_depth), kern_by, by_owner(d_vecs)], 1)
    small_grad = jnp.pad(small_grad, ((0, 0), (0, -small_grad.shape[1] % LANES)))
    small_grad = small_grad.reshape(devices, -1, LANES)
    dq, dk, dv = attend_back(proj, probs, att, inv, dctx, dq_conv)
    mask_col = masked[:, None]
    if near:
        mine, other = weight_grad(inputs, dq, dk, dv, dcv, d_point, small_grad, core)
        parts = fold_xy(me, mine, hop(other, CORE_BIT))
        parts = [parts[0]] + [hop(part, bit) for part, bit in zip(parts[1:], (Y_BIT, X_BIT, X_BIT + Y_BIT))]
        parts[0], dq = tie(parts[0], dq)
        d_tokens = leave(dq, dk, dv, dcv, d_rest, mask_col, to_row, w_in)
        d_tokens, parts = tie(d_tokens, parts)
        parts = fold_z(me, parts)
        parts = [parts[0]] + [hop(parts[k], k * Z_BIT) for k in (1, 2, 3)]
        parts[0], mid_sum = tie(parts[0], mid_sum)
        d_out, d_up, d_down = finish_mid(scale, mid_sum)
        d_in, d_point, small_sum = finish(scale, parts)
        small_sum = small_sum.reshape(-1)
    else:
        (grads,) = weight_grad(inputs, dq, dk, dv, dcv, d_point, jnp.zeros((32, 8, LANES), F32))
        d_in = grads[:, :96].reshape(32, 4, 24, ATT).transpose(0, 2, 1, 3).reshape(devices, -1, LANES)
        d_point = grads[:, 96:120].reshape(devices, -1, LANES)
        w_out = mid_grad[:, :48].reshape(BLOCKS, 2, 24, ATT).transpose(0, 2, 1, 3).reshape(devices, -1, LANES)
        w_ffn = mid_grad[:, 48:].reshape(BLOCKS, 4, 48, ATT).transpose(1, 0, 2, 3)
        w_ffn = w_ffn.reshape(4, devices, hid, ATT).transpose(1, 0, 2, 3).reshape(devices, -1, LANES)
        packed = jnp.concatenate([w_out, w_ffn, d_in, d_point, small_grad.astype(BF)], 1)
        total = lax.psum_scatter(packed, AXES, scatter_dimension=0, tiled=True)[0].astype(F32) * scale
        cuts = [2 * own, 2 * own + 2 * hid, 2 * own + 4 * hid, 6 * own + 4 * hid, 7 * own + 4 * hid]
        d_out, d_up, d_down, d_in, d_point, small_sum = jnp.split(total, cuts)
        d_out, d_in, small_sum = d_out.reshape(own, WIDTH), d_in.reshape(own, 4 * ATT), small_sum.reshape(-1)
        d_up, d_down = d_up.reshape(2, hid, ATT).transpose(0, 2, 1), d_down.reshape(2, hid, ATT)
        d_tokens = leave(dq, dk, dv, dcv, d_rest, mask_col, to_row, w_in)
    kern_sum = small_sum[n_depth : n_depth + n_kern].reshape(kernel_weight.shape)
    vec_sum = small_sum[n_depth + n_kern :][:n_vec].reshape(4, own)
    return (
        out,
        d_tokens,
        d_in,
        small_sum[:n_depth].reshape(KER, own),
        d_point,
        kern_sum,
        d_out,
        vec_sum[0],
        vec_sum[1],
        d_up,
        d_down,
        vec_sum[2],
        vec_sum[3],
    )


def solution(mesh):
    return jax.shard_map(
        per_device,
        mesh=mesh,
        in_specs=(
            P(("dp", "fsdp"), None),
            P(("dp", "fsdp")),
            P(("dp", "fsdp")),
            P(("dp", "fsdp"), None),
            P(None, ("dp", "fsdp")),
            P(("dp", "fsdp"), None),
            P("fsdp", None),
            P(("dp", "fsdp"), None),
            P(("dp", "fsdp")),
            P(("dp", "fsdp")),
            P(None, None, ("dp", "fsdp")),
            P(None, ("dp", "fsdp"), None),
            P(("dp", "fsdp")),
            P(("dp", "fsdp")),
            P(("dp", "fsdp"), None),
        ),
        out_specs=(
            P(("dp", "fsdp"), None),
            P(("dp", "fsdp"), None),
            P(("dp", "fsdp"), None),
            P(None, ("dp", "fsdp")),
            P(("dp", "fsdp"), None),
            P("fsdp", None),
            P(("dp", "fsdp"), None),
            P(("dp", "fsdp")),
            P(("dp", "fsdp")),
            P(None, None, ("dp", "fsdp")),
            P(None, ("dp", "fsdp"), None),
            P(("dp", "fsdp")),
            P(("dp", "fsdp")),
        ),
        check_vma=False,
    )
```

time: 578 us -> 339 us (0.59)
  waiting for transfers between devices: 236 us -> 37.3 us
  Pallas kernels: 268 us -> 228 us
  starting transfers between devices: 0.16 us -> 22.4 us
  local copies, waits for them, and re-layouts: 44 us -> 25.2 us
  other arithmetic: 15.8 us -> 5.42 us
    reduce_scatter x2 -> x1, waiting for transfers between devices: 179 us -> 0.01 us  [per_device(): lax.psum_scatter(mid_grad, AXES, scatter_dimension=0, tiled=True)[0]]
    all_gather x1 -> x0, waiting for transfers between devices: 56.1 us -> none  [per_device(): head = lax.all_gather(head_own, AXES, axis=0)]
    ppermute x0 -> x23, waiting for transfers between devices: none -> 37.3 us  [hop(): return lax.ppermute(x, AXES, [(i, i ^ mask) for i in range(32)])]
    ppermute x0 -> x23, starting transfers between devices: none -> 22.3 us  [hop(): return lax.ppermute(x, AXES, [(i, i ^ mask) for i in range(32)])]
    pallas_call x1, Pallas kernels: 37.6 us -> 23.1 us  [attend(): pl.pallas_call(attend_kernel, grid=(rows // SEQ, pairs), in_specs=[col(0)...]
    reshape x12 -> x4, local copies, waits for them, and re-layouts: 17.6 us -> 3.11 us  [the longest x1 0.89 us: per_device(): in_weight.reshape(own, 4, ATT).transpose(1, 0, 2)]
    pallas_call x1, Pallas kernels: 36.5 us -> 25.5 us  [attend_back(): pl.pallas_call(attend_back_kernel, grid=(rows // SEQ, pairs), in_specs=[c...]
    slice x12 -> x7, local copies, waits for them, and re-layouts: 10.6 us -> 0.18 us  [the longest x1 0.08 us: per_device(): small_all[:fsdp, n_depth:n_depth + n_kern].reshape(ATT, HEADS * KER)]
  transfers between devices with their start and end apart: 4 -> 25, of which waited for: 3 -> 13; matrix products, arithmetic and copies ran while one was open for 6% -> 5% of each run, Pallas kernels for 17% -> 44%
where the time goes in v2:
time: 339 us; the launch traced here: 334 us
  Pallas kernels  228 us (67%)
  waiting for transfers between devices  37.3 us (11%)
  local copies, waits for them, and re-layouts  25.2 us (7%)
  starting transfers between devices  22.4 us (7%)
  between operations  15 us (4%)
  other arithmetic  5.42 us (2%)
    pallas_call x1, Pallas kernels, middle(): pl.pallas_call(middle_kernel, grid=(rows // MID,), in_specs=[block(ATT),...  76.9 us
    ppermute x23, waiting for transfers between devices, hop(): return lax.ppermute(x, AXES, [(i, i ^ mask) for i in range(32)])  37.3 us
    pallas_call x1, Pallas kernels, conv_back(): pl.pallas_call(conv_back_kernel, grid=(rows // SEQ,), in_specs=[at(1), bl...  35.8 us
    pallas_call x1, Pallas kernels, attend_back(): pl.pallas_call(attend_back_kernel, grid=(rows // SEQ, pairs), in_specs=[c...  25.5 us
    pallas_call x1, Pallas kernels, enter(): pl.pallas_call(enter_slabs_kernel, grid=(rows // SEQ,), in_specs=[pl.Bloc...  23.6 us
    pallas_call x1, Pallas kernels, attend(): pl.pallas_call(attend_kernel, grid=(rows // SEQ, pairs), in_specs=[col(0)...  23.1 us
    ppermute x23, starting transfers between devices, hop(): return lax.ppermute(x, AXES, [(i, i ^ mask) for i in range(32)])  22.3 us
    pallas_call x1, Pallas kernels, leave(): pl.pallas_call(leave_kernel, grid=(rows // SEQ, 2 * STEPS), in_specs=[blo...  16.6 us
  transfers between devices with their start and end apart: 25, of which 13 were waited for; matrix products, arithmetic and copies ran while one was open for 5% of the time, Pallas kernels for 44%

profile of v2, /device:TPU:0, one launch (start us, length us, event | category | flops | bytes accessed | tf_op | source)
XLA Modules:
  0.0 333.5 jit_solution(1669518372517243003)
XLA Ops:
  11.4 3.0 collective-permute-start
  19.1 3.7 %collective-permute-start.3 = (bf16[256,384]{1,0:T(8,128)(2,1)S(1)}, bf16[256,384]{1,0:T(8,128)(2,1)S(1)}, u32[]{:S(2)}, u32[]{:S(2)}) collective-permute-start(bf16[256,384]{1,0:T(8,128)(2,1)S(1)} %pad_maximum_fusion.refs_0_), channel_id=1, source_target_pairs={{0,6},{1,7},{2,4},{3,5},{4,2},{5,3},{6,0},{7,1},{8,14},{9,15},{10,... | collective-permute-start | bytes 589832 | tf_op jit(solution)/shard_map/ppermute | solution.py:70
  24.9 6.5 %pick.1.inp_ref = bf16[2048,768]{1,0:T(8,128)(2,1)} custom-call(s32[2048,1]{1,0:T(8,128)} %copy.35.pick_ref, bf16[2048,768]{1,0:T(8,128)(2,1)} %tok_ref.1), custom_call_target="tpu_custom_call" | custom-call | flops 6000000000 | bytes 6000000 | tf_op jit(solution)/shard_map/pick/pallas_call | solution.py:214
  31.3 7.8 %collective-permute-done.2.refs_2_ = bf16[256,384]{1,0:T(8,128)(2,1)S(1)} collective-permute-done((bf16[256,384]{1,0:T(8,128)(2,1)S(1)}, bf16[256,384]{1,0:T(8,128)(2,1)S(1)}, u32[]{:S(2)}, u32[]{:S(2)}) %collective-permute-start.2) | collective-permute-done | bytes 196640 | tf_op jit(solution)/shard_map/ppermute | solution.py:70
  42.4 5.4 %collective-permute-done.4.refs_4_ = bf16[256,384]{1,0:T(8,128)(2,1)S(1)} collective-permute-done((bf16[256,384]{1,0:T(8,128)(2,1)S(1)}, bf16[256,384]{1,0:T(8,128)(2,1)S(1)}, u32[]{:S(2)}, u32[]{:S(2)}) %collective-permute-start.4) | collective-permute-done | bytes 196640 | tf_op jit(solution)/shard_map/ppermute | solution.py:70
  49.4 4.0 %collective-permute-done.5.refs_5_ = bf16[256,384]{1,0:T(8,128)(2,1)S(1)} collective-permute-done((bf16[256,384]{1,0:T(8,128)(2,1)S(1)}, bf16[256,384]{1,0:T(8,128)(2,1)S(1)}, u32[]{:S(2)}, u32[]{:S(2)}) %collective-permute-start.5) | collective-permute-done | bytes 196640 | tf_op jit(solution)/shard_map/ppermute | solution.py:70
  53.4 3.7 %collective-permute-done.6.refs_6_ = bf16[256,384]{1,0:T(8,128)(2,1)S(1)} collective-permute-done((bf16[256,384]{1,0:T(8,128)(2,1)S(1)}, bf16[256,384]{1,0:T(8,128)(2,1)S(1)}, u32[]{:S(2)}, u32[]{:S(2)}) %collective-permute-start.6) | collective-permute-done | bytes 196640 | tf_op jit(solution)/shard_map/ppermute | solution.py:70
  58.6 5.1 %collective-permute-done.7.refs_7_ = bf16[256,384]{1,0:T(8,128)(2,1)S(1)} collective-permute-done((bf16[256,384]{1,0:T(8,128)(2,1)S(1)}, bf16[256,384]{1,0:T(8,128)(2,1)S(1)}, u32[]{:S(2)}, u32[]{:S(2)}) %collective-permute-start.7) | collective-permute-done | bytes 196640 | tf_op jit(solution)/shard_map/ppermute | solution.py:70
  71.0 23.6 %enter.1 = (bf16[2048,1536]{1,0:T(8,128)(2,1)}, bf16[2048,768]{1,0:T(8,128)(2,1)}, bf16[2048,384]{1,0:T(8,128)(2,1)}, f32[2048,128]{1,0:T(8,128)}, bf16[2048,384...) custom-call(s32[1]{0:T(128)} %select_n.107.pair_ref, bf16[2048,768]{1,0:T(8,128)(2,1)} %pick.1.inp_ref, ...), custom_call_target="tpu_custom_call" | custom-call | flops 20000000000 | bytes 20000000 | tf_op jit(solution)/shard_map/enter/pallas_call | solution.py:312
  94.6 23.1 %attend.1 = (bf16[2,6,1024,1024]{3,2,1,0:T(8,128)(2,1)}, bf16[2048,384]{1,0:T(8,128)(2,1)}, f32[2048,384]{1,0:T(8,128)}) custom-call(bf16[2048,1536]{1,0:T(8,128)(2,1)} %get-tuple-element.85.q_ref.k_ref.v_ref.cv_ref, bf16[2048,1536]{1,0:T(8,128)(2,1)} %get-tuple-element.85.q_ref.k_ref.v_ref.cv_ref, bf16[2048,1536]{1,0:T(8,128)(2,1)} %get-tuple-element.85.q_ref.k_ref.v_ref.cv_ref), custom_call_target="tpu_custom_call" | custom-call | flops 24999999488 | bytes 35000000 | tf_op jit(solution)/shard_map/attend/pallas_call | solution.py:369
  117.7 76.9 %middle.1 = (bf16[2048,768]{1,0:T(8,128)(2,1)}, bf16[2048,768]{1,0:T(8,128)(2,1)}, f32[2048,768]{1,0:T(8,128)}, f32[4,768]{1,0:T(4,128)}, bf16[32,240,384]{2,1,0:T(8,128)(2,1)}) custom-call(bf16[2048,384]{1,0:T(8,128)(2,1)} %get-tuple-element.86.att_ref.o_ref, bf16[2048,384]{1,0:T(8,128)(2,1)} %get-tuple-element.87.conv_ref, bf16[2048,768]{1,0:T(8,128)(2,1)} %pick.1.inp_ref, ...), custom_call_target="tpu_custom_call" | custom-call | flops 60000002048 | bytes 40000000 | tf_op jit(solution)/shard_map/middle/pallas_call | solution.py:542
  195.5 35.8 %conv_back.1 = (f32[2048,384]{1,0:T(8,128)}, bf16[2048,384]{1,0:T(8,128)(2,1)}, f32[2048,768]{1,0:T(8,128)}, f32[768,384]{1,0:T(8,128)}, f32[384,128]{1,0:T(8,128)}, /*index=5*/f32[9,768]{1,0:T(8,128)}) custom-call(bf16[2048,768]{1,0:T(8,128)(2,1)} %get-tuple-element.92.dconv_ref.datt_ref, f32[2048,128]{1,0:T(8,128)} %get-tuple-element.93.kern_ref, ...), custom_call_target="tpu_custom_call" | custom-call | flops 24999999488 | bytes 30000000 | tf_op jit(solution)/shard_map/conv_back/pallas_call | solution.py:682
  235.8 25.5 %attend_back.1 = (bf16[2048,384]{1,0:T(8,128)(2,1)}, bf16[2048,384]{1,0:T(8,128)(2,1)}, bf16[2048,384]{1,0:T(8,128)(2,1)}) custom-call(bf16[2048,1536]{1,0:T(8,128)(2,1)} %get-tuple-element.85.q_ref.k_ref.v_ref.cv_ref, bf16[2048,1536]{1,0:T(8,128)(2,1)} %get-tuple-element.85.q_ref.k_ref.v_ref.cv_ref, ...), custom_call_target="tpu_custom_call" | custom-call | flops 30000001024 | bytes 40000000 | tf_op jit(solution)/shard_map/attend_back/pallas_call | solution.py:746
  261.2 12.7 %weight_grad.1 = (bf16[16,128,384]{2,1,0:T(8,128)(2,1)}, bf16[16,128,384]{2,1,0:T(8,128)(2,1)}) custom-call(s32[1]{0:T(128)S(6)} %select_n.123.core_ref, bf16[2048,768]{1,0:T(8,128)(2,1)} %pick.1.inp_ref, bf16[2048,384]{1,0:T(8,128)(2,1)} %get-tuple-element.110.dq_ref, bf16[2048,384]{1,0:T(8,128)(2,1)} %get-tuple-element.100.dk_ref, ...), custom_call_target="tpu_custom_call" | custom-call | flops 12000000000 | bytes 12000000 | tf_op jit(solution)/shard_map/weight_grad/pallas_call | solution.py:800
  275.6 1.9 collective-permute-done.16
  278.7 3.9 %fold_xy.1 = (bf16[4,128,384]{2,1,0:T(8,128)(2,1)}, bf16[4,128,384]{2,1,0:T(8,128)(2,1)}, bf16[4,128,384]{2,1,0:T(8,128)(2,1)}, bf16[4,128,384]{2,1,0:T(8,128)(2,1)}) custom-call(s32[1]{0:T(128)} %bitcast.me_ref, bf16[2,4,2,128,384]{4,3,2,1,0:T(8,128)(2,1)} %bitcast.115, bf16[2,4,2,128,384]{4,3,2,1,0:T(8,128)(2,1)} %bitcast.116), custom_call_target="tpu_custom_call" | custom-call | bytes 4718592 | tf_op jit(solution)/shard_map/fold_xy/pallas_call | solution.py:87
  284.4 1.7 collective-permute-start.19
  286.1 16.6 %leave.1 = f32[2048,768]{1,0:T(8,128)} custom-call(bf16[2048,384]{1,0:T(8,128)(2,1)} %get-tuple-element.110.dq_ref, bf16[2048,384]{1,0:T(8,128)(2,1)} %get-tuple-element.100.dk_ref, bf16[2048,384]{1,0:T(8,128)(2,1)} %get-tuple-element.101.dv_ref, bf16[2048,384]{1,0:T(8,128)(2,1)} %get-tuple-element.102.dcv_ref, f32[2048,768]{1,0:T(8,128)} %get-tuple-element.111.rest_ref, ...), custom_call_target="tpu_custom_call" | custom-call | flops 15000000512 | bytes 30000000 | tf_op jit(solution)/shard_map/leave/pallas_call | solution.py:842
  302.6 2.4 collective-permute-done.19.refs_3_
  305.9 2.8 collective-permute-start.21
  311.0 5.0 %collective-permute-done.21.c_ref = bf16[128,384]{1,0:T(8,128)(2,1)S(1)} collective-permute-done((bf16[128,384]{1,0:T(8,128)(2,1)S(1)}, bf16[128,384]{1,0:T(8,128)(2,1)S(1)}, u32[]{:S(2)}, u32[]{:S(2)}) %collective-permute-start.21) | collective-permute-done | bytes 98336 | tf_op jit(solution)/shard_map/ppermute | solution.py:70
  317.3 1.7 finish.1
  322.6 1.9 finish_mid.1
  324.5 1.8 copy.49
  (174 shorter events, 42.1 us)
Async XLA Ops:
  7.2 110.5 %all-gather.3.cloned.1.call-start = ((), (), s32[]{:S(2)}) async-start(), calls=%async_computation.2 | async-start | bytes 6082560 | tf_op jit(solution)/shard_map/all_gather | solution.py:914
  11.4 7.5 %collective-permute-start = (bf16[128,384]{1,0:T(8,128)(2,1)S(1)}, bf16[128,384]{1,0:T(8,128)(2,1)S(1)}, u32[]{:S(2)}, u32[]{:S(2)}) collective-permute-start(bf16[128,384]{1,0:T(8,128)(2,1)S(1)} %pad_maximum_fusion.3), channel_id=1, source_target_pairs={{0,1},{1,0},{2,3},{3,2},{4,5},{5,4},{6,7},{7,6},{8,9},{9,8},{10,11... | collective-permute-start | bytes 294920 | tf_op jit(solution)/shard_map/ppermute | solution.py:70
  19.1 12.3 %collective-permute-start.3 = (bf16[256,384]{1,0:T(8,128)(2,1)S(1)}, bf16[256,384]{1,0:T(8,128)(2,1)S(1)}, u32[]{:S(2)}, u32[]{:S(2)}) collective-permute-start(bf16[256,384]{1,0:T(8,128)(2,1)S(1)} %pad_maximum_fusion.refs_0_), channel_id=1, source_target_pairs={{0,6},{1,7},{2,4},{3,5},{4,2},{5,3},{6,0},{7,1},{8,14},{9,15},{10,... | collective-permute-start | bytes 589832 | tf_op jit(solution)/shard_map/ppermute | solution.py:70
  22.7 16.4 %collective-permute-start.2 = (bf16[256,384]{1,0:T(8,128)(2,1)S(1)}, bf16[256,384]{1,0:T(8,128)(2,1)S(1)}, u32[]{:S(2)}, u32[]{:S(2)}) collective-permute-start(bf16[256,384]{1,0:T(8,128)(2,1)S(1)} %pad_maximum_fusion.refs_0_), channel_id=1, source_target_pairs={{0,4},{1,5},{2,6},{3,7},{4,0},{5,1},{6,2},{7,3},{8,12},{9,13},{10,... | collective-permute-start | bytes 589832 | tf_op jit(solution)/shard_map/ppermute | solution.py:70
  22.7 16.4 %collective-permute-start.1 = (bf16[256,384]{1,0:T(8,128)(2,1)S(1)}, bf16[256,384]{1,0:T(8,128)(2,1)S(1)}, u32[]{:S(2)}, u32[]{:S(2)}) collective-permute-start(bf16[256,384]{1,0:T(8,128)(2,1)S(1)} %pad_maximum_fusion.refs_0_), channel_id=1, source_target_pairs={{0,2},{1,3},{2,0},{3,1},{4,6},{5,7},{6,4},{7,5},{8,10},{9,11},{10,... | collective-permute-start | bytes 589832 | tf_op jit(solution)/shard_map/ppermute | solution.py:70
  39.2 271.1 %reduce-scatter.2.cloned.1.call-start = ((), (), s32[]{:S(2)}) async-start(), calls=%async_computation.1 | async-start | bytes 6082560 | tf_op jit(solution)/shard_map/reduce_scatter | solution.py:940
  40.0 23.7 %collective-permute-start.8 = (bf16[256,384]{1,0:T(8,128)(2,1)S(1)}, bf16[256,384]{1,0:T(8,128)(2,1)S(1)}, u32[]{:S(2)}, u32[]{:S(2)}) collective-permute-start(bf16[256,384]{1,0:T(8,128)(2,1)S(1)} %pad_maximum_fusion.refs_0_), channel_id=1, source_target_pairs={{0,8},{1,9},{2,10},{3,11},{4,12},{5,13},{6,14},{7,15},{8,0},{9,1},... | collective-permute-start | bytes 589832 | tf_op jit(solution)/shard_map/ppermute | solution.py:70
  40.1 7.8 %collective-permute-start.4 = (bf16[256,384]{1,0:T(8,128)(2,1)S(1)}, bf16[256,384]{1,0:T(8,128)(2,1)S(1)}, u32[]{:S(2)}, u32[]{:S(2)}) collective-permute-start(bf16[256,384]{1,0:T(8,128)(2,1)S(1)} %pad_maximum_fusion.refs_0_), channel_id=1, source_target_pairs={{0,16},{1,17},{2,18},{3,19},{4,20},{5,21},{6,22},{7,23},{8,24},{9,... | collective-permute-start | bytes 589832 | tf_op jit(solution)/shard_map/ppermute | solution.py:70
  41.6 22.7 %collective-permute-start.9 = (bf16[256,384]{1,0:T(8,128)(2,1)S(1)}, bf16[256,384]{1,0:T(8,128)(2,1)S(1)}, u32[]{:S(2)}, u32[]{:S(2)}) collective-permute-start(bf16[256,384]{1,0:T(8,128)(2,1)S(1)} %collective-permute-done.1.refs_1_), channel_id=1, source_target_pairs={{0,8},{1,9},{2,10},{3,11},{4,12},{5,13},{6,14},{7,15},{8,0},{9,1},... | collective-permute-start | bytes 589832 | tf_op jit(solution)/shard_map/ppermute | solution.py:70
  41.8 11.6 %collective-permute-start.5 = (bf16[256,384]{1,0:T(8,128)(2,1)S(1)}, bf16[256,384]{1,0:T(8,128)(2,1)S(1)}, u32[]{:S(2)}, u32[]{:S(2)}) collective-permute-start(bf16[256,384]{1,0:T(8,128)(2,1)S(1)} %collective-permute-done.1.refs_1_), channel_id=1, source_target_pairs={{0,16},{1,17},{2,18},{3,19},{4,20},{5,21},{6,22},{7,23},{8,24},{9,... | collective-permute-start | bytes 589832 | tf_op jit(solution)/shard_map/ppermute | solution.py:70
  42.3 22.1 %collective-permute-start.10 = (bf16[256,384]{1,0:T(8,128)(2,1)S(1)}, bf16[256,384]{1,0:T(8,128)(2,1)S(1)}, u32[]{:S(2)}, u32[]{:S(2)}) collective-permute-start(bf16[256,384]{1,0:T(8,128)(2,1)S(1)} %collective-permute-done.2.refs_2_), channel_id=1, source_target_pairs={{0,8},{1,9},{2,10},{3,11},{4,12},{5,13},{6,14},{7,15},{8,0},{9,1},... | collective-permute-start | bytes 589832 | tf_op jit(solution)/shard_map/ppermute | solution.py:70
  47.9 9.3 %collective-permute-start.6 = (bf16[256,384]{1,0:T(8,128)(2,1)S(1)}, bf16[256,384]{1,0:T(8,128)(2,1)S(1)}, u32[]{:S(2)}, u32[]{:S(2)}) collective-permute-start(bf16[256,384]{1,0:T(8,128)(2,1)S(1)} %collective-permute-done.2.refs_2_), channel_id=1, source_target_pairs={{0,16},{1,17},{2,18},{3,19},{4,20},{5,21},{6,22},{7,23},{8,24},{9,... | collective-permute-start | bytes 589832 | tf_op jit(solution)/shard_map/ppermute | solution.py:70
  53.4 11.6 %collective-permute-start.11 = (bf16[256,384]{1,0:T(8,128)(2,1)S(1)}, bf16[256,384]{1,0:T(8,128)(2,1)S(1)}, u32[]{:S(2)}, u32[]{:S(2)}) collective-permute-start(bf16[256,384]{1,0:T(8,128)(2,1)S(1)} %collective-permute-done.3.refs_3_), channel_id=1, source_target_pairs={{0,8},{1,9},{2,10},{3,11},{4,12},{5,13},{6,14},{7,15},{8,0},{9,1},... | collective-permute-start | bytes 589832 | tf_op jit(solution)/shard_map/ppermute | solution.py:70
  57.1 6.6 %collective-permute-start.7 = (bf16[256,384]{1,0:T(8,128)(2,1)S(1)}, bf16[256,384]{1,0:T(8,128)(2,1)S(1)}, u32[]{:S(2)}, u32[]{:S(2)}) collective-permute-start(bf16[256,384]{1,0:T(8,128)(2,1)S(1)} %collective-permute-done.3.refs_3_), channel_id=1, source_target_pairs={{0,16},{1,17},{2,18},{3,19},{4,20},{5,21},{6,22},{7,23},{8,24},{9,... | collective-permute-start | bytes 589832 | tf_op jit(solution)/shard_map/ppermute | solution.py:70
  63.8 1.7 collective-permute-start.13
  64.3 1.5 collective-permute-start.14
  64.4 1.7 collective-permute-start.15
  273.9 3.6 %collective-permute-start.16 = (bf16[16,128,384]{2,1,0:T(8,128)(2,1)}, bf16[16,128,384]{2,1,0:T(8,128)(2,1)S(1)}, u32[]{:S(2)}, u32[]{:S(2)}) collective-permute-start(bf16[16,128,384]{2,1,0:T(8,128)(2,1)} %get-tuple-element.108), channel_id=1, source_target_pairs={{0,8},{1,9},{2,10},{3,11},{4,12},{5,13},{6,14},{7,15},{8,0},{9,1},... | collective-permute-start | bytes 4718600 | tf_op jit(solution)/shard_map/ppermute | solution.py:70
  282.5 20.1 %collective-permute-start.17 = (bf16[4,128,384]{2,1,0:T(8,128)(2,1)}, bf16[4,128,384]{2,1,0:T(8,128)(2,1)S(1)}, u32[]{:S(2)}, u32[]{:S(2)}) collective-permute-start(bf16[4,128,384]{2,1,0:T(8,128)(2,1)} %get-tuple-element.114), channel_id=1, source_target_pairs={{0,1},{1,0},{2,3},{3,2},{4,5},{5,4},{6,7},{7,6},{8,9},{9,8},{10,11... | collective-permute-start | bytes 1179656 | tf_op jit(solution)/shard_map/ppermute | solution.py:70
  282.8 19.8 %collective-permute-start.18 = (bf16[4,128,384]{2,1,0:T(8,128)(2,1)}, bf16[4,128,384]{2,1,0:T(8,128)(2,1)S(1)}, u32[]{:S(2)}, u32[]{:S(2)}) collective-permute-start(bf16[4,128,384]{2,1,0:T(8,128)(2,1)} %get-tuple-element.115), channel_id=1, source_target_pairs={{0,16},{1,17},{2,18},{3,19},{4,20},{5,21},{6,22},{7,23},{8,24},{9,... | collective-permute-start | bytes 1179656 | tf_op jit(solution)/shard_map/ppermute | solution.py:70
  284.4 20.7 %collective-permute-start.19 = (bf16[4,128,384]{2,1,0:T(8,128)(2,1)}, bf16[4,128,384]{2,1,0:T(8,128)(2,1)S(1)}, u32[]{:S(2)}, u32[]{:S(2)}) collective-permute-start(bf16[4,128,384]{2,1,0:T(8,128)(2,1)} %get-tuple-element.116), channel_id=1, source_target_pairs={{0,17},{1,16},{2,19},{3,18},{4,21},{5,20},{6,23},{7,22},{8,25},{9,... | collective-permute-start | bytes 1179656 | tf_op jit(solution)/shard_map/ppermute | solution.py:70
  305.9 5.1 %collective-permute-start.20 = (bf16[128,384]{1,0:T(8,128)(2,1)S(1)}, bf16[128,384]{1,0:T(8,128)(2,1)S(1)}, u32[]{:S(2)}, u32[]{:S(2)}) collective-permute-start(bf16[128,384]{1,0:T(8,128)(2,1)S(1)} %get-tuple-element.125), channel_id=1, source_target_pairs={{0,2},{1,3},{2,0},{3,1},{4,6},{5,7},{6,4},{7,5},{8,10},{9,11},{10,... | collective-permute-start | bytes 294920 | tf_op jit(solution)/shard_map/ppermute | solution.py:70
  305.9 10.1 %collective-permute-start.21 = (bf16[128,384]{1,0:T(8,128)(2,1)S(1)}, bf16[128,384]{1,0:T(8,128)(2,1)S(1)}, u32[]{:S(2)}, u32[]{:S(2)}) collective-permute-start(bf16[128,384]{1,0:T(8,128)(2,1)S(1)} %get-tuple-element.126), channel_id=1, source_target_pairs={{0,4},{1,5},{2,6},{3,7},{4,0},{5,1},{6,2},{7,3},{8,12},{9,13},{10,... | collective-permute-start | bytes 294920 | tf_op jit(solution)/shard_map/ppermute | solution.py:70
  308.7 7.4 %collective-permute-start.22 = (bf16[128,384]{1,0:T(8,128)(2,1)S(1)}, bf16[128,384]{1,0:T(8,128)(2,1)S(1)}, u32[]{:S(2)}, u32[]{:S(2)}) collective-permute-start(bf16[128,384]{1,0:T(8,128)(2,1)S(1)} %get-tuple-element.127), channel_id=1, source_target_pairs={{0,6},{1,7},{2,4},{3,5},{4,2},{5,3},{6,0},{7,1},{8,14},{9,15},{10,... | collective-permute-start | bytes 294920 | tf_op jit(solution)/shard_map/ppermute | solution.py:70
  (26 other events, 285.7 us)
Sparse Core Ops, SparseCore 0:
  39.3 67.8 all-gather.2
  194.7 113.1 reduce-scatter.1

commit v3 on v2

--- a/solution.py
+++ b/solution.py
@@ -147,7 +147,7 @@
     out_ref[:, :ATT] = total[:24]
     out_ref[:, ATT:] = total[24:48]
     for g in (0, 1):
-        up_ref[g] = total[48 + 48 * g : 96 + 48 * g].T
+        up_ref[g] = total[48 + 48 * g : 96 + 48 * g]
         down_ref[g] = total[144 + 48 * g : 192 + 48 * g]
 
 
@@ -159,7 +159,7 @@
         out_specs=[vmem] * 3,
         out_shape=[
             jax.ShapeDtypeStruct((24, WIDTH), F32),
-            jax.ShapeDtypeStruct((2, ATT, 48), F32),
+            jax.ShapeDtypeStruct((2, 48, ATT), F32),
             jax.ShapeDtypeStruct((2, 48, ATT), F32),
         ],
         name="finish_mid",
@@ -388,13 +388,12 @@
 
 
 def gelu_both(u):
-    mag = jnp.abs(u)
-    t = 1.0 / (1.0 + ERF_P * mag)
-    poly = ERF_A[4]
+    t = 1.0 / (1.0 + ERF_P * jnp.abs(u))
+    poly = 0.5 * ERF_A[4]
     for a in ERF_A[3::-1]:
-        poly = poly * t + a
-    e = jnp.exp(-0.5 * (u * u))
-    tail = (0.5 * t) * poly * e
+        poly = poly * t + 0.5 * a
+    e = jnp.exp2((-0.5 * math.log2(math.e)) * (u * u))
+    tail = t * poly * e
     cdf = jnp.where(u > 0, 1.0 - tail, tail)
     return u * cdf, cdf + (PHI * u) * e
 
@@ -909,10 +908,11 @@
         pair, core = me // 2, me // CORE_BIT % 2
         slab, pick = tie(pair_slab(head_own, small_own), pick)
         slabs = [slab] + [hop(slab, k * Z_BIT) for k in (1, 2, 3)]
-        inputs, slabs = tie(pick_rows(pick, tokens), slabs)
-        slabs, mid_own = tie(slabs, mid_own)
+        across = [hop(slab, X_BIT)]
+        inputs, (across, slabs[1:]) = tie(pick_rows(pick, tokens), (across, slabs[1:]))
+        slabs[1:], mid_own = tie(slabs[1:], mid_own)
         mid = lax.all_gather(mid_own, AXES, axis=0)
-        slabs = slabs + [hop(slab, X_BIT) for slab in slabs]
+        slabs = slabs + across + [hop(slab, X_BIT) for slab in slabs[1:]]
         slabs = slabs + [hop(slab, CORE_BIT) for slab in slabs]
         small_all = small_rows(slabs, pair)
     else:
@@ -959,6 +959,8 @@
         parts = [parts[0]] + [hop(parts[k], k * Z_BIT) for k in (1, 2, 3)]
         parts[0], mid_sum = tie(parts[0], mid_sum)
         d_out, d_up, d_down = finish_mid(scale, mid_sum)
+        d_up = d_up.transpose(0, 2, 1)
+        parts[3], d_out = tie(parts[3], d_out)
         d_in, d_point, small_sum = finish(scale, parts)
         small_sum = small_sum.reshape(-1)
     else:

time: 339 us -> 329 us (0.971)
  waiting for transfers between devices: 37.3 us -> 30.4 us
    ppermute x23, waiting for transfers between devices: 37.3 us -> 30.4 us  [hop(): return lax.ppermute(x, AXES, [(i, i ^ mask) for i in range(32)])]
    unnamed x69 -> x68, local copies, waits for them, and re-layouts: 7.17 us -> 5.37 us
  transfers between devices with their start and end apart: 25 -> 25, of which waited for: 13 -> 12; matrix products, arithmetic and copies ran while one was open for 5% -> 5% of each run, Pallas kernels for 44% -> 46%
where the time goes in v3:
time: 329 us; the launch traced here: 323 us
  Pallas kernels  227 us (69%)
  waiting for transfers between devices  30.4 us (9%)
  local copies, waits for them, and re-layouts  23.4 us (7%)
  starting transfers between devices  22.5 us (7%)
  between operations  15.1 us (5%)
  other arithmetic  5.42 us (2%)
    pallas_call x1, Pallas kernels, middle(): pl.pallas_call(middle_kernel, grid=(rows // MID,), in_specs=[block(ATT),...  75.4 us
    pallas_call x1, Pallas kernels, conv_back(): pl.pallas_call(conv_back_kernel, grid=(rows // SEQ,), in_specs=[at(1), bl...  35.8 us
    ppermute x23, waiting for transfers between devices, hop(): return lax.ppermute(x, AXES, [(i, i ^ mask) for i in range(32)])  30.4 us
    pallas_call x1, Pallas kernels, attend_back(): pl.pallas_call(attend_back_kernel, grid=(rows // SEQ, pairs), in_specs=[c...  25.5 us
    pallas_call x1, Pallas kernels, enter(): pl.pallas_call(enter_slabs_kernel, grid=(rows // SEQ,), in_specs=[pl.Bloc...  23.6 us
    pallas_call x1, Pallas kernels, attend(): pl.pallas_call(attend_kernel, grid=(rows // SEQ, pairs), in_specs=[col(0)...  23.1 us
    ppermute x23, starting transfers between devices, hop(): return lax.ppermute(x, AXES, [(i, i ^ mask) for i in range(32)])  22.4 us
    pallas_call x1, Pallas kernels, leave(): pl.pallas_call(leave_kernel, grid=(rows // SEQ, 2 * STEPS), in_specs=[blo...  16.6 us
  transfers between devices with their start and end apart: 25, of which 12 were waited for; matrix products, arithmetic and copies ran while one was open for 5% of the time, Pallas kernels for 46%

profile of v3, /device:TPU:0, one launch (start us, length us, event | category | flops | bytes accessed | tf_op | source)
XLA Modules:
  0.0 323.4 jit_solution(552090548481671690)
XLA Ops:
  11.4 3.0 collective-permute-start
  19.1 3.7 %collective-permute-start.4 = (bf16[256,384]{1,0:T(8,128)(2,1)S(1)}, bf16[256,384]{1,0:T(8,128)(2,1)S(1)}, u32[]{:S(2)}, u32[]{:S(2)}) collective-permute-start(bf16[256,384]{1,0:T(8,128)(2,1)S(1)} %pad_maximum_fusion.refs_0_), channel_id=1, source_target_pairs={{0,6},{1,7},{2,4},{3,5},{4,2},{5,3},{6,0},{7,1},{8,14},{9,15},{10,... | collective-permute-start | bytes 589832 | tf_op jit(solution)/shard_map/ppermute | solution.py:70
  26.4 6.5 %pick.1.inp_ref = bf16[2048,768]{1,0:T(8,128)(2,1)} custom-call(s32[2048,1]{1,0:T(8,128)} %copy.34.pick_ref, bf16[2048,768]{1,0:T(8,128)(2,1)} %tok_ref.1), custom_call_target="tpu_custom_call" | custom-call | flops 6000000000 | bytes 6000000 | tf_op jit(solution)/shard_map/pick/pallas_call | solution.py:214
  32.8 6.3 %collective-permute-done.3.refs_2_ = bf16[256,384]{1,0:T(8,128)(2,1)S(1)} collective-permute-done((bf16[256,384]{1,0:T(8,128)(2,1)S(1)}, bf16[256,384]{1,0:T(8,128)(2,1)S(1)}, u32[]{:S(2)}, u32[]{:S(2)}) %collective-permute-start.3) | collective-permute-done | bytes 196640 | tf_op jit(solution)/shard_map/ppermute | solution.py:70
  42.7 5.7 %collective-permute-done.5.refs_5_ = bf16[256,384]{1,0:T(8,128)(2,1)S(1)} collective-permute-done((bf16[256,384]{1,0:T(8,128)(2,1)S(1)}, bf16[256,384]{1,0:T(8,128)(2,1)S(1)}, u32[]{:S(2)}, u32[]{:S(2)}) %collective-permute-start.5) | collective-permute-done | bytes 196640 | tf_op jit(solution)/shard_map/ppermute | solution.py:70
  48.4 4.7 %collective-permute-done.6.refs_6_ = bf16[256,384]{1,0:T(8,128)(2,1)S(1)} collective-permute-done((bf16[256,384]{1,0:T(8,128)(2,1)S(1)}, bf16[256,384]{1,0:T(8,128)(2,1)S(1)}, u32[]{:S(2)}, u32[]{:S(2)}) %collective-permute-start.6) | collective-permute-done | bytes 196640 | tf_op jit(solution)/shard_map/ppermute | solution.py:70
  54.5 4.4 %collective-permute-done.7.refs_7_ = bf16[256,384]{1,0:T(8,128)(2,1)S(1)} collective-permute-done((bf16[256,384]{1,0:T(8,128)(2,1)S(1)}, bf16[256,384]{1,0:T(8,128)(2,1)S(1)}, u32[]{:S(2)}, u32[]{:S(2)}) %collective-permute-start.7) | collective-permute-done | bytes 196640 | tf_op jit(solution)/shard_map/ppermute | solution.py:70
  66.2 23.6 %enter.1 = (bf16[2048,1536]{1,0:T(8,128)(2,1)}, bf16[2048,768]{1,0:T(8,128)(2,1)}, bf16[2048,384]{1,0:T(8,128)(2,1)}, f32[2048,128]{1,0:T(8,128)}, bf16[2048,384...) custom-call(s32[1]{0:T(128)} %select_n.107.pair_ref, bf16[2048,768]{1,0:T(8,128)(2,1)} %pick.1.inp_ref, ...), custom_call_target="tpu_custom_call" | custom-call | flops 20000000000 | bytes 20000000 | tf_op jit(solution)/shard_map/enter/pallas_call | solution.py:312
  89.8 23.1 %attend.1 = (bf16[2,6,1024,1024]{3,2,1,0:T(8,128)(2,1)}, bf16[2048,384]{1,0:T(8,128)(2,1)}, f32[2048,384]{1,0:T(8,128)}) custom-call(bf16[2048,1536]{1,0:T(8,128)(2,1)} %get-tuple-element.85.q_ref.k_ref.v_ref.cv_ref, bf16[2048,1536]{1,0:T(8,128)(2,1)} %get-tuple-element.85.q_ref.k_ref.v_ref.cv_ref, bf16[2048,1536]{1,0:T(8,128)(2,1)} %get-tuple-element.85.q_ref.k_ref.v_ref.cv_ref), custom_call_target="tpu_custom_call" | custom-call | flops 24999999488 | bytes 35000000 | tf_op jit(solution)/shard_map/attend/pallas_call | solution.py:369
  112.9 75.4 %middle.1 = (bf16[2048,768]{1,0:T(8,128)(2,1)}, bf16[2048,768]{1,0:T(8,128)(2,1)}, f32[2048,768]{1,0:T(8,128)}, f32[4,768]{1,0:T(4,128)}, bf16[32,240,384]{2,1,0:T(8,128)(2,1)}) custom-call(bf16[2048,384]{1,0:T(8,128)(2,1)} %get-tuple-element.86.att_ref.o_ref, bf16[2048,384]{1,0:T(8,128)(2,1)} %get-tuple-element.87.conv_ref, bf16[2048,768]{1,0:T(8,128)(2,1)} %pick.1.inp_ref, ...), custom_call_target="tpu_custom_call" | custom-call | flops 60000002048 | bytes 40000000 | tf_op jit(solution)/shard_map/middle/pallas_call | solution.py:541
  189.3 35.8 %conv_back.1 = (f32[2048,384]{1,0:T(8,128)}, bf16[2048,384]{1,0:T(8,128)(2,1)}, f32[2048,768]{1,0:T(8,128)}, f32[768,384]{1,0:T(8,128)}, f32[384,128]{1,0:T(8,128)}, /*index=5*/f32[9,768]{1,0:T(8,128)}) custom-call(bf16[2048,768]{1,0:T(8,128)(2,1)} %get-tuple-element.92.dconv_ref.datt_ref, f32[2048,128]{1,0:T(8,128)} %get-tuple-element.93.kern_ref, ...), custom_call_target="tpu_custom_call" | custom-call | flops 24999999488 | bytes 30000000 | tf_op jit(solution)/shard_map/conv_back/pallas_call | solution.py:681
  229.6 25.5 %attend_back.1 = (bf16[2048,384]{1,0:T(8,128)(2,1)}, bf16[2048,384]{1,0:T(8,128)(2,1)}, bf16[2048,384]{1,0:T(8,128)(2,1)}) custom-call(bf16[2048,1536]{1,0:T(8,128)(2,1)} %get-tuple-element.85.q_ref.k_ref.v_ref.cv_ref, bf16[2048,1536]{1,0:T(8,128)(2,1)} %get-tuple-element.85.q_ref.k_ref.v_ref.cv_ref, ...), custom_call_target="tpu_custom_call" | custom-call | flops 30000001024 | bytes 40000000 | tf_op jit(solution)/shard_map/attend_back/pallas_call | solution.py:745
  255.0 12.7 %weight_grad.1 = (bf16[16,128,384]{2,1,0:T(8,128)(2,1)}, bf16[16,128,384]{2,1,0:T(8,128)(2,1)}) custom-call(s32[1]{0:T(128)S(6)} %select_n.123.core_ref, bf16[2048,768]{1,0:T(8,128)(2,1)} %pick.1.inp_ref, bf16[2048,384]{1,0:T(8,128)(2,1)} %get-tuple-element.110.dq_ref, bf16[2048,384]{1,0:T(8,128)(2,1)} %get-tuple-element.100.dk_ref, ...), custom_call_target="tpu_custom_call" | custom-call | flops 12000000000 | bytes 12000000 | tf_op jit(solution)/shard_map/weight_grad/pallas_call | solution.py:799
  269.4 2.0 collective-permute-done.16
  272.5 3.9 %fold_xy.1 = (bf16[4,128,384]{2,1,0:T(8,128)(2,1)}, bf16[4,128,384]{2,1,0:T(8,128)(2,1)}, bf16[4,128,384]{2,1,0:T(8,128)(2,1)}, bf16[4,128,384]{2,1,0:T(8,128)(2,1)}) custom-call(s32[1]{0:T(128)} %bitcast.me_ref, bf16[2,4,2,128,384]{4,3,2,1,0:T(8,128)(2,1)} %bitcast.114, bf16[2,4,2,128,384]{4,3,2,1,0:T(8,128)(2,1)} %bitcast.115), custom_call_target="tpu_custom_call" | custom-call | bytes 4718592 | tf_op jit(solution)/shard_map/fold_xy/pallas_call | solution.py:87
  276.5 1.7 collective-permute-start.18
  278.2 1.7 collective-permute-start.19
  279.9 16.6 %leave.1 = f32[2048,768]{1,0:T(8,128)} custom-call(bf16[2048,384]{1,0:T(8,128)(2,1)} %get-tuple-element.110.dq_ref, bf16[2048,384]{1,0:T(8,128)(2,1)} %get-tuple-element.100.dk_ref, bf16[2048,384]{1,0:T(8,128)(2,1)} %get-tuple-element.101.dv_ref, bf16[2048,384]{1,0:T(8,128)(2,1)} %get-tuple-element.102.dcv_ref, f32[2048,768]{1,0:T(8,128)} %get-tuple-element.111.rest_ref, ...), custom_call_target="tpu_custom_call" | custom-call | flops 15000000512 | bytes 30000000 | tf_op jit(solution)/shard_map/leave/pallas_call | solution.py:841
  296.5 2.4 collective-permute-done.19.refs_3_
  299.7 2.1 collective-permute-start.22
  301.8 2.3 collective-permute-start.21
  304.1 1.7 finish_mid.1
  307.2 2.4 collective-permute-done.20.b_ref
  310.9 1.7 finish.1
  (173 shorter events, 39.7 us)
Async XLA Ops:
  7.2 105.8 %all-gather.3.cloned.1.call-start = ((), (), s32[]{:S(2)}) async-start(), calls=%async_computation.2 | async-start | bytes 6082560 | tf_op jit(solution)/shard_map/all_gather | solution.py:914
  11.4 7.5 %collective-permute-start = (bf16[128,384]{1,0:T(8,128)(2,1)S(1)}, bf16[128,384]{1,0:T(8,128)(2,1)S(1)}, u32[]{:S(2)}, u32[]{:S(2)}) collective-permute-start(bf16[128,384]{1,0:T(8,128)(2,1)S(1)} %pad_maximum_fusion.3), channel_id=1, source_target_pairs={{0,1},{1,0},{2,3},{3,2},{4,5},{5,4},{6,7},{7,6},{8,9},{9,8},{10,11... | collective-permute-start | bytes 294920 | tf_op jit(solution)/shard_map/ppermute | solution.py:70
  19.1 13.8 %collective-permute-start.4 = (bf16[256,384]{1,0:T(8,128)(2,1)S(1)}, bf16[256,384]{1,0:T(8,128)(2,1)S(1)}, u32[]{:S(2)}, u32[]{:S(2)}) collective-permute-start(bf16[256,384]{1,0:T(8,128)(2,1)S(1)} %pad_maximum_fusion.refs_0_), channel_id=1, source_target_pairs={{0,6},{1,7},{2,4},{3,5},{4,2},{5,3},{6,0},{7,1},{8,14},{9,15},{10,... | collective-permute-start | bytes 589832 | tf_op jit(solution)/shard_map/ppermute | solution.py:70
  22.7 16.4 %collective-permute-start.3 = (bf16[256,384]{1,0:T(8,128)(2,1)S(1)}, bf16[256,384]{1,0:T(8,128)(2,1)S(1)}, u32[]{:S(2)}, u32[]{:S(2)}) collective-permute-start(bf16[256,384]{1,0:T(8,128)(2,1)S(1)} %pad_maximum_fusion.refs_0_), channel_id=1, source_target_pairs={{0,4},{1,5},{2,6},{3,7},{4,0},{5,1},{6,2},{7,3},{8,12},{9,13},{10,... | collective-permute-start | bytes 589832 | tf_op jit(solution)/shard_map/ppermute | solution.py:70
  22.7 16.4 %collective-permute-start.2 = (bf16[256,384]{1,0:T(8,128)(2,1)S(1)}, bf16[256,384]{1,0:T(8,128)(2,1)S(1)}, u32[]{:S(2)}, u32[]{:S(2)}) collective-permute-start(bf16[256,384]{1,0:T(8,128)(2,1)S(1)} %pad_maximum_fusion.refs_0_), channel_id=1, source_target_pairs={{0,2},{1,3},{2,0},{3,1},{4,6},{5,7},{6,4},{7,5},{8,10},{9,11},{10,... | collective-permute-start | bytes 589832 | tf_op jit(solution)/shard_map/ppermute | solution.py:70
  23.5 15.6 %collective-permute-start.1 = (bf16[256,384]{1,0:T(8,128)(2,1)S(1)}, bf16[256,384]{1,0:T(8,128)(2,1)S(1)}, u32[]{:S(2)}, u32[]{:S(2)}) collective-permute-start(bf16[256,384]{1,0:T(8,128)(2,1)S(1)} %pad_maximum_fusion.refs_0_), channel_id=1, source_target_pairs={{0,16},{1,17},{2,18},{3,19},{4,20},{5,21},{6,22},{7,23},{8,24},{9,... | collective-permute-start | bytes 589832 | tf_op jit(solution)/shard_map/ppermute | solution.py:70
  39.2 264.9 %reduce-scatter.2.cloned.1.call-start = ((), (), s32[]{:S(2)}) async-start(), calls=%async_computation.1 | async-start | bytes 6082560 | tf_op jit(solution)/shard_map/reduce_scatter | solution.py:940
  40.0 19.0 %collective-permute-start.8 = (bf16[256,384]{1,0:T(8,128)(2,1)S(1)}, bf16[256,384]{1,0:T(8,128)(2,1)S(1)}, u32[]{:S(2)}, u32[]{:S(2)}) collective-permute-start(bf16[256,384]{1,0:T(8,128)(2,1)S(1)} %pad_maximum_fusion.refs_0_), channel_id=1, source_target_pairs={{0,8},{1,9},{2,10},{3,11},{4,12},{5,13},{6,14},{7,15},{8,0},{9,1},... | collective-permute-start | bytes 589832 | tf_op jit(solution)/shard_map/ppermute | solution.py:70
  40.1 19.4 %collective-permute-start.9 = (bf16[256,384]{1,0:T(8,128)(2,1)S(1)}, bf16[256,384]{1,0:T(8,128)(2,1)S(1)}, u32[]{:S(2)}, u32[]{:S(2)}) collective-permute-start(bf16[256,384]{1,0:T(8,128)(2,1)S(1)} %collective-permute-done.2.refs_1_), channel_id=1, source_target_pairs={{0,8},{1,9},{2,10},{3,11},{4,12},{5,13},{6,14},{7,15},{8,0},{9,1},... | collective-permute-start | bytes 589832 | tf_op jit(solution)/shard_map/ppermute | solution.py:70
  40.6 7.8 %collective-permute-start.5 = (bf16[256,384]{1,0:T(8,128)(2,1)S(1)}, bf16[256,384]{1,0:T(8,128)(2,1)S(1)}, u32[]{:S(2)}, u32[]{:S(2)}) collective-permute-start(bf16[256,384]{1,0:T(8,128)(2,1)S(1)} %collective-permute-done.2.refs_1_), channel_id=1, source_target_pairs={{0,16},{1,17},{2,18},{3,19},{4,20},{5,21},{6,22},{7,23},{8,24},{9,... | collective-permute-start | bytes 589832 | tf_op jit(solution)/shard_map/ppermute | solution.py:70
  42.1 17.6 %collective-permute-start.10 = (bf16[256,384]{1,0:T(8,128)(2,1)S(1)}, bf16[256,384]{1,0:T(8,128)(2,1)S(1)}, u32[]{:S(2)}, u32[]{:S(2)}) collective-permute-start(bf16[256,384]{1,0:T(8,128)(2,1)S(1)} %collective-permute-done.3.refs_2_), channel_id=1, source_target_pairs={{0,8},{1,9},{2,10},{3,11},{4,12},{5,13},{6,14},{7,15},{8,0},{9,1},... | collective-permute-start | bytes 589832 | tf_op jit(solution)/shard_map/ppermute | solution.py:70
  42.1 10.9 %collective-permute-start.6 = (bf16[256,384]{1,0:T(8,128)(2,1)S(1)}, bf16[256,384]{1,0:T(8,128)(2,1)S(1)}, u32[]{:S(2)}, u32[]{:S(2)}) collective-permute-start(bf16[256,384]{1,0:T(8,128)(2,1)S(1)} %collective-permute-done.3.refs_2_), channel_id=1, source_target_pairs={{0,16},{1,17},{2,18},{3,19},{4,20},{5,21},{6,22},{7,23},{8,24},{9,... | collective-permute-start | bytes 589832 | tf_op jit(solution)/shard_map/ppermute | solution.py:70
  48.4 11.9 %collective-permute-start.11 = (bf16[256,384]{1,0:T(8,128)(2,1)S(1)}, bf16[256,384]{1,0:T(8,128)(2,1)S(1)}, u32[]{:S(2)}, u32[]{:S(2)}) collective-permute-start(bf16[256,384]{1,0:T(8,128)(2,1)S(1)} %collective-permute-done.4.refs_3_), channel_id=1, source_target_pairs={{0,8},{1,9},{2,10},{3,11},{4,12},{5,13},{6,14},{7,15},{8,0},{9,1},... | collective-permute-start | bytes 589832 | tf_op jit(solution)/shard_map/ppermute | solution.py:70
  53.0 5.9 %collective-permute-start.7 = (bf16[256,384]{1,0:T(8,128)(2,1)S(1)}, bf16[256,384]{1,0:T(8,128)(2,1)S(1)}, u32[]{:S(2)}, u32[]{:S(2)}) collective-permute-start(bf16[256,384]{1,0:T(8,128)(2,1)S(1)} %collective-permute-done.4.refs_3_), channel_id=1, source_target_pairs={{0,16},{1,17},{2,18},{3,19},{4,20},{5,21},{6,22},{7,23},{8,24},{9,... | collective-permute-start | bytes 589832 | tf_op jit(solution)/shard_map/ppermute | solution.py:70
  59.0 1.7 collective-permute-start.13
  59.6 1.5 collective-permute-start.14
  59.7 1.7 collective-permute-start.15
  267.7 3.6 %collective-permute-start.16 = (bf16[16,128,384]{2,1,0:T(8,128)(2,1)}, bf16[16,128,384]{2,1,0:T(8,128)(2,1)S(1)}, u32[]{:S(2)}, u32[]{:S(2)}) collective-permute-start(bf16[16,128,384]{2,1,0:T(8,128)(2,1)} %get-tuple-element.108), channel_id=1, source_target_pairs={{0,8},{1,9},{2,10},{3,11},{4,12},{5,13},{6,14},{7,15},{8,0},{9,1},... | collective-permute-start | bytes 4718600 | tf_op jit(solution)/shard_map/ppermute | solution.py:70
  276.4 20.1 %collective-permute-start.17 = (bf16[4,128,384]{2,1,0:T(8,128)(2,1)}, bf16[4,128,384]{2,1,0:T(8,128)(2,1)S(1)}, u32[]{:S(2)}, u32[]{:S(2)}) collective-permute-start(bf16[4,128,384]{2,1,0:T(8,128)(2,1)} %get-tuple-element.114), channel_id=1, source_target_pairs={{0,1},{1,0},{2,3},{3,2},{4,5},{5,4},{6,7},{7,6},{8,9},{9,8},{10,11... | collective-permute-start | bytes 1179656 | tf_op jit(solution)/shard_map/ppermute | solution.py:70
  276.5 20.0 %collective-permute-start.18 = (bf16[4,128,384]{2,1,0:T(8,128)(2,1)}, bf16[4,128,384]{2,1,0:T(8,128)(2,1)S(1)}, u32[]{:S(2)}, u32[]{:S(2)}) collective-permute-start(bf16[4,128,384]{2,1,0:T(8,128)(2,1)} %get-tuple-element.115), channel_id=1, source_target_pairs={{0,16},{1,17},{2,18},{3,19},{4,20},{5,21},{6,22},{7,23},{8,24},{9,... | collective-permute-start | bytes 1179656 | tf_op jit(solution)/shard_map/ppermute | solution.py:70
  278.2 20.7 %collective-permute-start.19 = (bf16[4,128,384]{2,1,0:T(8,128)(2,1)}, bf16[4,128,384]{2,1,0:T(8,128)(2,1)S(1)}, u32[]{:S(2)}, u32[]{:S(2)}) collective-permute-start(bf16[4,128,384]{2,1,0:T(8,128)(2,1)} %get-tuple-element.116), channel_id=1, source_target_pairs={{0,17},{1,16},{2,19},{3,18},{4,21},{5,20},{6,23},{7,22},{8,25},{9,... | collective-permute-start | bytes 1179656 | tf_op jit(solution)/shard_map/ppermute | solution.py:70
  299.7 7.5 %collective-permute-start.22 = (bf16[128,384]{1,0:T(8,128)(2,1)S(1)}, bf16[128,384]{1,0:T(8,128)(2,1)S(1)}, u32[]{:S(2)}, u32[]{:S(2)}) collective-permute-start(bf16[128,384]{1,0:T(8,128)(2,1)S(1)} %get-tuple-element.127), channel_id=1, source_target_pairs={{0,6},{1,7},{2,4},{3,5},{4,2},{5,3},{6,0},{7,1},{8,14},{9,15},{10,... | collective-permute-start | bytes 294920 | tf_op jit(solution)/shard_map/ppermute | solution.py:70
  301.8 7.8 %collective-permute-start.20 = (bf16[128,384]{1,0:T(8,128)(2,1)S(1)}, bf16[128,384]{1,0:T(8,128)(2,1)S(1)}, u32[]{:S(2)}, u32[]{:S(2)}) collective-permute-start(bf16[128,384]{1,0:T(8,128)(2,1)S(1)} %get-tuple-element.125), channel_id=1, source_target_pairs={{0,2},{1,3},{2,0},{3,1},{4,6},{5,7},{6,4},{7,5},{8,10},{9,11},{10,... | collective-permute-start | bytes 294920 | tf_op jit(solution)/shard_map/ppermute | solution.py:70
  301.8 7.8 %collective-permute-start.21 = (bf16[128,384]{1,0:T(8,128)(2,1)S(1)}, bf16[128,384]{1,0:T(8,128)(2,1)S(1)}, u32[]{:S(2)}, u32[]{:S(2)}) collective-permute-start(bf16[128,384]{1,0:T(8,128)(2,1)S(1)} %get-tuple-element.126), channel_id=1, source_target_pairs={{0,4},{1,5},{2,6},{3,7},{4,0},{5,1},{6,2},{7,3},{8,12},{9,13},{10,... | collective-permute-start | bytes 294920 | tf_op jit(solution)/shard_map/ppermute | solution.py:70
  (26 other events, 266.9 us)
Sparse Core Ops, SparseCore 0:
  39.3 66.9 all-gather.2
  188.5 113.4 reduce-scatter.1

commit v4 on v3

--- a/solution.py
+++ b/solution.py
@@ -119,25 +119,34 @@
     )(me, *arrays)
 
 
-def finish_kernel(scale, a_ref, b_ref, c_ref, d_ref, in_ref, point_ref, small_ref):
+def finish_kernel(scale, a_ref, b_ref, c_ref, d_ref, in_ref, point_ref, depth_ref, kern_ref, vec_ref):
     total = sum(ref[...].astype(F32) for ref in (a_ref, b_ref, c_ref, d_ref)) * scale
     for n in range(4):
         in_ref[:, n * ATT : (n + 1) * ATT] = total[24 * n : 24 * n + 24]
     point_ref[...] = total[96:120]
-    small_ref[...] = total[120:128]
-
-
-def finish(scale, arrays):
+    at = 0
+    for ref in (depth_ref, kern_ref, vec_ref):
+        count, width = ref.shape
+        for i in range(count):
+            row, lane = 120 + at // LANES, at % LANES
+            here = min(width, LANES - lane)
+            ref[i : i + 1, :here] = total[row : row + 1, lane : lane + here]
+            if here < width:
+                ref[i : i + 1, here:] = total[row + 1 : row + 2, : width - here]
+            at += width
+
+
+def finish(scale, arrays, small_shapes):
     vmem = pl.BlockSpec(memory_space=pltpu.VMEM)
     return pl.pallas_call(
         partial(finish_kernel, scale),
         in_specs=[vmem] * 4,
-        out_specs=[vmem] * 3,
+        out_specs=[vmem] * 5,
         out_shape=[
             jax.ShapeDtypeStruct((24, 4 * ATT), F32),
             jax.ShapeDtypeStruct((24, ATT), F32),
-            jax.ShapeDtypeStruct((8, LANES), F32),
-        ],
+        ]
+        + [jax.ShapeDtypeStruct(shape, F32) for shape in small_shapes],
         name="finish",
     )(*arrays)
 
@@ -961,8 +970,8 @@
         d_out, d_up, d_down = finish_mid(scale, mid_sum)
         d_up = d_up.transpose(0, 2, 1)
         parts[3], d_out = tie(parts[3], d_out)
-        d_in, d_point, small_sum = finish(scale, parts)
-        small_sum = small_sum.reshape(-1)
+        small_shapes = [(KER, own), kernel_weight.shape, (4, own)]
+        d_in, d_point, depth_sum, kern_sum, vec_sum = finish(scale, parts, small_shapes)
     else:
         (grads,) = weight_grad(inputs, dq, dk, dv, dcv, d_point, jnp.zeros((32, 8, LANES), F32))
         d_in = grads[:, :96].reshape(32, 4, 24, ATT).transpose(0, 2, 1, 3).reshape(devices, -1, LANES)
@@ -977,13 +986,14 @@
         d_out, d_in, small_sum = d_out.reshape(own, WIDTH), d_in.reshape(own, 4 * ATT), small_sum.reshape(-1)
         d_up, d_down = d_up.reshape(2, hid, ATT).transpose(0, 2, 1), d_down.reshape(2, hid, ATT)
         d_tokens = leave(dq, dk, dv, dcv, d_rest, mask_col, to_row, w_in)
-    kern_sum = small_sum[n_depth : n_depth + n_kern].reshape(kernel_weight.shape)
-    vec_sum = small_sum[n_depth + n_kern :][:n_vec].reshape(4, own)
+        depth_sum = small_sum[:n_depth].reshape(KER, own)
+        kern_sum = small_sum[n_depth : n_depth + n_kern].reshape(kernel_weight.shape)
+        vec_sum = small_sum[n_depth + n_kern :][:n_vec].reshape(4, own)
     return (
         out,
         d_tokens,
         d_in,
-        small_sum[:n_depth].reshape(KER, own),
+        depth_sum,
         d_point,
         kern_sum,
         d_out,

time: 329 us -> 327 us (level)
  no operation moved by 1% of the time
where the time goes in v4:
time: 327 us; the launch traced here: 321 us
  Pallas kernels  227 us (69%)
  waiting for transfers between devices  30.4 us (9%)
  starting transfers between devices  22.5 us (7%)
  local copies, waits for them, and re-layouts  21.3 us (7%)
  between operations  15.1 us (5%)
  other arithmetic  5.42 us (2%)
    pallas_call x1, Pallas kernels, middle(): pl.pallas_call(middle_kernel, grid=(rows // MID,), in_specs=[block(ATT),...  75.4 us
    pallas_call x1, Pallas kernels, conv_back(): pl.pallas_call(conv_back_kernel, grid=(rows // SEQ,), in_specs=[at(1), bl...  35.8 us
    ppermute x23, waiting for transfers between devices, hop(): return lax.ppermute(x, AXES, [(i, i ^ mask) for i in range(32)])  30.4 us
    pallas_call x1, Pallas kernels, attend_back(): pl.pallas_call(attend_back_kernel, grid=(rows // SEQ, pairs), in_specs=[c...  25.5 us
    pallas_call x1, Pallas kernels, enter(): pl.pallas_call(enter_slabs_kernel, grid=(rows // SEQ,), in_specs=[pl.Bloc...  23.6 us
    pallas_call x1, Pallas kernels, attend(): pl.pallas_call(attend_kernel, grid=(rows // SEQ, pairs), in_specs=[col(0)...  23.1 us
    ppermute x23, starting transfers between devices, hop(): return lax.ppermute(x, AXES, [(i, i ^ mask) for i in range(32)])  22.4 us
    pallas_call x1, Pallas kernels, leave(): pl.pallas_call(leave_kernel, grid=(rows // SEQ, 2 * STEPS), in_specs=[blo...  16.6 us
  transfers between devices with their start and end apart: 25, of which 12 were waited for; matrix products, arithmetic and copies ran while one was open for 5% of the time, Pallas kernels for 46%

profile of v4, /device:TPU:0, one launch (start us, length us, event | category | flops | bytes accessed | tf_op | source)
XLA Modules:
  0.0 321.4 jit_solution(11213795955379549552)
XLA Ops:
  11.4 3.0 collective-permute-start
  19.1 3.7 %collective-permute-start.4 = (bf16[256,384]{1,0:T(8,128)(2,1)S(1)}, bf16[256,384]{1,0:T(8,128)(2,1)S(1)}, u32[]{:S(2)}, u32[]{:S(2)}) collective-permute-start(bf16[256,384]{1,0:T(8,128)(2,1)S(1)} %pad_maximum_fusion.refs_0_), channel_id=1, source_target_pairs={{0,6},{1,7},{2,4},{3,5},{4,2},{5,3},{6,0},{7,1},{8,14},{9,15},{10,... | collective-permute-start | bytes 589832 | tf_op jit(solution)/shard_map/ppermute | solution.py:70
  26.4 6.5 %pick.1.inp_ref = bf16[2048,768]{1,0:T(8,128)(2,1)} custom-call(s32[2048,1]{1,0:T(8,128)} %copy.34.pick_ref, bf16[2048,768]{1,0:T(8,128)(2,1)} %tok_ref.1), custom_call_target="tpu_custom_call" | custom-call | flops 6000000000 | bytes 6000000 | tf_op jit(solution)/shard_map/pick/pallas_call | solution.py:223
  32.8 6.3 %collective-permute-done.3.refs_2_ = bf16[256,384]{1,0:T(8,128)(2,1)S(1)} collective-permute-done((bf16[256,384]{1,0:T(8,128)(2,1)S(1)}, bf16[256,384]{1,0:T(8,128)(2,1)S(1)}, u32[]{:S(2)}, u32[]{:S(2)}) %collective-permute-start.3) | collective-permute-done | bytes 196640 | tf_op jit(solution)/shard_map/ppermute | solution.py:70
  42.7 5.7 %collective-permute-done.5.refs_5_ = bf16[256,384]{1,0:T(8,128)(2,1)S(1)} collective-permute-done((bf16[256,384]{1,0:T(8,128)(2,1)S(1)}, bf16[256,384]{1,0:T(8,128)(2,1)S(1)}, u32[]{:S(2)}, u32[]{:S(2)}) %collective-permute-start.5) | collective-permute-done | bytes 196640 | tf_op jit(solution)/shard_map/ppermute | solution.py:70
  48.4 4.7 %collective-permute-done.6.refs_6_ = bf16[256,384]{1,0:T(8,128)(2,1)S(1)} collective-permute-done((bf16[256,384]{1,0:T(8,128)(2,1)S(1)}, bf16[256,384]{1,0:T(8,128)(2,1)S(1)}, u32[]{:S(2)}, u32[]{:S(2)}) %collective-permute-start.6) | collective-permute-done | bytes 196640 | tf_op jit(solution)/shard_map/ppermute | solution.py:70
  54.5 4.4 %collective-permute-done.7.refs_7_ = bf16[256,384]{1,0:T(8,128)(2,1)S(1)} collective-permute-done((bf16[256,384]{1,0:T(8,128)(2,1)S(1)}, bf16[256,384]{1,0:T(8,128)(2,1)S(1)}, u32[]{:S(2)}, u32[]{:S(2)}) %collective-permute-start.7) | collective-permute-done | bytes 196640 | tf_op jit(solution)/shard_map/ppermute | solution.py:70
  66.2 23.6 %enter.1 = (bf16[2048,1536]{1,0:T(8,128)(2,1)}, bf16[2048,768]{1,0:T(8,128)(2,1)}, bf16[2048,384]{1,0:T(8,128)(2,1)}, f32[2048,128]{1,0:T(8,128)}, bf16[2048,384...) custom-call(s32[1]{0:T(128)} %select_n.107.pair_ref, bf16[2048,768]{1,0:T(8,128)(2,1)} %pick.1.inp_ref, ...), custom_call_target="tpu_custom_call" | custom-call | flops 20000000000 | bytes 20000000 | tf_op jit(solution)/shard_map/enter/pallas_call | solution.py:321
  89.8 23.1 %attend.1 = (bf16[2,6,1024,1024]{3,2,1,0:T(8,128)(2,1)}, bf16[2048,384]{1,0:T(8,128)(2,1)}, f32[2048,384]{1,0:T(8,128)}) custom-call(bf16[2048,1536]{1,0:T(8,128)(2,1)} %get-tuple-element.87.q_ref.k_ref.v_ref.cv_ref, bf16[2048,1536]{1,0:T(8,128)(2,1)} %get-tuple-element.87.q_ref.k_ref.v_ref.cv_ref, bf16[2048,1536]{1,0:T(8,128)(2,1)} %get-tuple-element.87.q_ref.k_ref.v_ref.cv_ref), custom_call_target="tpu_custom_call" | custom-call | flops 24999999488 | bytes 35000000 | tf_op jit(solution)/shard_map/attend/pallas_call | solution.py:378
  112.9 75.4 %middle.1 = (bf16[2048,768]{1,0:T(8,128)(2,1)}, bf16[2048,768]{1,0:T(8,128)(2,1)}, f32[2048,768]{1,0:T(8,128)}, f32[4,768]{1,0:T(4,128)}, bf16[32,240,384]{2,1,0:T(8,128)(2,1)}) custom-call(bf16[2048,384]{1,0:T(8,128)(2,1)} %get-tuple-element.88.att_ref.o_ref, bf16[2048,384]{1,0:T(8,128)(2,1)} %get-tuple-element.89.conv_ref, bf16[2048,768]{1,0:T(8,128)(2,1)} %pick.1.inp_ref, ...), custom_call_target="tpu_custom_call" | custom-call | flops 60000002048 | bytes 40000000 | tf_op jit(solution)/shard_map/middle/pallas_call | solution.py:550
  189.3 35.8 %conv_back.1 = (f32[2048,384]{1,0:T(8,128)}, bf16[2048,384]{1,0:T(8,128)(2,1)}, f32[2048,768]{1,0:T(8,128)}, f32[768,384]{1,0:T(8,128)}, f32[384,128]{1,0:T(8,128)}, /*index=5*/f32[9,768]{1,0:T(8,128)}) custom-call(bf16[2048,768]{1,0:T(8,128)(2,1)} %get-tuple-element.94.dconv_ref.datt_ref, f32[2048,128]{1,0:T(8,128)} %get-tuple-element.95.kern_ref, ...), custom_call_target="tpu_custom_call" | custom-call | flops 24999999488 | bytes 30000000 | tf_op jit(solution)/shard_map/conv_back/pallas_call | solution.py:690
  229.6 25.5 %attend_back.1 = (bf16[2048,384]{1,0:T(8,128)(2,1)}, bf16[2048,384]{1,0:T(8,128)(2,1)}, bf16[2048,384]{1,0:T(8,128)(2,1)}) custom-call(bf16[2048,1536]{1,0:T(8,128)(2,1)} %get-tuple-element.87.q_ref.k_ref.v_ref.cv_ref, bf16[2048,1536]{1,0:T(8,128)(2,1)} %get-tuple-element.87.q_ref.k_ref.v_ref.cv_ref, ...), custom_call_target="tpu_custom_call" | custom-call | flops 30000001024 | bytes 40000000 | tf_op jit(solution)/shard_map/attend_back/pallas_call | solution.py:754
  255.0 12.7 %weight_grad.1 = (bf16[16,128,384]{2,1,0:T(8,128)(2,1)}, bf16[16,128,384]{2,1,0:T(8,128)(2,1)}) custom-call(s32[1]{0:T(128)S(6)} %select_n.123.core_ref, bf16[2048,768]{1,0:T(8,128)(2,1)} %pick.1.inp_ref, bf16[2048,384]{1,0:T(8,128)(2,1)} %get-tuple-element.112.dq_ref, bf16[2048,384]{1,0:T(8,128)(2,1)} %get-tuple-element.102.dk_ref, ...), custom_call_target="tpu_custom_call" | custom-call | flops 12000000000 | bytes 12000000 | tf_op jit(solution)/shard_map/weight_grad/pallas_call | solution.py:808
  269.4 2.0 collective-permute-done.16
  272.5 3.9 %fold_xy.1 = (bf16[4,128,384]{2,1,0:T(8,128)(2,1)}, bf16[4,128,384]{2,1,0:T(8,128)(2,1)}, bf16[4,128,384]{2,1,0:T(8,128)(2,1)}, bf16[4,128,384]{2,1,0:T(8,128)(2,1)}) custom-call(s32[1]{0:T(128)} %bitcast.me_ref, bf16[2,4,2,128,384]{4,3,2,1,0:T(8,128)(2,1)} %bitcast.122, bf16[2,4,2,128,384]{4,3,2,1,0:T(8,128)(2,1)} %bitcast.123), custom_call_target="tpu_custom_call" | custom-call | bytes 4718592 | tf_op jit(solution)/shard_map/fold_xy/pallas_call | solution.py:87
  276.5 1.7 collective-permute-start.18
  278.2 1.7 collective-permute-start.19
  279.9 16.6 %leave.1 = f32[2048,768]{1,0:T(8,128)} custom-call(bf16[2048,384]{1,0:T(8,128)(2,1)} %get-tuple-element.112.dq_ref, bf16[2048,384]{1,0:T(8,128)(2,1)} %get-tuple-element.102.dk_ref, bf16[2048,384]{1,0:T(8,128)(2,1)} %get-tuple-element.103.dv_ref, bf16[2048,384]{1,0:T(8,128)(2,1)} %get-tuple-element.104.dcv_ref, f32[2048,768]{1,0:T(8,128)} %get-tuple-element.113.rest_ref, ...), custom_call_target="tpu_custom_call" | custom-call | flops 15000000512 | bytes 30000000 | tf_op jit(solution)/shard_map/leave/pallas_call | solution.py:850
  296.5 2.4 collective-permute-done.19.refs_3_
  299.7 2.1 collective-permute-start.22
  301.8 2.3 collective-permute-start.21
  304.1 1.7 finish_mid.1
  307.2 2.4 collective-permute-done.20.b_ref
  310.9 1.8 finish.1
  (168 shorter events, 37.5 us)
Async XLA Ops:
  7.2 105.8 %all-gather.3.cloned.1.call-start = ((), (), s32[]{:S(2)}) async-start(), calls=%async_computation.2 | async-start | bytes 6082560 | tf_op jit(solution)/shard_map/all_gather | solution.py:923
  11.4 7.5 %collective-permute-start = (bf16[128,384]{1,0:T(8,128)(2,1)S(1)}, bf16[128,384]{1,0:T(8,128)(2,1)S(1)}, u32[]{:S(2)}, u32[]{:S(2)}) collective-permute-start(bf16[128,384]{1,0:T(8,128)(2,1)S(1)} %pad_maximum_fusion.3), channel_id=1, source_target_pairs={{0,1},{1,0},{2,3},{3,2},{4,5},{5,4},{6,7},{7,6},{8,9},{9,8},{10,11... | collective-permute-start | bytes 294920 | tf_op jit(solution)/shard_map/ppermute | solution.py:70
  19.1 13.8 %collective-permute-start.4 = (bf16[256,384]{1,0:T(8,128)(2,1)S(1)}, bf16[256,384]{1,0:T(8,128)(2,1)S(1)}, u32[]{:S(2)}, u32[]{:S(2)}) collective-permute-start(bf16[256,384]{1,0:T(8,128)(2,1)S(1)} %pad_maximum_fusion.refs_0_), channel_id=1, source_target_pairs={{0,6},{1,7},{2,4},{3,5},{4,2},{5,3},{6,0},{7,1},{8,14},{9,15},{10,... | collective-permute-start | bytes 589832 | tf_op jit(solution)/shard_map/ppermute | solution.py:70
  22.7 16.4 %collective-permute-start.3 = (bf16[256,384]{1,0:T(8,128)(2,1)S(1)}, bf16[256,384]{1,0:T(8,128)(2,1)S(1)}, u32[]{:S(2)}, u32[]{:S(2)}) collective-permute-start(bf16[256,384]{1,0:T(8,128)(2,1)S(1)} %pad_maximum_fusion.refs_0_), channel_id=1, source_target_pairs={{0,4},{1,5},{2,6},{3,7},{4,0},{5,1},{6,2},{7,3},{8,12},{9,13},{10,... | collective-permute-start | bytes 589832 | tf_op jit(solution)/shard_map/ppermute | solution.py:70
  22.7 16.4 %collective-permute-start.2 = (bf16[256,384]{1,0:T(8,128)(2,1)S(1)}, bf16[256,384]{1,0:T(8,128)(2,1)S(1)}, u32[]{:S(2)}, u32[]{:S(2)}) collective-permute-start(bf16[256,384]{1,0:T(8,128)(2,1)S(1)} %pad_maximum_fusion.refs_0_), channel_id=1, source_target_pairs={{0,2},{1,3},{2,0},{3,1},{4,6},{5,7},{6,4},{7,5},{8,10},{9,11},{10,... | collective-permute-start | bytes 589832 | tf_op jit(solution)/shard_map/ppermute | solution.py:70
  23.5 15.6 %collective-permute-start.1 = (bf16[256,384]{1,0:T(8,128)(2,1)S(1)}, bf16[256,384]{1,0:T(8,128)(2,1)S(1)}, u32[]{:S(2)}, u32[]{:S(2)}) collective-permute-start(bf16[256,384]{1,0:T(8,128)(2,1)S(1)} %pad_maximum_fusion.refs_0_), channel_id=1, source_target_pairs={{0,16},{1,17},{2,18},{3,19},{4,20},{5,21},{6,22},{7,23},{8,24},{9,... | collective-permute-start | bytes 589832 | tf_op jit(solution)/shard_map/ppermute | solution.py:70
  39.2 264.9 %reduce-scatter.2.cloned.1.call-start = ((), (), s32[]{:S(2)}) async-start(), calls=%async_computation.1 | async-start | bytes 6082560 | tf_op jit(solution)/shard_map/reduce_scatter | solution.py:949
  40.0 19.0 %collective-permute-start.8 = (bf16[256,384]{1,0:T(8,128)(2,1)S(1)}, bf16[256,384]{1,0:T(8,128)(2,1)S(1)}, u32[]{:S(2)}, u32[]{:S(2)}) collective-permute-start(bf16[256,384]{1,0:T(8,128)(2,1)S(1)} %pad_maximum_fusion.refs_0_), channel_id=1, source_target_pairs={{0,8},{1,9},{2,10},{3,11},{4,12},{5,13},{6,14},{7,15},{8,0},{9,1},... | collective-permute-start | bytes 589832 | tf_op jit(solution)/shard_map/ppermute | solution.py:70
  40.1 19.4 %collective-permute-start.9 = (bf16[256,384]{1,0:T(8,128)(2,1)S(1)}, bf16[256,384]{1,0:T(8,128)(2,1)S(1)}, u32[]{:S(2)}, u32[]{:S(2)}) collective-permute-start(bf16[256,384]{1,0:T(8,128)(2,1)S(1)} %collective-permute-done.2.refs_1_), channel_id=1, source_target_pairs={{0,8},{1,9},{2,10},{3,11},{4,12},{5,13},{6,14},{7,15},{8,0},{9,1},... | collective-permute-start | bytes 589832 | tf_op jit(solution)/shard_map/ppermute | solution.py:70
  40.6 7.8 %collective-permute-start.5 = (bf16[256,384]{1,0:T(8,128)(2,1)S(1)}, bf16[256,384]{1,0:T(8,128)(2,1)S(1)}, u32[]{:S(2)}, u32[]{:S(2)}) collective-permute-start(bf16[256,384]{1,0:T(8,128)(2,1)S(1)} %collective-permute-done.2.refs_1_), channel_id=1, source_target_pairs={{0,16},{1,17},{2,18},{3,19},{4,20},{5,21},{6,22},{7,23},{8,24},{9,... | collective-permute-start | bytes 589832 | tf_op jit(solution)/shard_map/ppermute | solution.py:70
  42.1 17.6 %collective-permute-start.10 = (bf16[256,384]{1,0:T(8,128)(2,1)S(1)}, bf16[256,384]{1,0:T(8,128)(2,1)S(1)}, u32[]{:S(2)}, u32[]{:S(2)}) collective-permute-start(bf16[256,384]{1,0:T(8,128)(2,1)S(1)} %collective-permute-done.3.refs_2_), channel_id=1, source_target_pairs={{0,8},{1,9},{2,10},{3,11},{4,12},{5,13},{6,14},{7,15},{8,0},{9,1},... | collective-permute-start | bytes 589832 | tf_op jit(solution)/shard_map/ppermute | solution.py:70
  42.1 10.9 %collective-permute-start.6 = (bf16[256,384]{1,0:T(8,128)(2,1)S(1)}, bf16[256,384]{1,0:T(8,128)(2,1)S(1)}, u32[]{:S(2)}, u32[]{:S(2)}) collective-permute-start(bf16[256,384]{1,0:T(8,128)(2,1)S(1)} %collective-permute-done.3.refs_2_), channel_id=1, source_target_pairs={{0,16},{1,17},{2,18},{3,19},{4,20},{5,21},{6,22},{7,23},{8,24},{9,... | collective-permute-start | bytes 589832 | tf_op jit(solution)/shard_map/ppermute | solution.py:70
  48.4 11.9 %collective-permute-start.11 = (bf16[256,384]{1,0:T(8,128)(2,1)S(1)}, bf16[256,384]{1,0:T(8,128)(2,1)S(1)}, u32[]{:S(2)}, u32[]{:S(2)}) collective-permute-start(bf16[256,384]{1,0:T(8,128)(2,1)S(1)} %collective-permute-done.4.refs_3_), channel_id=1, source_target_pairs={{0,8},{1,9},{2,10},{3,11},{4,12},{5,13},{6,14},{7,15},{8,0},{9,1},... | collective-permute-start | bytes 589832 | tf_op jit(solution)/shard_map/ppermute | solution.py:70
  53.0 5.9 %collective-permute-start.7 = (bf16[256,384]{1,0:T(8,128)(2,1)S(1)}, bf16[256,384]{1,0:T(8,128)(2,1)S(1)}, u32[]{:S(2)}, u32[]{:S(2)}) collective-permute-start(bf16[256,384]{1,0:T(8,128)(2,1)S(1)} %collective-permute-done.4.refs_3_), channel_id=1, source_target_pairs={{0,16},{1,17},{2,18},{3,19},{4,20},{5,21},{6,22},{7,23},{8,24},{9,... | collective-permute-start | bytes 589832 | tf_op jit(solution)/shard_map/ppermute | solution.py:70
  59.0 1.7 collective-permute-start.13
  59.6 1.5 collective-permute-start.14
  59.7 1.7 collective-permute-start.15
  267.7 3.6 %collective-permute-start.16 = (bf16[16,128,384]{2,1,0:T(8,128)(2,1)}, bf16[16,128,384]{2,1,0:T(8,128)(2,1)S(1)}, u32[]{:S(2)}, u32[]{:S(2)}) collective-permute-start(bf16[16,128,384]{2,1,0:T(8,128)(2,1)} %get-tuple-element.110), channel_id=1, source_target_pairs={{0,8},{1,9},{2,10},{3,11},{4,12},{5,13},{6,14},{7,15},{8,0},{9,1},... | collective-permute-start | bytes 4718600 | tf_op jit(solution)/shard_map/ppermute | solution.py:70
  276.4 20.1 %collective-permute-start.17 = (bf16[4,128,384]{2,1,0:T(8,128)(2,1)}, bf16[4,128,384]{2,1,0:T(8,128)(2,1)S(1)}, u32[]{:S(2)}, u32[]{:S(2)}) collective-permute-start(bf16[4,128,384]{2,1,0:T(8,128)(2,1)} %get-tuple-element.116), channel_id=1, source_target_pairs={{0,1},{1,0},{2,3},{3,2},{4,5},{5,4},{6,7},{7,6},{8,9},{9,8},{10,11... | collective-permute-start | bytes 1179656 | tf_op jit(solution)/shard_map/ppermute | solution.py:70
  276.5 20.0 %collective-permute-start.18 = (bf16[4,128,384]{2,1,0:T(8,128)(2,1)}, bf16[4,128,384]{2,1,0:T(8,128)(2,1)S(1)}, u32[]{:S(2)}, u32[]{:S(2)}) collective-permute-start(bf16[4,128,384]{2,1,0:T(8,128)(2,1)} %get-tuple-element.117), channel_id=1, source_target_pairs={{0,16},{1,17},{2,18},{3,19},{4,20},{5,21},{6,22},{7,23},{8,24},{9,... | collective-permute-start | bytes 1179656 | tf_op jit(solution)/shard_map/ppermute | solution.py:70
  278.2 20.7 %collective-permute-start.19 = (bf16[4,128,384]{2,1,0:T(8,128)(2,1)}, bf16[4,128,384]{2,1,0:T(8,128)(2,1)S(1)}, u32[]{:S(2)}, u32[]{:S(2)}) collective-permute-start(bf16[4,128,384]{2,1,0:T(8,128)(2,1)} %get-tuple-element.118), channel_id=1, source_target_pairs={{0,17},{1,16},{2,19},{3,18},{4,21},{5,20},{6,23},{7,22},{8,25},{9,... | collective-permute-start | bytes 1179656 | tf_op jit(solution)/shard_map/ppermute | solution.py:70
  299.7 7.5 %collective-permute-start.22 = (bf16[128,384]{1,0:T(8,128)(2,1)S(1)}, bf16[128,384]{1,0:T(8,128)(2,1)S(1)}, u32[]{:S(2)}, u32[]{:S(2)}) collective-permute-start(bf16[128,384]{1,0:T(8,128)(2,1)S(1)} %get-tuple-element.129), channel_id=1, source_target_pairs={{0,6},{1,7},{2,4},{3,5},{4,2},{5,3},{6,0},{7,1},{8,14},{9,15},{10,... | collective-permute-start | bytes 294920 | tf_op jit(solution)/shard_map/ppermute | solution.py:70
  301.8 7.8 %collective-permute-start.20 = (bf16[128,384]{1,0:T(8,128)(2,1)S(1)}, bf16[128,384]{1,0:T(8,128)(2,1)S(1)}, u32[]{:S(2)}, u32[]{:S(2)}) collective-permute-start(bf16[128,384]{1,0:T(8,128)(2,1)S(1)} %get-tuple-element.127), channel_id=1, source_target_pairs={{0,2},{1,3},{2,0},{3,1},{4,6},{5,7},{6,4},{7,5},{8,10},{9,11},{10,... | collective-permute-start | bytes 294920 | tf_op jit(solution)/shard_map/ppermute | solution.py:70
  301.8 7.8 %collective-permute-start.21 = (bf16[128,384]{1,0:T(8,128)(2,1)S(1)}, bf16[128,384]{1,0:T(8,128)(2,1)S(1)}, u32[]{:S(2)}, u32[]{:S(2)}) collective-permute-start(bf16[128,384]{1,0:T(8,128)(2,1)S(1)} %get-tuple-element.128), channel_id=1, source_target_pairs={{0,4},{1,5},{2,6},{3,7},{4,0},{5,1},{6,2},{7,3},{8,12},{9,13},{10,... | collective-permute-start | bytes 294920 | tf_op jit(solution)/shard_map/ppermute | solution.py:70
  (26 other events, 266.9 us)
Sparse Core Ops, SparseCore 0:
  39.3 66.9 all-gather.2
  188.5 113.4 reduce-scatter.1

commit v5 on v4

--- a/solution.py
+++ b/solution.py
@@ -665,7 +665,7 @@
             low_part = pltpu.roll(low_part, (DB + 16) - 4, 0)
             high_part = pltpu.roll(high_part, 4, 0)
             taps = (low_part + mid_part + high_part)[8 : 8 + DB]
-            din_ref[rows, lanes] = taps + first_ref[rows, lanes]
+            din_ref[rows, lanes] = (taps + first_ref[rows, lanes]).astype(BF)
             xs = x_pad[pl.ds(r + 8, DB), lanes]
             far_low = [pltpu.roll(shifted[s], (DB + 16) - 4, 0) for s in range(4)]
             far_high = pltpu.roll(dsh, 4, 0)
@@ -701,7 +701,7 @@
         out_shape=[
             jax.ShapeDtypeStruct((rows, ATT), F32),
             jax.ShapeDtypeStruct((rows, ATT), BF),
-            jax.ShapeDtypeStruct((rows, WIDTH), F32),
+            jax.ShapeDtypeStruct((rows, WIDTH), BF),
             jax.ShapeDtypeStruct((WIDTH, ATT), F32),
             jax.ShapeDtypeStruct((ATT, 128), F32),
             jax.ShapeDtypeStruct((KER, WIDTH), F32),
@@ -833,7 +833,7 @@
     @pl.when(step < STEPS)
     def _():
         d_proj = jnp.concatenate([dq_ref[...], dk_ref[...], dv_ref[...], dcv_ref[...]], 1)
-        total = mm_nt(d_proj, w_in_ref[...]) + rest_ref[...]
+        total = mm_nt(d_proj, w_in_ref[...]) + rest_ref[...].astype(F32)
         moved[rows, :] = total.astype(BF)
         kept[rows, :] = jnp.where(mask_ref[...] == 1, 0.0, total)
 

time: 327 us -> 326 us (level)
  no operation moved by 1% of the time
where the time goes in v5:
time: 326 us; the launch traced here: 321 us
  Pallas kernels  226 us (69%)
  waiting for transfers between devices  30.9 us (9%)
  starting transfers between devices  22.6 us (7%)
  local copies, waits for them, and re-layouts  21.3 us (7%)
  between operations  15.1 us (5%)
  other arithmetic  5.42 us (2%)
    pallas_call x1, Pallas kernels, middle(): pl.pallas_call(middle_kernel, grid=(rows // MID,), in_specs=[block(ATT),...  75.5 us
    pallas_call x1, Pallas kernels, conv_back(): pl.pallas_call(conv_back_kernel, grid=(rows // SEQ,), in_specs=[at(1), bl...  35.5 us
    ppermute x23, waiting for transfers between devices, hop(): return lax.ppermute(x, AXES, [(i, i ^ mask) for i in range(32)])  30.8 us
    pallas_call x1, Pallas kernels, attend_back(): pl.pallas_call(attend_back_kernel, grid=(rows // SEQ, pairs), in_specs=[c...  25.5 us
    pallas_call x1, Pallas kernels, enter(): pl.pallas_call(enter_slabs_kernel, grid=(rows // SEQ,), in_specs=[pl.Bloc...  23.6 us
    pallas_call x1, Pallas kernels, attend(): pl.pallas_call(attend_kernel, grid=(rows // SEQ, pairs), in_specs=[col(0)...  23.1 us
    ppermute x23, starting transfers between devices, hop(): return lax.ppermute(x, AXES, [(i, i ^ mask) for i in range(32)])  22.5 us
    pallas_call x1, Pallas kernels, leave(): pl.pallas_call(leave_kernel, grid=(rows // SEQ, 2 * STEPS), in_specs=[blo...  16.2 us
  transfers between devices with their start and end apart: 25, of which 12 were waited for; matrix products, arithmetic and copies ran while one was open for 5% of the time, Pallas kernels for 46%

profile of v5, /device:TPU:0, one launch (start us, length us, event | category | flops | bytes accessed | tf_op | source)
XLA Modules:
  0.0 321.2 jit_solution(11381347468555489040)
XLA Ops:
  11.4 3.0 collective-permute-start
  19.1 3.7 %collective-permute-start.4 = (bf16[256,384]{1,0:T(8,128)(2,1)S(1)}, bf16[256,384]{1,0:T(8,128)(2,1)S(1)}, u32[]{:S(2)}, u32[]{:S(2)}) collective-permute-start(bf16[256,384]{1,0:T(8,128)(2,1)S(1)} %pad_maximum_fusion.refs_0_), channel_id=1, source_target_pairs={{0,6},{1,7},{2,4},{3,5},{4,2},{5,3},{6,0},{7,1},{8,14},{9,15},{10,... | collective-permute-start | bytes 589832 | tf_op jit(solution)/shard_map/ppermute | solution.py:70
  26.4 6.5 %pick.1.inp_ref = bf16[2048,768]{1,0:T(8,128)(2,1)} custom-call(s32[2048,1]{1,0:T(8,128)} %copy.34.pick_ref, bf16[2048,768]{1,0:T(8,128)(2,1)} %tok_ref.1), custom_call_target="tpu_custom_call" | custom-call | flops 6000000000 | bytes 6000000 | tf_op jit(solution)/shard_map/pick/pallas_call | solution.py:223
  32.8 6.3 %collective-permute-done.3.refs_2_ = bf16[256,384]{1,0:T(8,128)(2,1)S(1)} collective-permute-done((bf16[256,384]{1,0:T(8,128)(2,1)S(1)}, bf16[256,384]{1,0:T(8,128)(2,1)S(1)}, u32[]{:S(2)}, u32[]{:S(2)}) %collective-permute-start.3) | collective-permute-done | bytes 196640 | tf_op jit(solution)/shard_map/ppermute | solution.py:70
  42.7 5.7 %collective-permute-done.5.refs_5_ = bf16[256,384]{1,0:T(8,128)(2,1)S(1)} collective-permute-done((bf16[256,384]{1,0:T(8,128)(2,1)S(1)}, bf16[256,384]{1,0:T(8,128)(2,1)S(1)}, u32[]{:S(2)}, u32[]{:S(2)}) %collective-permute-start.5) | collective-permute-done | bytes 196640 | tf_op jit(solution)/shard_map/ppermute | solution.py:70
  48.4 4.7 %collective-permute-done.6.refs_6_ = bf16[256,384]{1,0:T(8,128)(2,1)S(1)} collective-permute-done((bf16[256,384]{1,0:T(8,128)(2,1)S(1)}, bf16[256,384]{1,0:T(8,128)(2,1)S(1)}, u32[]{:S(2)}, u32[]{:S(2)}) %collective-permute-start.6) | collective-permute-done | bytes 196640 | tf_op jit(solution)/shard_map/ppermute | solution.py:70
  54.5 4.4 %collective-permute-done.7.refs_7_ = bf16[256,384]{1,0:T(8,128)(2,1)S(1)} collective-permute-done((bf16[256,384]{1,0:T(8,128)(2,1)S(1)}, bf16[256,384]{1,0:T(8,128)(2,1)S(1)}, u32[]{:S(2)}, u32[]{:S(2)}) %collective-permute-start.7) | collective-permute-done | bytes 196640 | tf_op jit(solution)/shard_map/ppermute | solution.py:70
  66.2 23.6 %enter.1 = (bf16[2048,1536]{1,0:T(8,128)(2,1)}, bf16[2048,768]{1,0:T(8,128)(2,1)}, bf16[2048,384]{1,0:T(8,128)(2,1)}, f32[2048,128]{1,0:T(8,128)}, bf16[2048,384...) custom-call(s32[1]{0:T(128)} %select_n.107.pair_ref, bf16[2048,768]{1,0:T(8,128)(2,1)} %pick.1.inp_ref, ...), custom_call_target="tpu_custom_call" | custom-call | flops 20000000000 | bytes 20000000 | tf_op jit(solution)/shard_map/enter/pallas_call | solution.py:321
  89.8 23.1 %attend.1 = (bf16[2,6,1024,1024]{3,2,1,0:T(8,128)(2,1)}, bf16[2048,384]{1,0:T(8,128)(2,1)}, f32[2048,384]{1,0:T(8,128)}) custom-call(bf16[2048,1536]{1,0:T(8,128)(2,1)} %get-tuple-element.87.q_ref.k_ref.v_ref.cv_ref, bf16[2048,1536]{1,0:T(8,128)(2,1)} %get-tuple-element.87.q_ref.k_ref.v_ref.cv_ref, bf16[2048,1536]{1,0:T(8,128)(2,1)} %get-tuple-element.87.q_ref.k_ref.v_ref.cv_ref), custom_call_target="tpu_custom_call" | custom-call | flops 24999999488 | bytes 35000000 | tf_op jit(solution)/shard_map/attend/pallas_call | solution.py:378
  112.9 75.5 %middle.1 = (bf16[2048,768]{1,0:T(8,128)(2,1)}, bf16[2048,768]{1,0:T(8,128)(2,1)}, f32[2048,768]{1,0:T(8,128)}, f32[4,768]{1,0:T(4,128)}, bf16[32,240,384]{2,1,0:T(8,128)(2,1)}) custom-call(bf16[2048,384]{1,0:T(8,128)(2,1)} %get-tuple-element.88.att_ref.o_ref, bf16[2048,384]{1,0:T(8,128)(2,1)} %get-tuple-element.89.conv_ref, bf16[2048,768]{1,0:T(8,128)(2,1)} %pick.1.inp_ref, ...), custom_call_target="tpu_custom_call" | custom-call | flops 60000002048 | bytes 40000000 | tf_op jit(solution)/shard_map/middle/pallas_call | solution.py:550
  189.3 35.5 %conv_back.1 = (f32[2048,384]{1,0:T(8,128)}, bf16[2048,384]{1,0:T(8,128)(2,1)}, bf16[2048,768]{1,0:T(8,128)(2,1)}, f32[768,384]{1,0:T(8,128)}, f32[384,128]{1,0:T(8,128)}, /*index=5*/f32[9,768]{1,0:T(8,128)}) custom-call(bf16[2048,768]{1,0:T(8,128)(2,1)} %get-tuple-element.94.dconv_ref.datt_ref, f32[2048,128]{1,0:T(8,128)} %get-tuple-element.95.kern_ref, ...), custom_call_target="tpu_custom_call" | custom-call | flops 24999999488 | bytes 30000000 | tf_op jit(solution)/shard_map/conv_back/pallas_call | solution.py:690
  229.3 25.5 %attend_back.1 = (bf16[2048,384]{1,0:T(8,128)(2,1)}, bf16[2048,384]{1,0:T(8,128)(2,1)}, bf16[2048,384]{1,0:T(8,128)(2,1)}) custom-call(bf16[2048,1536]{1,0:T(8,128)(2,1)} %get-tuple-element.87.q_ref.k_ref.v_ref.cv_ref, bf16[2048,1536]{1,0:T(8,128)(2,1)} %get-tuple-element.87.q_ref.k_ref.v_ref.cv_ref, ...), custom_call_target="tpu_custom_call" | custom-call | flops 30000001024 | bytes 40000000 | tf_op jit(solution)/shard_map/attend_back/pallas_call | solution.py:754
  254.7 12.6 %weight_grad.1 = (bf16[16,128,384]{2,1,0:T(8,128)(2,1)}, bf16[16,128,384]{2,1,0:T(8,128)(2,1)}) custom-call(s32[1]{0:T(128)S(6)} %select_n.123.core_ref, bf16[2048,768]{1,0:T(8,128)(2,1)} %pick.1.inp_ref, bf16[2048,384]{1,0:T(8,128)(2,1)} %get-tuple-element.112.dq_ref, bf16[2048,384]{1,0:T(8,128)(2,1)} %get-tuple-element.102.dk_ref, ...), custom_call_target="tpu_custom_call" | custom-call | flops 12000000000 | bytes 12000000 | tf_op jit(solution)/shard_map/weight_grad/pallas_call | solution.py:808
  269.1 1.9 collective-permute-done.16
  272.2 3.9 %fold_xy.1 = (bf16[4,128,384]{2,1,0:T(8,128)(2,1)}, bf16[4,128,384]{2,1,0:T(8,128)(2,1)}, bf16[4,128,384]{2,1,0:T(8,128)(2,1)}, bf16[4,128,384]{2,1,0:T(8,128)(2,1)}) custom-call(s32[1]{0:T(128)} %bitcast.me_ref, bf16[2,4,2,128,384]{4,3,2,1,0:T(8,128)(2,1)} %bitcast.122, bf16[2,4,2,128,384]{4,3,2,1,0:T(8,128)(2,1)} %bitcast.123), custom_call_target="tpu_custom_call" | custom-call | bytes 4718592 | tf_op jit(solution)/shard_map/fold_xy/pallas_call | solution.py:87
  276.2 1.7 collective-permute-start.18
  277.9 1.7 collective-permute-start.19
  279.6 16.2 %leave.1 = f32[2048,768]{1,0:T(8,128)} custom-call(bf16[2048,384]{1,0:T(8,128)(2,1)} %get-tuple-element.112.dq_ref, bf16[2048,384]{1,0:T(8,128)(2,1)} %get-tuple-element.102.dk_ref, bf16[2048,384]{1,0:T(8,128)(2,1)} %get-tuple-element.103.dv_ref, bf16[2048,384]{1,0:T(8,128)(2,1)} %get-tuple-element.104.dcv_ref, ...), custom_call_target="tpu_custom_call" | custom-call | flops 15000000512 | bytes 30000000 | tf_op jit(solution)/shard_map/leave/pallas_call | solution.py:850
  295.8 2.8 collective-permute-done.19.refs_3_
  299.5 2.1 collective-permute-start.22
  301.6 2.3 collective-permute-start.21
  303.9 1.7 finish_mid.1
  307.0 2.4 collective-permute-done.20.b_ref
  310.7 1.8 finish.1
  (168 shorter events, 37.6 us)
Async XLA Ops:
  7.2 105.7 %all-gather.3.cloned.1.call-start = ((), (), s32[]{:S(2)}) async-start(), calls=%async_computation.2 | async-start | bytes 6082560 | tf_op jit(solution)/shard_map/all_gather | solution.py:923
  11.4 7.5 %collective-permute-start = (bf16[128,384]{1,0:T(8,128)(2,1)S(1)}, bf16[128,384]{1,0:T(8,128)(2,1)S(1)}, u32[]{:S(2)}, u32[]{:S(2)}) collective-permute-start(bf16[128,384]{1,0:T(8,128)(2,1)S(1)} %pad_maximum_fusion.3), channel_id=1, source_target_pairs={{0,1},{1,0},{2,3},{3,2},{4,5},{5,4},{6,7},{7,6},{8,9},{9,8},{10,11... | collective-permute-start | bytes 294920 | tf_op jit(solution)/shard_map/ppermute | solution.py:70
  19.1 13.8 %collective-permute-start.4 = (bf16[256,384]{1,0:T(8,128)(2,1)S(1)}, bf16[256,384]{1,0:T(8,128)(2,1)S(1)}, u32[]{:S(2)}, u32[]{:S(2)}) collective-permute-start(bf16[256,384]{1,0:T(8,128)(2,1)S(1)} %pad_maximum_fusion.refs_0_), channel_id=1, source_target_pairs={{0,6},{1,7},{2,4},{3,5},{4,2},{5,3},{6,0},{7,1},{8,14},{9,15},{10,... | collective-permute-start | bytes 589832 | tf_op jit(solution)/shard_map/ppermute | solution.py:70
  22.7 16.4 %collective-permute-start.3 = (bf16[256,384]{1,0:T(8,128)(2,1)S(1)}, bf16[256,384]{1,0:T(8,128)(2,1)S(1)}, u32[]{:S(2)}, u32[]{:S(2)}) collective-permute-start(bf16[256,384]{1,0:T(8,128)(2,1)S(1)} %pad_maximum_fusion.refs_0_), channel_id=1, source_target_pairs={{0,4},{1,5},{2,6},{3,7},{4,0},{5,1},{6,2},{7,3},{8,12},{9,13},{10,... | collective-permute-start | bytes 589832 | tf_op jit(solution)/shard_map/ppermute | solution.py:70
  22.7 16.4 %collective-permute-start.2 = (bf16[256,384]{1,0:T(8,128)(2,1)S(1)}, bf16[256,384]{1,0:T(8,128)(2,1)S(1)}, u32[]{:S(2)}, u32[]{:S(2)}) collective-permute-start(bf16[256,384]{1,0:T(8,128)(2,1)S(1)} %pad_maximum_fusion.refs_0_), channel_id=1, source_target_pairs={{0,2},{1,3},{2,0},{3,1},{4,6},{5,7},{6,4},{7,5},{8,10},{9,11},{10,... | collective-permute-start | bytes 589832 | tf_op jit(solution)/shard_map/ppermute | solution.py:70
  23.5 15.6 %collective-permute-start.1 = (bf16[256,384]{1,0:T(8,128)(2,1)S(1)}, bf16[256,384]{1,0:T(8,128)(2,1)S(1)}, u32[]{:S(2)}, u32[]{:S(2)}) collective-permute-start(bf16[256,384]{1,0:T(8,128)(2,1)S(1)} %pad_maximum_fusion.refs_0_), channel_id=1, source_target_pairs={{0,16},{1,17},{2,18},{3,19},{4,20},{5,21},{6,22},{7,23},{8,24},{9,... | collective-permute-start | bytes 589832 | tf_op jit(solution)/shard_map/ppermute | solution.py:70
  39.2 264.7 %reduce-scatter.2.cloned.1.call-start = ((), (), s32[]{:S(2)}) async-start(), calls=%async_computation.1 | async-start | bytes 6082560 | tf_op jit(solution)/shard_map/reduce_scatter | solution.py:949
  40.0 19.0 %collective-permute-start.8 = (bf16[256,384]{1,0:T(8,128)(2,1)S(1)}, bf16[256,384]{1,0:T(8,128)(2,1)S(1)}, u32[]{:S(2)}, u32[]{:S(2)}) collective-permute-start(bf16[256,384]{1,0:T(8,128)(2,1)S(1)} %pad_maximum_fusion.refs_0_), channel_id=1, source_target_pairs={{0,8},{1,9},{2,10},{3,11},{4,12},{5,13},{6,14},{7,15},{8,0},{9,1},... | collective-permute-start | bytes 589832 | tf_op jit(solution)/shard_map/ppermute | solution.py:70
  40.1 19.4 %collective-permute-start.9 = (bf16[256,384]{1,0:T(8,128)(2,1)S(1)}, bf16[256,384]{1,0:T(8,128)(2,1)S(1)}, u32[]{:S(2)}, u32[]{:S(2)}) collective-permute-start(bf16[256,384]{1,0:T(8,128)(2,1)S(1)} %collective-permute-done.2.refs_1_), channel_id=1, source_target_pairs={{0,8},{1,9},{2,10},{3,11},{4,12},{5,13},{6,14},{7,15},{8,0},{9,1},... | collective-permute-start | bytes 589832 | tf_op jit(solution)/shard_map/ppermute | solution.py:70
  40.6 7.8 %collective-permute-start.5 = (bf16[256,384]{1,0:T(8,128)(2,1)S(1)}, bf16[256,384]{1,0:T(8,128)(2,1)S(1)}, u32[]{:S(2)}, u32[]{:S(2)}) collective-permute-start(bf16[256,384]{1,0:T(8,128)(2,1)S(1)} %collective-permute-done.2.refs_1_), channel_id=1, source_target_pairs={{0,16},{1,17},{2,18},{3,19},{4,20},{5,21},{6,22},{7,23},{8,24},{9,... | collective-permute-start | bytes 589832 | tf_op jit(solution)/shard_map/ppermute | solution.py:70
  42.1 17.6 %collective-permute-start.10 = (bf16[256,384]{1,0:T(8,128)(2,1)S(1)}, bf16[256,384]{1,0:T(8,128)(2,1)S(1)}, u32[]{:S(2)}, u32[]{:S(2)}) collective-permute-start(bf16[256,384]{1,0:T(8,128)(2,1)S(1)} %collective-permute-done.3.refs_2_), channel_id=1, source_target_pairs={{0,8},{1,9},{2,10},{3,11},{4,12},{5,13},{6,14},{7,15},{8,0},{9,1},... | collective-permute-start | bytes 589832 | tf_op jit(solution)/shard_map/ppermute | solution.py:70
  42.1 10.9 %collective-permute-start.6 = (bf16[256,384]{1,0:T(8,128)(2,1)S(1)}, bf16[256,384]{1,0:T(8,128)(2,1)S(1)}, u32[]{:S(2)}, u32[]{:S(2)}) collective-permute-start(bf16[256,384]{1,0:T(8,128)(2,1)S(1)} %collective-permute-done.3.refs_2_), channel_id=1, source_target_pairs={{0,16},{1,17},{2,18},{3,19},{4,20},{5,21},{6,22},{7,23},{8,24},{9,... | collective-permute-start | bytes 589832 | tf_op jit(solution)/shard_map/ppermute | solution.py:70
  48.4 11.9 %collective-permute-start.11 = (bf16[256,384]{1,0:T(8,128)(2,1)S(1)}, bf16[256,384]{1,0:T(8,128)(2,1)S(1)}, u32[]{:S(2)}, u32[]{:S(2)}) collective-permute-start(bf16[256,384]{1,0:T(8,128)(2,1)S(1)} %collective-permute-done.4.refs_3_), channel_id=1, source_target_pairs={{0,8},{1,9},{2,10},{3,11},{4,12},{5,13},{6,14},{7,15},{8,0},{9,1},... | collective-permute-start | bytes 589832 | tf_op jit(solution)/shard_map/ppermute | solution.py:70
  53.0 5.9 %collective-permute-start.7 = (bf16[256,384]{1,0:T(8,128)(2,1)S(1)}, bf16[256,384]{1,0:T(8,128)(2,1)S(1)}, u32[]{:S(2)}, u32[]{:S(2)}) collective-permute-start(bf16[256,384]{1,0:T(8,128)(2,1)S(1)} %collective-permute-done.4.refs_3_), channel_id=1, source_target_pairs={{0,16},{1,17},{2,18},{3,19},{4,20},{5,21},{6,22},{7,23},{8,24},{9,... | collective-permute-start | bytes 589832 | tf_op jit(solution)/shard_map/ppermute | solution.py:70
  59.0 1.7 collective-permute-start.13
  59.6 1.5 collective-permute-start.14
  59.7 1.7 collective-permute-start.15
  267.3 3.6 %collective-permute-start.16 = (bf16[16,128,384]{2,1,0:T(8,128)(2,1)}, bf16[16,128,384]{2,1,0:T(8,128)(2,1)S(1)}, u32[]{:S(2)}, u32[]{:S(2)}) collective-permute-start(bf16[16,128,384]{2,1,0:T(8,128)(2,1)} %get-tuple-element.110), channel_id=1, source_target_pairs={{0,8},{1,9},{2,10},{3,11},{4,12},{5,13},{6,14},{7,15},{8,0},{9,1},... | collective-permute-start | bytes 4718600 | tf_op jit(solution)/shard_map/ppermute | solution.py:70
  276.1 19.7 %collective-permute-start.17 = (bf16[4,128,384]{2,1,0:T(8,128)(2,1)}, bf16[4,128,384]{2,1,0:T(8,128)(2,1)S(1)}, u32[]{:S(2)}, u32[]{:S(2)}) collective-permute-start(bf16[4,128,384]{2,1,0:T(8,128)(2,1)} %get-tuple-element.116), channel_id=1, source_target_pairs={{0,1},{1,0},{2,3},{3,2},{4,5},{5,4},{6,7},{7,6},{8,9},{9,8},{10,11... | collective-permute-start | bytes 1179656 | tf_op jit(solution)/shard_map/ppermute | solution.py:70
  276.2 19.6 %collective-permute-start.18 = (bf16[4,128,384]{2,1,0:T(8,128)(2,1)}, bf16[4,128,384]{2,1,0:T(8,128)(2,1)S(1)}, u32[]{:S(2)}, u32[]{:S(2)}) collective-permute-start(bf16[4,128,384]{2,1,0:T(8,128)(2,1)} %get-tuple-element.117), channel_id=1, source_target_pairs={{0,16},{1,17},{2,18},{3,19},{4,20},{5,21},{6,22},{7,23},{8,24},{9,... | collective-permute-start | bytes 1179656 | tf_op jit(solution)/shard_map/ppermute | solution.py:70
  277.9 20.7 %collective-permute-start.19 = (bf16[4,128,384]{2,1,0:T(8,128)(2,1)}, bf16[4,128,384]{2,1,0:T(8,128)(2,1)S(1)}, u32[]{:S(2)}, u32[]{:S(2)}) collective-permute-start(bf16[4,128,384]{2,1,0:T(8,128)(2,1)} %get-tuple-element.118), channel_id=1, source_target_pairs={{0,17},{1,16},{2,19},{3,18},{4,21},{5,20},{6,23},{7,22},{8,25},{9,... | collective-permute-start | bytes 1179656 | tf_op jit(solution)/shard_map/ppermute | solution.py:70
  299.5 7.5 %collective-permute-start.22 = (bf16[128,384]{1,0:T(8,128)(2,1)S(1)}, bf16[128,384]{1,0:T(8,128)(2,1)S(1)}, u32[]{:S(2)}, u32[]{:S(2)}) collective-permute-start(bf16[128,384]{1,0:T(8,128)(2,1)S(1)} %get-tuple-element.129), channel_id=1, source_target_pairs={{0,6},{1,7},{2,4},{3,5},{4,2},{5,3},{6,0},{7,1},{8,14},{9,15},{10,... | collective-permute-start | bytes 294920 | tf_op jit(solution)/shard_map/ppermute | solution.py:70
  301.6 7.8 %collective-permute-start.20 = (bf16[128,384]{1,0:T(8,128)(2,1)S(1)}, bf16[128,384]{1,0:T(8,128)(2,1)S(1)}, u32[]{:S(2)}, u32[]{:S(2)}) collective-permute-start(bf16[128,384]{1,0:T(8,128)(2,1)S(1)} %get-tuple-element.127), channel_id=1, source_target_pairs={{0,2},{1,3},{2,0},{3,1},{4,6},{5,7},{6,4},{7,5},{8,10},{9,11},{10,... | collective-permute-start | bytes 294920 | tf_op jit(solution)/shard_map/ppermute | solution.py:70
  301.6 7.9 %collective-permute-start.21 = (bf16[128,384]{1,0:T(8,128)(2,1)S(1)}, bf16[128,384]{1,0:T(8,128)(2,1)S(1)}, u32[]{:S(2)}, u32[]{:S(2)}) collective-permute-start(bf16[128,384]{1,0:T(8,128)(2,1)S(1)} %get-tuple-element.128), channel_id=1, source_target_pairs={{0,4},{1,5},{2,6},{3,7},{4,0},{5,1},{6,2},{7,3},{8,12},{9,13},{10,... | collective-permute-start | bytes 294920 | tf_op jit(solution)/shard_map/ppermute | solution.py:70
  (26 other events, 267.1 us)
Sparse Core Ops, SparseCore 0:
  39.3 66.9 all-gather.2
  188.6 113.4 reduce-scatter.1
